TPU v7x, 32 devices: a whole 2x2x4 slice. The times are simulated.
32 devices in a mesh: dp: 4 (over y, x), fsdp: 8 (over z, core).
Axes of the slice: x: 2, y: 2, z: 4, core: 2. Of those that a mesh axis runs over, the one named last changes fastest.
Arguments:
- tokens: bfloat16 [30720, 768], P(('dp', 'fsdp')), may hold values from -6 to 6
- ln1_gain: bfloat16 [768], P('fsdp'), may hold values from 0.5 to 1.5
- ln1_bias: bfloat16 [768], P('fsdp'), may hold values from -3 to 3
- w_qkv: bfloat16 [768, 2304], P('fsdp'), may hold values from -0.21875 to 0.21875
- qv_bias: bfloat16 [2, 768], P(None, 'fsdp'), may hold values from -3 to 3
- w_proj: bfloat16 [768, 768], P('fsdp'), may hold values from -2 to 2
- proj_bias: bfloat16 [768], P('fsdp'), may hold values from -3 to 3
- ln2_gain: bfloat16 [768], P('fsdp'), may hold values from 0.5 to 1.5
- ln2_bias: bfloat16 [768], P('fsdp'), may hold values from -3 to 3
- w_up: bfloat16 [768, 3072], P('fsdp'), may hold values from -0.21875 to 0.21875
- up_bias: bfloat16 [3072], P('fsdp'), may hold values from -3 to 3
- w_down: bfloat16 [3072, 768], P('fsdp'), may hold values from -0.109375 to 0.109375
- down_bias: bfloat16 [768], P('fsdp'), may hold values from -3 to 3
- w_head: bfloat16 [768, 1024], P('fsdp'), may hold values from -0.21875 to 0.21875
- head_bias: bfloat16 [1024], P('fsdp'), may hold values from -3 to 3
- clip_counts: int32 [32, 32], replicated, may hold values from 0 to 157, as said below
- cot_out: bfloat16 [30720, 768], P(('dp', 'fsdp')), may hold values from -6 to 6
- cot_align: bfloat16 [30720, 1024], P(('dp', 'fsdp')), may hold values from -6 to 6
Outputs:
- block_out: bfloat16 [30720, 768], P(('dp', 'fsdp'))
- aligned: bfloat16 [30720, 1024], P(('dp', 'fsdp'))
- grad_tokens: bfloat16 [30720, 768], P(('dp', 'fsdp'))
- grad_ln1_gain: float32 [768], P('fsdp')
- grad_ln1_bias: float32 [768], P('fsdp')
- grad_w_qkv: float32 [768, 2304], P('fsdp')
- grad_qv_bias: float32 [2, 768], P(None, 'fsdp')
- grad_w_proj: float32 [768, 768], P('fsdp')
- grad_proj_bias: float32 [768], P('fsdp')
- grad_ln2_gain: float32 [768], P('fsdp')
- grad_ln2_bias: float32 [768], P('fsdp')
- grad_w_up: float32 [768, 3072], P('fsdp')
- grad_up_bias: float32 [3072], P('fsdp')
- grad_w_down: float32 [3072, 768], P('fsdp')
- grad_down_bias: float32 [768], P('fsdp')
- grad_w_head: float32 [768, 1024], P('fsdp')
- grad_head_bias: float32 [1024], P('fsdp')
Inputs may be any that keep to these rules, and one draw needn't show every extreme that they name: `clip_counts`: in each sequence the nonzero counts come first and lie between 40 and 157, the rest are 0; they sum to at most 960 and to more than 803.
All inputs are finite; a program needn't handle non-finite values.
Results may differ from a plain program's by a relative error of at most 0.012.
Values may be sent and summed in bfloat16 or wider, within the bound.
No kernel may reach another device: no remote copies, remote signals or barrier semaphores. Data moves between devices by JAX's collectives and lax.ppermute only.
A program may use at most 192 MiB of HBM per device.

v0:
```python
import math

import jax
import jax.numpy as jnp
from jax import lax
from jax.sharding import PartitionSpec as P

HEADS = 12


epsilon = 1e-06
masked_score = -1e30


def layer_norm(values, gain, shift):
    center = values - jnp.mean(values, axis=-1, keepdims=True)
    spread = jnp.mean(center * center, axis=-1, keepdims=True)
    inverse = lax.rsqrt(spread + epsilon)
    normed = center * inverse
    return (normed, inverse, normed * gain + shift)


def norm_back(grad, normed, inverse, gain):
    gain_grad = jnp.sum(grad * normed, axis=0)
    shift_grad = jnp.sum(grad, axis=0)
    scaled = grad * gain
    inner = scaled - jnp.mean(scaled, axis=-1, keepdims=True)
    inner = inner - normed * jnp.mean(scaled * normed, axis=-1, keepdims=True)
    return (inverse * inner, gain_grad, shift_grad)


def gelu_slope(values):
    normal_cdf = 0.5 * (1.0 + lax.erf(values / math.sqrt(2.0)))
    normal_pdf = jnp.exp(-0.5 * values * values) / math.sqrt(2.0 * math.pi)
    return normal_cdf + values * normal_pdf


def dot_right_t(left, right):
    return lax.dot_general(
        left, right, (((1,), (1,)), ((), ())), preferred_element_type=jnp.float32
    )


def dot_left_t(left, right):
    return lax.dot_general(
        left, right, (((0,), (0,)), ((), ())), preferred_element_type=jnp.float32
    )


def local(
    tokens,
    ln1_gain,
    ln1_bias,
    w_qkv,
    qv_bias,
    w_proj,
    proj_bias,
    ln2_gain,
    ln2_bias,
    w_up,
    up_bias,
    w_down,
    down_bias,
    w_head,
    head_bias,
    clip_counts,
    cot_out,
    cot_align,
):
    num_rows = tokens.shape[0]
    width = tokens.shape[1]
    head_size = width // HEADS
    span = 2 * head_size
    pair_count = HEADS // 2
    scale = head_size ** (-0.5)
    (
        gain_one,
        shift_one,
        weight_qkv,
        bias_qv,
        weight_proj,
        bias_proj,
        gain_two,
        shift_two,
        weight_up,
        bias_up,
        weight_down,
        bias_down,
        weight_head,
        bias_head,
    ) = (
        lax.all_gather(ln1_gain, "fsdp", axis=0, tiled=True),
        lax.all_gather(ln1_bias, "fsdp", axis=0, tiled=True),
        lax.all_gather(w_qkv, "fsdp", axis=0, tiled=True),
        lax.all_gather(qv_bias, "fsdp", axis=1, tiled=True),
        lax.all_gather(w_proj, "fsdp", axis=0, tiled=True),
        lax.all_gather(proj_bias, "fsdp", axis=0, tiled=True),
        lax.all_gather(ln2_gain, "fsdp", axis=0, tiled=True),
        lax.all_gather(ln2_bias, "fsdp", axis=0, tiled=True),
        lax.all_gather(w_up, "fsdp", axis=0, tiled=True),
        lax.all_gather(up_bias, "fsdp", axis=0, tiled=True),
        lax.all_gather(w_down, "fsdp", axis=0, tiled=True),
        lax.all_gather(down_bias, "fsdp", axis=0, tiled=True),
        lax.all_gather(w_head, "fsdp", axis=0, tiled=True),
        lax.all_gather(head_bias, "fsdp", axis=0, tiled=True),
    )
    seq_index = lax.axis_index("dp") * lax.axis_size("fsdp") + lax.axis_index("fsdp")
    my_counts = lax.dynamic_slice_in_dim(clip_counts, seq_index, 1, 0)[0]
    ends = jnp.cumsum(my_counts)
    places = jnp.arange(num_rows, dtype=jnp.int32)
    seg_own = jnp.sum((ends[None, :] <= places[:, None]).astype(jnp.int32), axis=1)
    valid_rows = (places < ends[-1]).astype(jnp.float32)[:, None]
    allowed = seg_own[:, None] == seg_own[None, :]
    inputs = tokens.astype(jnp.float32)
    normed_one, inverse_one, pre_one = layer_norm(
        inputs, gain_one.astype(jnp.float32), shift_one.astype(jnp.float32)
    )
    hidden_one = pre_one.astype(jnp.bfloat16)
    projected = jnp.dot(hidden_one, weight_qkv, preferred_element_type=jnp.float32)
    bias_float = bias_qv.astype(jnp.float32)
    queries = ((projected[:, :width] + bias_float[0]) * scale).astype(jnp.bfloat16)
    keys_all = projected[:, width : 2 * width].astype(jnp.bfloat16)
    values_all = (projected[:, 2 * width :] + bias_float[1]).astype(jnp.bfloat16)

    def pair_slices(pair_index):
        start = pair_index * span
        query_pair = lax.dynamic_slice_in_dim(queries, start, span, 1).reshape(
            num_rows, 2, head_size
        )
        key_pair = lax.dynamic_slice_in_dim(keys_all, start, span, 1).reshape(
            num_rows, 2, head_size
        )
        value_pair = lax.dynamic_slice_in_dim(values_all, start, span, 1).reshape(
            num_rows, 2, head_size
        )
        scores = jnp.einsum(
            "qhd,khd->hqk", query_pair, key_pair, preferred_element_type=jnp.float32
        )
        scores = jnp.where(allowed[None], scores, masked_score)
        return (query_pair, key_pair, value_pair, scores)

    def attend(pair_index):
        query_pair, key_pair, value_pair, scores = pair_slices(pair_index)
        top_score = jnp.max(scores, axis=-1, keepdims=True)
        weights = jnp.exp(scores - top_score)
        total = jnp.sum(weights, axis=-1, keepdims=True)
        probs = (weights / total).astype(jnp.bfloat16)
        out_pair = jnp.einsum("hqk,khd->qhd", probs, value_pair, preferred_element_type=jnp.float32)
        return (out_pair.reshape(num_rows, span), (top_score + jnp.log(total))[..., 0])

    out_pairs, log_totals = lax.map(attend, jnp.arange(pair_count, dtype=jnp.int32))
    attended = out_pairs.transpose(1, 0, 2).reshape(num_rows, width).astype(jnp.bfloat16)
    middle = (
        inputs
        + jnp.dot(attended, weight_proj, preferred_element_type=jnp.float32)
        + bias_proj.astype(jnp.float32)
    )
    normed_two, inverse_two, pre_two = layer_norm(
        middle, gain_two.astype(jnp.float32), shift_two.astype(jnp.float32)
    )
    hidden_two = pre_two.astype(jnp.bfloat16)
    up_value = jnp.dot(hidden_two, weight_up, preferred_element_type=jnp.float32) + bias_up.astype(
        jnp.float32
    )
    activated = jax.nn.gelu(up_value, approximate=False).astype(jnp.bfloat16)
    result = (
        middle
        + jnp.dot(activated, weight_down, preferred_element_type=jnp.float32)
        + bias_down.astype(jnp.float32)
    )
    result_low = result.astype(jnp.bfloat16)
    head_value = (
        jnp.dot(result_low, weight_head, preferred_element_type=jnp.float32)
        + bias_head.astype(jnp.float32)
    ) * valid_rows
    block_out = (result * valid_rows).astype(jnp.bfloat16)
    back_gain_one, back_qkv, back_proj, back_gain_two, back_up, back_down, back_head = (
        lax.all_gather(ln1_gain, "fsdp", axis=0, tiled=True),
        lax.all_gather(w_qkv, "fsdp", axis=0, tiled=True),
        lax.all_gather(w_proj, "fsdp", axis=0, tiled=True),
        lax.all_gather(ln2_gain, "fsdp", axis=0, tiled=True),
        lax.all_gather(w_up, "fsdp", axis=0, tiled=True),
        lax.all_gather(w_down, "fsdp", axis=0, tiled=True),
        lax.all_gather(w_head, "fsdp", axis=0, tiled=True),
    )
    align_grad = (cot_align.astype(jnp.float32) * valid_rows).astype(jnp.bfloat16)
    grad_head = dot_left_t(result_low, align_grad)
    grad_head_bias = jnp.sum(align_grad.astype(jnp.float32), axis=0)
    result_grad = cot_out.astype(jnp.float32) * valid_rows + dot_right_t(align_grad, back_head)
    down_in = result_grad.astype(jnp.bfloat16)
    grad_down = dot_left_t(activated, down_in)
    grad_down_bias = jnp.sum(down_in.astype(jnp.float32), axis=0)
    up_grad = (dot_right_t(down_in, back_down) * gelu_slope(up_value)).astype(jnp.bfloat16)
    grad_up = dot_left_t(hidden_two, up_grad)
    grad_up_bias = jnp.sum(up_grad.astype(jnp.float32), axis=0)
    hidden_two_grad = dot_right_t(up_grad, back_up)
    norm_two_back, grad_gain_two, grad_shift_two = norm_back(
        hidden_two_grad, normed_two, inverse_two, back_gain_two.astype(jnp.float32)
    )
    middle_grad = result_grad + norm_two_back
    proj_in = middle_grad.astype(jnp.bfloat16)
    grad_proj = dot_left_t(attended, proj_in)
    grad_proj_bias = jnp.sum(proj_in.astype(jnp.float32), axis=0)
    attended_grad = dot_right_t(proj_in, back_proj).astype(jnp.bfloat16)

    def attend_back(item):
        pair_index, log_total = item
        query_pair, key_pair, value_pair, scores = pair_slices(pair_index)
        probs = jnp.exp(scores - log_total[..., None])
        grad_pair = lax.dynamic_slice_in_dim(attended_grad, pair_index * span, span, 1).reshape(
            num_rows, 2, head_size
        )
        prob_grad = jnp.einsum(
            "qhd,khd->hqk", grad_pair, value_pair, preferred_element_type=jnp.float32
        )
        value_grad = jnp.einsum(
            "hqk,qhd->khd",
            probs.astype(jnp.bfloat16),
            grad_pair,
            preferred_element_type=jnp.float32,
        )
        row_dot = jnp.sum(probs * prob_grad, axis=-1, keepdims=True)
        score_grad = (probs * (prob_grad - row_dot)).astype(jnp.bfloat16)
        query_grad = jnp.einsum(
            "hqk,khd->qhd", score_grad, key_pair, preferred_element_type=jnp.float32
        )
        key_grad = jnp.einsum(
            "hqk,qhd->khd", score_grad, query_pair, preferred_element_type=jnp.float32
        )
        return (
            query_grad.reshape(num_rows, span),
            key_grad.reshape(num_rows, span),
            value_grad.reshape(num_rows, span),
        )

    query_pairs, key_pairs, value_pairs = lax.map(
        attend_back, (jnp.arange(pair_count, dtype=jnp.int32), log_totals)
    )
    query_grad = query_pairs.transpose(1, 0, 2).reshape(num_rows, width)
    key_low = key_pairs.transpose(1, 0, 2).reshape(num_rows, width).astype(jnp.bfloat16)
    value_low = value_pairs.transpose(1, 0, 2).reshape(num_rows, width).astype(jnp.bfloat16)
    query_low = query_grad.astype(jnp.bfloat16) * jnp.bfloat16(scale)
    qkv_grad = jnp.concatenate([query_low, key_low, value_low], axis=1)
    grad_qkv = dot_left_t(hidden_one, qkv_grad)
    grad_qv = jnp.stack(
        [
            jnp.sum(query_low.astype(jnp.float32), axis=0),
            jnp.sum(value_low.astype(jnp.float32), axis=0),
        ]
    )
    hidden_one_grad = dot_right_t(qkv_grad, back_qkv)
    norm_one_back, grad_gain_one, grad_shift_one = norm_back(
        hidden_one_grad, normed_one, inverse_one, back_gain_one.astype(jnp.float32)
    )
    grad_tokens = (middle_grad + norm_one_back).astype(jnp.bfloat16)
    (
        part_gain_one,
        part_shift_one,
        part_qkv,
        part_qv,
        part_proj,
        part_proj_bias,
        part_gain_two,
        part_shift_two,
        part_up,
        part_up_bias,
        part_down,
        part_down_bias,
        part_head,
        part_head_bias,
    ) = (
        lax.psum_scatter(grad_gain_one, "fsdp", scatter_dimension=0, tiled=True),
        lax.psum_scatter(grad_shift_one, "fsdp", scatter_dimension=0, tiled=True),
        lax.psum_scatter(grad_qkv, "fsdp", scatter_dimension=0, tiled=True),
        lax.psum_scatter(grad_qv, "fsdp", scatter_dimension=1, tiled=True),
        lax.psum_scatter(grad_proj, "fsdp", scatter_dimension=0, tiled=True),
        lax.psum_scatter(grad_proj_bias, "fsdp", scatter_dimension=0, tiled=True),
        lax.psum_scatter(grad_gain_two, "fsdp", scatter_dimension=0, tiled=True),
        lax.psum_scatter(grad_shift_two, "fsdp", scatter_dimension=0, tiled=True),
        lax.psum_scatter(grad_up, "fsdp", scatter_dimension=0, tiled=True),
        lax.psum_scatter(grad_up_bias, "fsdp", scatter_dimension=0, tiled=True),
        lax.psum_scatter(grad_down, "fsdp", scatter_dimension=0, tiled=True),
        lax.psum_scatter(grad_down_bias, "fsdp", scatter_dimension=0, tiled=True),
        lax.psum_scatter(grad_head, "fsdp", scatter_dimension=0, tiled=True),
        lax.psum_scatter(grad_head_bias, "fsdp", scatter_dimension=0, tiled=True),
    )
    totals = lax.psum(
        (
            part_gain_one,
            part_shift_one,
            part_qkv,
            part_qv,
            part_proj,
            part_proj_bias,
            part_gain_two,
            part_shift_two,
            part_up,
            part_up_bias,
            part_down,
            part_down_bias,
            part_head,
            part_head_bias,
        ),
        "dp",
    )
    return (block_out, head_value.astype(jnp.bfloat16), grad_tokens) + tuple(totals)


def solution(mesh):
    placed = (
        P(("dp", "fsdp"), None),
        P("fsdp"),
        P("fsdp"),
        P("fsdp", None),
        P(None, "fsdp"),
        P("fsdp", None),
        P("fsdp"),
        P("fsdp"),
        P("fsdp"),
        P("fsdp", None),
        P("fsdp"),
        P("fsdp", None),
        P("fsdp"),
        P("fsdp", None),
        P("fsdp"),
        P(),
        P(("dp", "fsdp"), None),
        P(("dp", "fsdp"), None),
    )
    return jax.shard_map(
        local,
        mesh=mesh,
        in_specs=placed,
        out_specs=(
            P(("dp", "fsdp"), None),
            P(("dp", "fsdp"), None),
            P(("dp", "fsdp"), None),
            P("fsdp"),
            P("fsdp"),
            P("fsdp", None),
            P(None, "fsdp"),
            P("fsdp", None),
            P("fsdp"),
            P("fsdp"),
            P("fsdp"),
            P("fsdp", None),
            P("fsdp"),
            P("fsdp", None),
            P("fsdp"),
            P("fsdp", None),
            P("fsdp"),
        ),
        check_vma=False,
    )
```

profile of v0, /device:TPU:0, one launch (start us, length us, event | category | flops | bytes accessed | tf_op | source)
XLA Modules:
  0.0 831.8 jit_solution(12414016800103136786)
XLA Ops:
  18.5 30.5 %all-reduce.17 = (bf16[768]{0:T(1024)(128)(2,1)S(1)}, bf16[768]{0:T(1024)(128)(2,1)S(1)}, bf16[768]{0:T(1024)(128)(2,1)S(1)}, bf16[768]{0:T(1024)(128)(2,1)S(1)}...) all-reduce(bf16[768]{0:T(1024)(128)(2,1)S(1)} %dynamic-update-slice, ...), channel_id=1, replica_groups=mesh['dp'=4,'fsdp'=8] {'fsdp'}, use_global_device_ids=true, to_apply=%add.1 | all-reduce | flops 4608 | bytes 18432
  50.0 8.6 %all-gather = bf16[8,96,2]{1,2,0:T(2,128)(2,1)S(1)} all-gather(bf16[1,96,2]{1,2,0:T(2,128)(2,1)S(1)} %bitcast.181), channel_id=1, replica_groups=mesh['dp'=4,'fsdp'=8] {'fsdp'}, dimensions={0}, use_global_device_ids=true | all-gather | bytes 3456 | tf_op jit(solution)/shard_map/all_gather | solution.py:95
  58.8 13.0 %all-gather.1 = bf16[8,1,384]{2,1,0:T(2,128)(2,1)S(1)} all-gather(bf16[1,1,384]{2,1,0:T(2,128)(2,1)S(1)} %reshape.194), channel_id=1, replica_groups=mesh['dp'=4,'fsdp'=8] {'fsdp'}, dimensions={0}, use_global_device_ids=true | all-gather | bytes 6912 | tf_op jit(solution)/shard_map/all_gather | solution.py:101
  73.1 6.3 convert_reduce_fusion.5
  80.6 5.9 fusion.61
  96.1 55.4 %while.28 = (s32[]{:T(128)}, bf16[6,960,128]{1,2,0:T(8,128)(2,1)}, f32[6,2,960]{2,1,0:T(2,128)S(1)}, s32[6]{0:T(128)S(1)}, bf16[960,768]{0,1:T(8,128)(2,1)S(1)},...) while((s32[]{:T(128)}, bf16[6,960,128]{1,2,0:T(8,128)(2,1)}, ...), condition=%wide.region_7.8_spmd.clone, body=%wide.region_4.7_spmd.clone.sunk | while | flops 489367680 | bytes 28837820 | solution.py:151
  157.5 35.3 %fusion.14 = (bf16[960,3072]{1,0:T(8,128)(2,1)}, f32[960,3072]{1,0:T(8,128)}) fusion(f32[3072]{0:T(1024)S(1)} %bitcast.176, bf16[768,3072]{1,0:T(8,128)(2,1)} %all-gather.13.cloned.1.call-done, f32[960,768]{1,0:T(8,128)S(1)} %get-tuple-element.359, f32[768]{0:T(1024)S(1)} %convert_element_type.171, f32[768]{0:T(1024)S(1)} %convert_element_type.170, ...), kind=kOutput, calls=%fused_computation.34 | convolution fusion | flops 4728176640 | bytes 25388544 | tf_op jit(solution)/shard_map/dot_general | solution.py:162
  192.8 16.1 %all-gather.15.cloned.1.call-done = bf16[3072,768]{1,0:T(8,128)(2,1)} async-done(((bf16[384,768]{1,0:T(8,128)(2,1)}), bf16[3072,768]{1,0:T(8,128)(2,1)}) %all-gather.15.cloned.1.call-update) | async-done | bytes 4718608 | tf_op jit(solution)/shard_map/all_gather | solution.py:102
  208.9 12.5 %convert_reduce_fusion = (f32[3072]{0:T(1024)}, bf16[960,3072]{1,0:T(8,128)(2,1)S(1)}) fusion(f32[960,3072]{1,0:T(8,128)} %get-tuple-element.363, f32[3072]{0:T(1024)S(1)} %bitcast.177, bf16[960,768]{1,0:T(8,128)(2,1)} %get-tuple-element.342, bf16[3072,768]{1,0:T(8,128)(2,1)} %all-gather.15.cloned.1.call-done), kind=kOutput, calls=%fused_computation.41 | convolution fusion | flops 4568183808 | bytes 23912448 | tf_op jit(solution)/shard_map/dot_general | solution.py:39
  221.5 5.8 multiply_reduce_fusion.1
  227.3 9.1 %convert_reduce_fusion.6 = (f32[768]{0:T(1024)}, f32[960,768]{1,0:T(8,128)S(1)}, bf16[960,768]{1,0:T(8,128)(2,1)}, bf16[960,768]{1,0:T(8,128)(2,1)}) fusion(f32[960]{0:T(1024)S(1)} %get-tuple-element.368, f32[960,768]{1,0:T(8,128)S(1)} %get-tuple-element.359, f32[960]{0:T(1024)S(1)} %broadcast_multiply_fusion.4, f32[960]{0:T(1024)S(1)} %get-tuple-element.369, ...), kind=kOutput, calls=%fused_computation.90 | convolution fusion | flops 4543855616 | bytes 26865408 | tf_op jit(solution)/shard_map/dot_general | solution.py:168
  238.0 4.4 fusion.56
  242.4 5.0 fusion.50
  255.9 138.9 %while.29 = (s32[]{:T(128)}, bf16[6,960,128]{1,2,0:T(8,128)(2,1)S(1)}, bf16[6,960,128]{1,2,0:T(8,128)(2,1)}, bf16[6,960,128]{1,2,0:T(8,128)(2,1)}, s32[6]{0:T(12...) while((s32[]{:T(128)}, ...), condition=%wide.region_14.15_spmd.clone, body=%wide.region_12.14_spmd.clone.sunk | while | flops 1202686080 | bytes 89089040 | solution.py:236
  259.1 4.3 fusion.138
  266.2 5.2 multiply_reduce_fusion.7
  289.3 5.2 multiply_reduce_fusion.7
  312.4 5.3 multiply_reduce_fusion.7
  335.5 5.2 multiply_reduce_fusion.7
  358.5 5.2 multiply_reduce_fusion.7
  381.6 5.2 multiply_reduce_fusion.7
  397.2 8.6 %fusion.47 = f32[768,2304]{1,0:T(8,128)} fusion(bf16[960,768]{0,1:T(8,128)(2,1)S(1)} %bitcast.165, bf16[960,768]{0,1:T(8,128)(2,1)} %bitcast.169, bf16[960,768]{0,1:T(8,128)(2,1)S(1)} %bitcast.167, bf16[960,768]{1,0:T(8,128)(2,1)S(1)} %copy-done.5, f32[768]{0:T(1024)S(1)} %copy-done.36, f32[768]{0:T(1024)S(1)} %copy-done.25, f32[960]{0:T(1024)S(1)} %copy-done.27, ...), kind=kOutput, calls=%fused_computation.101 | convolution fusion | flops 3415080960 | bytes 12989952 | tf_op jit(solution)/shard_map/dot_general | solution.py:45
  407.7 10.5 %fusion.63 = f32[768,3072]{1,0:T(8,128)} fusion(bf16[960,3072]{1,0:T(8,128)(2,1)} %copy-done.9, f32[960,768]{1,0:T(8,128)S(1)} %copy-done.3, f32[768]{0:T(1024)S(1)} %copy-done.21, f32[768]{0:T(1024)S(1)} %convert_element_type.170, f32[960]{0:T(1024)S(1)} %add_rsqrt_fusion, f32[960]{0:T(1024)S(1)} %broadcast_multiply_fusion.4), kind=kOutput, calls=%fused_computation.135 | convolution fusion | flops 4533534720 | bytes 18298368 | tf_op jit(solution)/shard_map/dot_general | solution.py:45
  419.6 10.1 %fusion.71 = f32[3072,768]{1,0:T(8,128)} fusion(bf16[960,3072]{1,0:T(8,128)(2,1)} %get-tuple-element.362, bf16[960,768]{1,0:T(8,128)(2,1)S(1)} %copy-done.47), kind=kOutput, calls=%fused_computation.142 | convolution fusion | flops 4529848320 | bytes 16809984 | tf_op jit(solution)/shard_map/dot_general | solution.py:45
  432.6 49.7 %reduce-scatter.9.cloned.1.call-done = f32[96,2304]{1,0:T(8,128)} async-done(((f32[768,2304]{1,0:T(8,128)}), f32[96,2304]{1,0:T(8,128)}) %reduce-scatter.9.cloned.1.call-update) | async-done | bytes 884752 | tf_op jit(solution)/shard_map/reduce_scatter | solution.py:274
  482.3 100.2 %reduce-scatter.13.cloned.1.call-done = f32[96,3072]{1,0:T(8,128)} async-done(((f32[768,3072]{1,0:T(8,128)}), f32[96,3072]{1,0:T(8,128)}) %reduce-scatter.13.cloned.1.call-update) | async-done | bytes 1179664 | tf_op jit(solution)/shard_map/reduce_scatter | solution.py:280
  582.5 100.0 %reduce-scatter.15.cloned.1.call-done = f32[384,768]{1,0:T(8,128)} async-done(((f32[3072,768]{1,0:T(8,128)}), f32[384,768]{1,0:T(8,128)}) %reduce-scatter.15.cloned.1.call-update) | async-done | bytes 1179664 | tf_op jit(solution)/shard_map/reduce_scatter | solution.py:282
  684.7 9.1 %all-gather.2 = bf16[8,1,128]{2,1,0:T(2,128)(2,1)S(1)} all-gather(bf16[1,1,128]{2,1,0:T(2,128)(2,1)S(1)} %bitcast.182), channel_id=1, replica_groups=mesh['dp'=4,'fsdp'=8] {'fsdp'}, dimensions={0}, use_global_device_ids=true | all-gather | bytes 2304 | tf_op jit(solution)/shard_map/all_gather | solution.py:105
  695.8 9.1 %fusion.41 = (f32[768]{0:T(1024)S(1)}, f32[960]{0:T(1024)S(1)}, f32[960]{0:T(1024)S(1)}, f32[768]{0:T(1024)S(1)}, f32[960,768]{1,0:T(8,128)}) fusion(bf16[960,768]{1,0:T(8,128)(2,1)S(1)} %copy-done.6, f32[960]{0:T(1024)S(1)} %copy-done.27, f32[960]{0:T(1024)S(1)} %copy-done.23, f32[768]{0:T(1024)S(1)} %copy-done.25, ...), kind=kOutput, calls=%fused_computation.79 | convolution fusion | flops 3418026496 | bytes 12410880 | tf_op jit(solution)/shard_map/dot_general | solution.py:39
  704.9 27.4 %all-reduce.14 = (f32[768]{0:T(1024)S(1)}, f32[768]{0:T(1024)S(1)}, f32[768]{0:T(1024)S(1)}, f32[768]{0:T(1024)S(1)}, f32[768]{0:T(1024)S(1)}, /*index=5*/f32[30...) all-reduce(f32[768]{0:T(1024)S(1)} %get-tuple-element.265, ...), channel_id=2, replica_groups=mesh['dp'=4,'fsdp'=8] {'fsdp'}, use_global_device_ids=true, to_apply=%region_18.19.clone | all-reduce | flops 8704 | bytes 69632
  741.1 10.6 %all-reduce.15 = (f32[96]{0:T(128)}, f32[96]{0:T(128)}, f32[2,96]{1,0:T(2,128)}, f32[96]{0:T(128)}, f32[96]{0:T(128)}, /*index=5*/f32[96]{0:T(128)}, f32[384]{0:T(512)}, f32[96]{0:T(128)}, f32[128]{0:T(128)}) all-reduce(f32[96]{0:T(128)S(1)} %dynamic-slice.7, f32[96]{0:T(128)S(1)} %dynamic-slice.9, ...), channel_id=1, replica_groups=mesh['dp'=4,'fsdp'=8] {'dp'}, use_global_device_ids=true, to_apply=%region_19.20 | all-reduce | flops 1280 | bytes 10240 | tf_op jit(solution)/shard_map/psum | solution.py:287
  751.6 66.3 %all-reduce.20.cloned.1.call-done = (f32[96,2304]{1,0:T(8,128)}, f32[96,768]{1,0:T(8,128)}, f32[96,3072]{1,0:T(8,128)}, f32[384,768]{1,0:T(8,128)}, f32[96,1024]{1,0:T(8,128)}) async-done(((f32[96,2304]{1,0:T(8,128)}, f32[96,768]{1,0:T(8,128)}, f32[96,3072]{1,0:T(8,128)}, f32[384,768]{1,0:T(8,128)}, f32[96,1024]{1,0:T(8,128)}), (f32[96,2304]{1,0:T(8,128)}, f32[96,768]{1,0:T(8,128)}, f32[96,3072]{1,0:T(8,128)}, ...) | async-done | bytes 3932176 | tf_op jit(solution)/shard_map/psum | solution.py:287
  (379 shorter events, 215.0 us)
Async XLA Ops:
  7.2 41.9 %copy-start.4 = (bf16[960,768]{1,0:T(8,128)(2,1)S(1)}, bf16[960,768]{1,0:T(8,128)(2,1)}, u32[]{:S(2)}) copy-start(bf16[960,768]{1,0:T(8,128)(2,1)} %param.22) | copy-start | bytes 4423684
  7.2 51.6 %copy-start.38 = (bf16[384]{0:T(512)(128)(2,1)S(1)}, bf16[384]{0:T(512)(128)(2,1)}, u32[]{:S(2)}) copy-start(bf16[384]{0:T(512)(128)(2,1)} %param.32) | copy-start | bytes 2308
  7.2 65.9 %copy-start.14 = (bf16[960,1024]{1,0:T(8,128)(2,1)S(1)}, bf16[960,1024]{1,0:T(8,128)(2,1)}, u32[]{:S(2)}) copy-start(bf16[960,1024]{1,0:T(8,128)(2,1)} %param.39) | copy-start | bytes 5898244
  7.2 65.9 %all-gather.17.cloned.1.call-start = ((), (), s32[]{:S(2)}) async-start(), calls=%async_computation.10 | async-start | bytes 1769472 | tf_op jit(solution)/shard_map/all_gather | solution.py:104
  8.0 72.7 %all-gather.9.cloned.1.call-start = ((), (), s32[]{:S(2)}) async-start(), calls=%async_computation.6 | async-start | bytes 3981312 | tf_op jit(solution)/shard_map/all_gather | solution.py:94
  8.7 142.8 %all-gather.11.cloned.1.call-start = ((), (), s32[]{:S(2)}) async-start(), calls=%async_computation.7 | async-start | bytes 1327104 | tf_op jit(solution)/shard_map/all_gather | solution.py:96
  9.5 148.0 %all-gather.13.cloned.1.call-start = ((), (), s32[]{:S(2)}) async-start(), calls=%async_computation.8 | async-start | bytes 5308416 | tf_op jit(solution)/shard_map/all_gather | solution.py:100
  10.0 198.9 %all-gather.15.cloned.1.call-start = ((), (), s32[]{:S(2)}) async-start(), calls=%async_computation.9 | async-start | bytes 5308416 | tf_op jit(solution)/shard_map/all_gather | solution.py:102
  10.6 421.9 %reduce-scatter.11.cloned.1.call-start = ((), (), s32[]{:S(2)}) async-start(), calls=%async_computation.12 | async-start | bytes 2654208 | tf_op jit(solution)/shard_map/reduce_scatter | solution.py:276
  49.0 31.6 %copy-start.24 = (f32[768]{0:T(1024)}, f32[768]{0:T(1024)S(1)}, u32[]{:S(2)}) copy-start(f32[768]{0:T(1024)S(1)} %convert_element_type.159) | copy-start | bytes 9220
  49.1 31.6 %copy-start.35 = (f32[768]{0:T(1024)}, f32[768]{0:T(1024)S(1)}, u32[]{:S(2)}) copy-start(f32[768]{0:T(1024)S(1)} %convert_element_type.160) | copy-start | bytes 9220
  49.4 31.3 %copy-start.22 = (f32[960]{0:T(1024)}, f32[960]{0:T(1024)S(1)}, u32[]{:S(2)}) copy-start(f32[960]{0:T(1024)S(1)} %broadcast_multiply_fusion.5) | copy-start | bytes 11524
  50.0 30.7 %copy-start.26 = (f32[960]{0:T(1024)}, f32[960]{0:T(1024)S(1)}, u32[]{:S(2)}) copy-start(f32[960]{0:T(1024)S(1)} %add_rsqrt_fusion.1) | copy-start | bytes 11524
  58.8 98.7 %copy-start.20 = (f32[768]{0:T(1024)}, f32[768]{0:T(1024)S(1)}, u32[]{:S(2)}) copy-start(f32[768]{0:T(1024)S(1)} %convert_element_type.171) | copy-start | bytes 9220
  72.5 7.0 copy-start.28
  157.0 70.3 %copy-start.2 = (f32[960,768]{1,0:T(8,128)}, f32[960,768]{1,0:T(8,128)S(1)}, u32[]{:S(2)}) copy-start(f32[960,768]{1,0:T(8,128)S(1)} %get-tuple-element.359) | copy-start | bytes 8847364
  208.9 12.5 %copy-start.42 = (bf16[768,3072]{1,0:T(8,128)(2,1)S(1)}, bf16[768,3072]{1,0:T(8,128)(2,1)}, u32[]{:S(2)}) copy-start(bf16[768,3072]{1,0:T(8,128)(2,1)} %all-gather.13.cloned.1.call-done) | copy-start | bytes 14155780
  242.3 190.2 %reduce-scatter.17.cloned.1.call-start = ((), (), s32[]{:S(2)}) async-start(), calls=%async_computation.15 | async-start | bytes 3538944 | tf_op jit(solution)/shard_map/reduce_scatter | solution.py:284
  247.4 234.9 %reduce-scatter.9.cloned.1.call-start = ((), (), s32[]{:S(2)}) async-start(), calls=%async_computation.11 | async-start | bytes 7962624 | tf_op jit(solution)/shard_map/reduce_scatter | solution.py:274
  311.7 5.9 slice-start
  405.9 176.6 %reduce-scatter.13.cloned.1.call-start = ((), (), s32[]{:S(2)}) async-start(), calls=%async_computation.13 | async-start | bytes 10616832 | tf_op jit(solution)/shard_map/reduce_scatter | solution.py:280
  418.2 264.3 %reduce-scatter.15.cloned.1.call-start = ((), (), s32[]{:S(2)}) async-start(), calls=%async_computation.14 | async-start | bytes 10616832 | tf_op jit(solution)/shard_map/reduce_scatter | solution.py:282
  429.8 310.5 %reduce-scatter.19.cloned.1.call-start = ((), (), s32[]{:S(2)}) async-start(), calls=%async_computation.16 | async-start | bytes 442368
  431.2 253.5 %copy-start.40 = (bf16[128]{0:T(256)(128)(2,1)S(1)}, bf16[128]{0:T(256)(128)(2,1)}, u32[]{:S(2)}) copy-start(bf16[128]{0:T(256)(128)(2,1)} %param.36) | copy-start | bytes 772
  432.5 385.4 %all-reduce.20.cloned.1.call-start = ((), (), s32[]{:S(2)}) async-start(), calls=%async_computation.17 | async-start | bytes 7864320 | tf_op jit(solution)/shard_map/psum | solution.py:287
  682.6 13.2 %copy-start.6 = (bf16[960,768]{1,0:T(8,128)(2,1)S(1)}, bf16[960,768]{1,0:T(8,128)(2,1)}, u32[]{:S(2)}) copy-start(bf16[960,768]{1,0:T(8,128)(2,1)} %param.22) | copy-start | bytes 4423684
  695.8 9.1 %copy-start.30 = (f32[3072]{0:T(1024)S(1)}, f32[3072]{0:T(1024)}, u32[]{:S(2)}) copy-start(f32[3072]{0:T(1024)} %get-tuple-element.366) | copy-start | bytes 36868
  695.8 9.1 %copy-start.31 = (f32[768]{0:T(1024)S(1)}, f32[768]{0:T(1024)}, u32[]{:S(2)}) copy-start(f32[768]{0:T(1024)} %get-tuple-element.341) | copy-start | bytes 9220
  695.8 9.1 %copy-start.32 = (f32[768]{0:T(1024)S(1)}, f32[768]{0:T(1024)}, u32[]{:S(2)}) copy-start(f32[768]{0:T(1024)} %get-tuple-element.263) | copy-start | bytes 9220
  695.8 9.1 %copy-start.33 = (f32[768]{0:T(1024)S(1)}, f32[768]{0:T(1024)}, u32[]{:S(2)}) copy-start(f32[768]{0:T(1024)} %get-tuple-element.269) | copy-start | bytes 9220
  695.8 9.1 %copy-start.34 = (f32[768]{0:T(1024)S(1)}, f32[768]{0:T(1024)}, u32[]{:S(2)}) copy-start(f32[768]{0:T(1024)} %get-tuple-element.343) | copy-start | bytes 9220
  817.9 6.8 copy-start.1
  (40 other events, 153.8 us)
Sparse Core Ops, SparseCore 0:
  9.7 28.1 all-gather.16
  39.6 41.0 all-gather.8
  82.3 21.5 all-gather.10
  105.3 51.4 all-gather.12
  158.3 50.5 all-gather.14
  242.5 35.0 reduce-scatter.10
  279.8 39.7 reduce-scatter.16
  406.0 76.2 reduce-scatter.8
  484.6 97.8 reduce-scatter.12
  584.7 97.8 reduce-scatter.14
  685.4 29.0 reduce-scatter.18
  718.4 99.4 all-reduce.19
where the time goes:
time: 840 us; the launch traced here: 832 us
  waiting for transfers between devices  337 us (40%)
  matrix products  239 us (28%)
  blocking collectives  99.2 us (12%)
  local copies, waits for them, and re-layouts  85.3 us (10%)
  other arithmetic  43.5 us (5%)
  between operations  17.8 us (2%)
  loops' own time  9.26 us (1%)
    reduce_scatter x1, waiting for transfers between devices, local(): lax.psum_scatter(grad_up, 'fsdp', scatter_dimension=0, tiled=True)  100 us
    reduce_scatter x1, waiting for transfers between devices, local(): lax.psum_scatter(grad_down, 'fsdp', scatter_dimension=0, tiled=True)  100 us
    psum x1, waiting for transfers between devices, local(): lax.psum((part_gain_one, part_shift_one, part_qkv, part_qv, part_proj, pa...  66.3 us
    unnamed x2, blocking collectives  57.9 us
    reduce_scatter x1, waiting for transfers between devices, local(): lax.psum_scatter(grad_qkv, 'fsdp', scatter_dimension=0, tiled=True)  49.7 us
    dot_general x5, matrix products, dot_left_t(): lax.dot_general(left, right, (((0,), (0,)), ((), ())), preferred_element_...  38.6 us
    dot_general x5, matrix products, dot_right_t(): lax.dot_general(left, right, (((1,), (1,)), ((), ())), preferred_element_...  37.5 us
    dot_general x12, matrix products, pair_slices(): jnp.einsum('qhd,khd->hqk', query_pair, key_pair, preferred_element_type=j...  35.4 us
  transfers between devices with their start and end apart: 12, of which 6 were waited for; matrix products, arithmetic and copies ran while one was open for 38% of the time, Pallas kernels for 0%

commit v1 on v0

v1 whole, which is shorter than its diff:
```python
import functools
import math

import jax
import jax.numpy as jnp
from jax import lax
from jax.experimental import pallas as pl
from jax.experimental.pallas import tpu as pltpu
from jax.sharding import PartitionSpec as P

HEADS = 12
LONGEST = 157
EPSILON = 1e-06
MASKED = -1e30
VMEM_BYTES = 56 * 1024 * 1024
TILE = 128

f32 = jnp.float32
bf16 = jnp.bfloat16


def dot_nn(left, right):
    return lax.dot_general(left, right, (((1,), (0,)), ((), ())), preferred_element_type=f32)


def dot_nt(left, right):
    return lax.dot_general(left, right, (((1,), (1,)), ((), ())), preferred_element_type=f32)


def dot_tn(left, right):
    return lax.dot_general(left, right, (((0,), (0,)), ((), ())), preferred_element_type=f32)


def attention_tiles(rows):
    tiles, offset = [], 0
    reach = LONGEST - 1
    for start in range(0, rows, TILE):
        size = min(TILE, rows - start)
        low = max(0, (start - reach) // 16 * 16)
        high = min(rows, -(-(start + size + reach) // 16) * 16)
        tiles.append((start, size, low, high - low, offset))
        offset += high - low
    return tiles, offset


def row_tile(rows, most):
    for size in range(most, 15, -16):
        if rows % size == 0:
            return size
    return rows


def params(*semantics):
    return pltpu.CompilerParams(vmem_limit_bytes=VMEM_BYTES)


def whole(shape):
    return pl.BlockSpec(shape, lambda *_: (0,) * len(shape), pipeline_mode=pl.Buffered(1))


def out_whole(shape):
    return pl.BlockSpec(shape, lambda *_: (0,) * len(shape))


SMEM = pl.BlockSpec(memory_space=pltpu.SMEM)


def mask_kernel(tiles, seq_ref, counts_ref, bias_ref, seg_ref):
    rows = seg_ref.shape[0]
    slots = counts_ref.shape[1]
    seq = seq_ref[0]
    ends, total = [], jnp.int32(0)
    for slot in range(slots):
        total = total + counts_ref[seq, slot]
        ends.append(total)
    places = lax.broadcasted_iota(jnp.int32, (rows, TILE), 0)
    seg = jnp.zeros((rows, TILE), jnp.int32)
    for end in ends:
        seg = seg + jnp.where(places >= end, 1, 0)
    seg_ref[...] = seg
    lanes = lax.broadcasted_iota(jnp.int32, (8, TILE), 1)
    for start, size, low, keys, offset in tiles:
        own = start + jnp.where(lanes >= size, lanes - size, lanes)
        seg_own = jnp.zeros((8, TILE), jnp.int32)
        for end in ends:
            seg_own = seg_own + jnp.where(own >= end, 1, 0)
        same = seg_ref[low : low + keys, :] == seg_own[0:1, :]
        bias_ref[offset : offset + keys, :] = jnp.where(same, 0.0, MASKED).astype(f32)


def make_masks(seq, counts, rows):
    tiles, total = attention_tiles(rows)
    return pl.pallas_call(
        functools.partial(mask_kernel, tiles),
        out_shape=jax.ShapeDtypeStruct((total, TILE), f32),
        in_specs=[SMEM, SMEM],
        out_specs=pl.BlockSpec(memory_space=pltpu.VMEM),
        scratch_shapes=[pltpu.VMEM((rows, TILE), jnp.int32)],
        compiler_params=params(),
        name="masks",
    )(seq, counts)


def normed(values):
    center = values - jnp.mean(values, axis=-1, keepdims=True)
    spread = jnp.mean(center * center, axis=-1, keepdims=True)
    inverse = lax.rsqrt(spread + EPSILON)
    return center * inverse, inverse


def qkv_kernel(scale, tok_ref, gain_ref, shift_ref, w_ref, qvb_ref, h_ref, q_ref, k_ref, v_ref):
    width = tok_ref.shape[1]
    n1, _ = normed(tok_ref[...].astype(f32))
    hidden = (n1 * gain_ref[...].astype(f32) + shift_ref[...].astype(f32)).astype(bf16)
    h_ref[...] = hidden
    qvb = qvb_ref[...].astype(f32)
    q = dot_nn(hidden, w_ref[:, :width])
    q_ref[...] = ((q + qvb[0:1, :]) * scale).astype(bf16)
    k = dot_nn(hidden, w_ref[:, width : 2 * width])
    k_ref[...] = k.astype(bf16)
    v = dot_nn(hidden, w_ref[:, 2 * width :])
    v_ref[...] = (v + qvb[1:2, :]).astype(bf16)


def project_qkv(tokens, gain, shift, w_qkv, qv_bias):
    rows, width = tokens.shape
    scale = (width // HEADS) ** (-0.5)
    size = row_tile(rows, 320)
    rowwise = pl.BlockSpec((size, width), lambda i: (i, 0))
    out = jax.ShapeDtypeStruct((rows, width), bf16)
    return pl.pallas_call(
        functools.partial(qkv_kernel, scale),
        grid=(rows // size,),
        out_shape=(out,) * 4,
        in_specs=[rowwise, whole(gain.shape), whole(shift.shape), whole(w_qkv.shape), whole(qv_bias.shape)],
        out_specs=(rowwise,) * 4,
        compiler_params=params(),
        name="norm_qkv",
    )(tokens, gain, shift, w_qkv, qv_bias)


def stack_heads(pair, size):
    lanes = lax.broadcasted_iota(jnp.int32, pair.shape, 1)
    half = pair.shape[1] // 2
    zero = jnp.zeros_like(pair)
    first = jnp.where(lanes < half, pair, zero)
    second = jnp.where(lanes < half, zero, pair)
    return jnp.concatenate([first, second], axis=0)


def both(bias, size):
    return bias if size < TILE else jnp.concatenate([bias, bias], axis=1)


def unstack(columns, size, half):
    return jnp.concatenate([columns[:half, :size], columns[half:, size:]], axis=0).T


def attend_kernel(tiles, bias_ref, q_ref, k_ref, v_ref, o_ref, lse_ref):
    half = q_ref.shape[1] // 2
    for index, (start, size, low, keys, offset) in enumerate(tiles):
        stacked = stack_heads(q_ref[start : start + size, :], size)
        scores = dot_nt(k_ref[low : low + keys, :], stacked)
        scores = scores + both(bias_ref[offset : offset + keys, :], size)
        top = jnp.max(scores, axis=0, keepdims=True)
        weights = jnp.exp(scores - top)
        total = jnp.sum(weights, axis=0, keepdims=True)
        probs = (weights * (1.0 / total)).astype(bf16)
        columns = dot_tn(v_ref[low : low + keys, :], probs)
        o_ref[start : start + size, :] = unstack(columns, size, half).astype(bf16)
        lse_ref[0, index : index + 1, : 2 * size] = top + jnp.log(total)


def attend(bias, q, k, v):
    rows, width = q.shape
    tiles, _ = attention_tiles(rows)
    span = 2 * (width // HEADS)
    pairs = HEADS // 2
    column = pl.BlockSpec((rows, span), lambda p: (0, p))
    return pl.pallas_call(
        functools.partial(attend_kernel, tiles),
        grid=(pairs,),
        out_shape=(
            jax.ShapeDtypeStruct((rows, width), bf16),
            jax.ShapeDtypeStruct((pairs, len(tiles), 2 * TILE), f32),
        ),
        in_specs=[whole(bias.shape), column, column, column],
        out_specs=(column, pl.BlockSpec((1, len(tiles), 2 * TILE), lambda p: (p, 0, 0))),
        compiler_params=params(),
        name="attend",
    )(bias, q, k, v)


def attend_back_kernel(
    tiles, scale, bias_ref, q_ref, k_ref, v_ref, o_ref, do_ref, lse_ref, dq_ref, dk_ref, dv_ref, dqv_ref, dk_sum, dv_sum
):
    half = q_ref.shape[1] // 2
    dk_sum[...] = jnp.zeros_like(dk_sum)
    dv_sum[...] = jnp.zeros_like(dv_sum)
    dq_total = jnp.zeros((1, 2 * half), f32)
    for index, (start, size, low, keys, offset) in enumerate(tiles):
        window = slice(low, low + keys)
        rows = slice(start, start + size)
        q2 = stack_heads(q_ref[rows, :], size)
        grads = do_ref[rows, :]
        do2 = stack_heads(grads, size)
        scores = dot_nt(k_ref[window, :], q2) + both(bias_ref[offset : offset + keys, :], size)
        probs = jnp.exp(scores - lse_ref[0, index : index + 1, : 2 * size])
        dprobs = dot_nt(v_ref[window, :], do2)
        meet = (grads.astype(f32) * o_ref[rows, :].astype(f32)).T
        delta = jnp.concatenate(
            [
                jnp.sum(meet[:half, :], axis=0, keepdims=True),
                jnp.sum(meet[half:, :], axis=0, keepdims=True),
            ],
            axis=1,
        )
        dv_sum[window, :] += dot_nn(probs.astype(bf16), do2)
        dscores = (probs * (dprobs - delta)).astype(bf16)
        dk_sum[window, :] += dot_nn(dscores, q2)
        columns = dot_tn(k_ref[window, :], dscores)
        dq = unstack(columns, size, half).astype(bf16) * bf16(scale)
        dq_ref[rows, :] = dq
        dq_total = dq_total + jnp.sum(dq.astype(f32), axis=0, keepdims=True)
    dk_ref[...] = dk_sum[...].astype(bf16)
    dv = dv_sum[...].astype(bf16)
    dv_ref[...] = dv
    dqv_ref[0:1, :] = dq_total
    dqv_ref[1:2, :] = jnp.sum(dv.astype(f32), axis=0, keepdims=True)


def attend_back(bias, q, k, v, o, do, lse):
    rows, width = q.shape
    tiles, _ = attention_tiles(rows)
    span = 2 * (width // HEADS)
    pairs = HEADS // 2
    scale = (width // HEADS) ** (-0.5)
    column = pl.BlockSpec((rows, span), lambda p: (0, p))
    out = jax.ShapeDtypeStruct((rows, width), bf16)
    return pl.pallas_call(
        functools.partial(attend_back_kernel, tiles, scale),
        grid=(pairs,),
        out_shape=(out, out, out, jax.ShapeDtypeStruct((2, width), f32)),
        in_specs=[whole(bias.shape)]
        + [column] * 5
        + [pl.BlockSpec((1, len(tiles), 2 * TILE), lambda p: (p, 0, 0))],
        out_specs=(column, column, column, pl.BlockSpec((2, span), lambda p: (0, p))),
        scratch_shapes=[pltpu.VMEM((rows, span), f32), pltpu.VMEM((rows, span), f32)],
        compiler_params=params(),
        name="attend_back",
    )(bias, q, k, v, o, do, lse)


PARTS = 4


def middle_kernel(
    seq_ref,
    counts_ref,
    tok_ref,
    o_ref,
    cot_out_ref,
    cot_align_ref,
    w_proj_ref,
    w_up_ref,
    w_down_ref,
    w_head_ref,
    b_proj_ref,
    gain_ref,
    shift_ref,
    b_up_ref,
    b_down_ref,
    b_head_ref,
    out_ref,
    aligned_ref,
    z_ref,
    e_ref,
    h_ref,
    g_ref,
    du_ref,
    dm_ref,
    dx_ref,
    da_ref,
    do_ref,
    s_head_ref,
    s_down_ref,
    s_up_ref,
    s_gain_ref,
    s_shift_ref,
    s_proj_ref,
):
    step = pl.program_id(0)
    size, width = tok_ref.shape
    hidden_units = w_up_ref.shape[1]
    part = hidden_units // PARTS
    seq = seq_ref[0]
    total = jnp.int32(0)
    for slot in range(counts_ref.shape[1]):
        total = total + counts_ref[seq, slot]
    places = lax.broadcasted_iota(jnp.int32, (size, 1), 0) + step * size
    valid = jnp.where(places < total, 1.0, 0.0).astype(f32)

    @pl.when(step == 0)
    def _():
        for ref in (s_head_ref, s_down_ref, s_up_ref, s_gain_ref, s_shift_ref, s_proj_ref):
            ref[...] = jnp.zeros_like(ref)

    x1 = tok_ref[...].astype(f32) + dot_nn(o_ref[...], w_proj_ref[...]) + b_proj_ref[...].astype(f32)
    n2, inverse = normed(x1)
    gain = gain_ref[...].astype(f32)
    h2 = (n2 * gain + shift_ref[...].astype(f32)).astype(bf16)
    h_ref[...] = h2

    e_al = (cot_align_ref[...].astype(f32) * valid).astype(bf16)
    e_ref[...] = e_al
    s_head_ref[...] += jnp.sum(e_al.astype(f32), axis=0, keepdims=True)
    dx2 = cot_out_ref[...].astype(f32) * valid + dot_nt(e_al, w_head_ref[...])
    dm = dx2.astype(bf16)
    dm_ref[...] = dm
    s_down_ref[...] += jnp.sum(dm.astype(f32), axis=0, keepdims=True)

    x2 = x1 + b_down_ref[...].astype(f32)
    dh2 = jnp.zeros((size, width), f32)
    for index in range(PARTS):
        span = slice(index * part, (index + 1) * part)
        u = dot_nn(h2, w_up_ref[:, span]) + b_up_ref[:, span].astype(f32)
        cdf = 0.5 * (1.0 + lax.erf(u * (1.0 / math.sqrt(2.0))))
        pdf = jnp.exp(-0.5 * u * u) * (1.0 / math.sqrt(2.0 * math.pi))
        g = (u * cdf).astype(bf16)
        g_ref[:, span] = g
        x2 = x2 + dot_nn(g, w_down_ref[span, :])
        du = (dot_nt(dm, w_down_ref[span, :]) * (cdf + u * pdf)).astype(bf16)
        du_ref[:, span] = du
        s_up_ref[:, span] += jnp.sum(du.astype(f32), axis=0, keepdims=True)
        dh2 = dh2 + dot_nt(du, w_up_ref[:, span])
    out_ref[...] = (x2 * valid).astype(bf16)
    z = x2.astype(bf16)
    z_ref[...] = z
    aligned_ref[...] = ((dot_nn(z, w_head_ref[...]) + b_head_ref[...].astype(f32)) * valid).astype(bf16)

    s_gain_ref[...] += jnp.sum(dh2 * n2, axis=0, keepdims=True)
    s_shift_ref[...] += jnp.sum(dh2, axis=0, keepdims=True)
    t = dh2 * gain
    inner = t - jnp.mean(t, axis=-1, keepdims=True) - n2 * jnp.mean(t * n2, axis=-1, keepdims=True)
    dx1 = dx2 + inverse * inner
    dx_ref[...] = dx1
    da = dx1.astype(bf16)
    da_ref[...] = da
    s_proj_ref[...] += jnp.sum(da.astype(f32), axis=0, keepdims=True)
    do_ref[...] = dot_nt(da, w_proj_ref[...]).astype(bf16)


def middle(seq, counts, tokens, o, cot_out, cot_align, w_proj, w_up, w_down, w_head, small):
    rows, width = tokens.shape
    hidden, align = w_up.shape[1], w_head.shape[1]
    size = row_tile(rows, 240)

    def by_row(columns):
        return pl.BlockSpec((size, columns), lambda i: (i, 0))

    def row_shape(columns, dtype=bf16):
        return jax.ShapeDtypeStruct((rows, columns), dtype)

    outs = [
        (by_row(width), row_shape(width)),
        (by_row(align), row_shape(align)),
        (by_row(width), row_shape(width)),
        (by_row(align), row_shape(align)),
        (by_row(width), row_shape(width)),
        (by_row(hidden), row_shape(hidden)),
        (by_row(hidden), row_shape(hidden)),
        (by_row(width), row_shape(width)),
        (by_row(width), row_shape(width, f32)),
        (by_row(width), row_shape(width)),
        (by_row(width), row_shape(width)),
    ]
    for columns in (align, width, hidden, width, width, width):
        outs.append((out_whole((1, columns)), jax.ShapeDtypeStruct((1, columns), f32)))
    weights = (w_proj, w_up, w_down, w_head) + tuple(small)
    return pl.pallas_call(
        middle_kernel,
        grid=(rows // size,),
        out_shape=tuple(shape for _, shape in outs),
        in_specs=[SMEM, SMEM, by_row(width), by_row(width), by_row(width), by_row(align)]
        + [whole(w.shape) for w in weights],
        out_specs=tuple(spec for spec, _ in outs),
        compiler_params=params(),
        name="middle",
    )(seq, counts, tokens, o, cot_out, cot_align, *weights)


def outer_kernel(l_ref, r_ref, out_ref):
    out_ref[...] = dot_tn(l_ref[...], r_ref[...]).astype(out_ref.dtype)


def outer(left, right, rows_out, columns_out, name):
    rows, m = left.shape
    n = right.shape[1]
    tm, tn = min(rows_out, m), min(columns_out, n)
    return pl.pallas_call(
        outer_kernel,
        grid=(m // tm, n // tn),
        out_shape=jax.ShapeDtypeStruct((m, n), bf16),
        in_specs=[
            pl.BlockSpec((rows, tm), lambda i, j: (0, i)),
            pl.BlockSpec((rows, tn), lambda i, j: (0, j)),
        ],
        out_specs=pl.BlockSpec((tm, tn), lambda i, j: (i, j)),
        compiler_params=params(),
        name=name,
    )(left, right)


def first_back_kernel(tok_ref, dx_ref, dq_ref, dk_ref, dv_ref, w_ref, gain_ref, out_ref, s_gain_ref, s_shift_ref):
    width = tok_ref.shape[1]

    @pl.when(pl.program_id(0) == 0)
    def _():
        s_gain_ref[...] = jnp.zeros_like(s_gain_ref)
        s_shift_ref[...] = jnp.zeros_like(s_shift_ref)

    dh = dot_nt(dq_ref[...], w_ref[:, :width])
    dh = dh + dot_nt(dk_ref[...], w_ref[:, width : 2 * width])
    dh = dh + dot_nt(dv_ref[...], w_ref[:, 2 * width :])
    n1, inverse = normed(tok_ref[...].astype(f32))
    s_gain_ref[...] += jnp.sum(dh * n1, axis=0, keepdims=True)
    s_shift_ref[...] += jnp.sum(dh, axis=0, keepdims=True)
    t = dh * gain_ref[...].astype(f32)
    inner = t - jnp.mean(t, axis=-1, keepdims=True) - n1 * jnp.mean(t * n1, axis=-1, keepdims=True)
    out_ref[...] = (dx_ref[...] + inverse * inner).astype(bf16)


def first_back(tokens, dx1, dq, dk, dv, w_qkv, gain):
    rows, width = tokens.shape
    size = row_tile(rows, 320)
    rowwise = pl.BlockSpec((size, width), lambda i: (i, 0))
    total = jax.ShapeDtypeStruct((1, width), f32)
    return pl.pallas_call(
        first_back_kernel,
        grid=(rows // size,),
        out_shape=(jax.ShapeDtypeStruct((rows, width), bf16), total, total),
        in_specs=[rowwise] * 5 + [whole(w_qkv.shape), whole(gain.shape)],
        out_specs=(rowwise, out_whole((1, width)), out_whole((1, width))),
        compiler_params=params(),
        name="first_back",
    )(tokens, dx1, dq, dk, dv, w_qkv, gain)


def local(
    tokens,
    ln1_gain,
    ln1_bias,
    w_qkv,
    qv_bias,
    w_proj,
    proj_bias,
    ln2_gain,
    ln2_bias,
    w_up,
    up_bias,
    w_down,
    down_bias,
    w_head,
    head_bias,
    clip_counts,
    cot_out,
    cot_align,
):
    rows, width = tokens.shape
    shards = lax.axis_size("fsdp")

    def gather(value):
        return lax.all_gather(value, "fsdp", axis=0, tiled=True)

    vectors = (ln1_gain, ln1_bias, qv_bias[0], qv_bias[1], proj_bias, ln2_gain, ln2_bias, up_bias, down_bias, head_bias)
    packed = gather(jnp.concatenate(vectors)[None])
    parts, at = [], 0
    for vector in vectors:
        parts.append(packed[:, at : at + vector.shape[0]].reshape(1, -1))
        at += vector.shape[0]
    gain_one, shift_one, b_q, b_v, b_proj, gain_two, shift_two, b_up, b_down, b_head = parts
    full_qkv, full_proj, full_up, full_down, full_head = (gather(w) for w in (w_qkv, w_proj, w_up, w_down, w_head))

    seq = (lax.axis_index("dp") * shards + lax.axis_index("fsdp")).astype(jnp.int32)[None]
    bias = make_masks(seq, clip_counts, rows)
    h1, q, k, v = project_qkv(tokens, gain_one, shift_one, full_qkv, jnp.concatenate([b_q, b_v]))
    o, lse = attend(bias, q, k, v)
    (block_out, aligned, z, e_al, h2, g, du, dm, dx1, da, do, s_head, s_down, s_up, s_gain, s_shift, s_proj) = middle(
        seq,
        clip_counts,
        tokens,
        o,
        cot_out,
        cot_align,
        full_proj,
        full_up,
        full_down,
        full_head,
        (b_proj, gain_two, shift_two, b_up, b_down, b_head),
    )
    g_up = outer(h2, du, 768, 512, "grad_up")
    g_down = outer(g, dm, 512, 768, "grad_down")
    g_head = outer(z, e_al, 768, 512, "grad_head")
    g_proj = outer(o, da, 768, 384, "grad_proj")
    dq, dk, dv, s_qv = attend_back(bias, q, k, v, o, do, lse)
    grad_tokens, s_gain_one, s_shift_one = first_back(tokens, dx1, dq, dk, dv, full_qkv, gain_one)
    g_qkv = outer(h1, jnp.concatenate([dq, dk, dv], axis=1), 768, 768, "grad_qkv")

    def reduce(value):
        part = lax.psum_scatter(value, "fsdp", scatter_dimension=0, tiled=True)
        return lax.psum(part.astype(f32), "dp")

    d_up, d_down, d_head, d_proj, d_qkv = (reduce(w) for w in (g_up, g_down, g_head, g_proj, g_qkv))
    sums = (s_gain_one, s_shift_one, s_qv[0:1], s_qv[1:2], s_proj, s_gain, s_shift, s_up, s_down, s_head)
    packed = jnp.concatenate([s.reshape(shards, -1) for s in sums], axis=1)
    mine = lax.psum(lax.psum_scatter(packed, "fsdp", scatter_dimension=0, tiled=True), "dp")[0]
    parts, at = [], 0
    for vector in vectors:
        parts.append(mine[at : at + vector.shape[0]])
        at += vector.shape[0]
    return (
        block_out,
        aligned,
        grad_tokens,
        parts[0],
        parts[1],
        d_qkv,
        jnp.stack([parts[2], parts[3]]),
        d_proj,
        parts[4],
        parts[5],
        parts[6],
        d_up,
        parts[7],
        d_down,
        parts[8],
        d_head,
        parts[9],
    )


def solution(mesh):
    rows = P(("dp", "fsdp"), None)
    matrix, vector, pair = P("fsdp", None), P("fsdp"), P(None, "fsdp")
    return jax.shard_map(
        local,
        mesh=mesh,
        in_specs=(
            rows,
            vector,
            vector,
            matrix,
            pair,
            matrix,
            vector,
            vector,
            vector,
            matrix,
            vector,
            matrix,
            vector,
            matrix,
            vector,
            P(),
            rows,
            rows,
        ),
        out_specs=(
            rows,
            rows,
            rows,
            vector,
            vector,
            matrix,
            pair,
            matrix,
            vector,
            vector,
            vector,
            matrix,
            vector,
            matrix,
            vector,
            matrix,
            vector,
        ),
        check_vma=False,
    )
```

time: 840 us -> 617 us (0.73)
  matrix products: 239 us -> 0 us
  Pallas kernels: 0 us -> 135 us
  blocking collectives: 99.2 us -> 178 us
  local copies, waits for them, and re-layouts: 85.3 us -> 10.6 us
  waiting for transfers between devices: 337 us -> 269 us
  other arithmetic: 43.5 us -> 7.1 us
  loops' own time: 9.26 us -> 0 us
    dot_general x57 -> x0, matrix products: 239 us -> none  [the longest x5 38.6 us: dot_left_t(): lax.dot_general(left, right, (((0,), (0,)), ((), ())), preferred_element_...]
    pallas_call x0 -> x11, Pallas kernels: none -> 135 us  [the longest x5 36.7 us: outer(): pl.pallas_call(outer_kernel, grid=(m // tm, n // tn), out_shape=jax.Shape...]
    reduce_scatter x5, waiting for transfers between devices: 250 us -> 125 us  [reduce(): part = lax.psum_scatter(value, 'fsdp', scatter_dimension=0, tiled=True)]
    all_gather x5, waiting for transfers between devices: 17.3 us -> 141 us  [gather(): return lax.all_gather(value, 'fsdp', axis=0, tiled=True)]
    psum x1, blocking collectives: 10.6 us -> 134 us  [local(): lax.psum(lax.psum_scatter(packed, 'fsdp', scatter_dimension=0, tiled=True...]
    psum x1 -> x0, waiting for transfers between devices: 66.3 us -> none  [local(): lax.psum((part_gain_one, part_shift_one, part_qkv, part_qv, part_proj, pa...]
    dynamic_slice x54 -> x0, local copies, waits for them, and re-layouts: 37.3 us -> none  [the longest x12 11.8 us: pair_slices(): lax.dynamic_slice_in_dim(keys_all, start, span, 1)]
    unnamed x2 -> x1, blocking collectives: 57.9 us -> 28.6 us
  transfers between devices with their start and end apart: 12 -> 10, of which waited for: 6 -> 7; matrix products, arithmetic and copies ran while one was open for 38% -> 2% of each run, Pallas kernels for 0% -> 15%
where the time goes in v1:
time: 617 us; the launch traced here: 615 us
  waiting for transfers between devices  269 us (44%)
  blocking collectives  178 us (29%)
  Pallas kernels  135 us (22%)
  between operations  14.5 us (2%)
  local copies, waits for them, and re-layouts  10.6 us (2%)
  other arithmetic  7.1 us (1%)
    all_gather x5, waiting for transfers between devices, gather(): return lax.all_gather(value, 'fsdp', axis=0, tiled=True)  141 us
    psum x1, blocking collectives, local(): lax.psum(lax.psum_scatter(packed, 'fsdp', scatter_dimension=0, tiled=True...  134 us
    reduce_scatter x5, waiting for transfers between devices, reduce(): part = lax.psum_scatter(value, 'fsdp', scatter_dimension=0, tiled=True)  125 us
    pallas_call x5, Pallas kernels, outer(): pl.pallas_call(outer_kernel, grid=(m // tm, n // tn), out_shape=jax.Shape...  36.7 us
    pallas_call x1, Pallas kernels, middle(): pl.pallas_call(middle_kernel, grid=(rows // size,), out_shape=tuple((shap...  35.8 us
    unnamed x1, blocking collectives  28.6 us
    pallas_call x1, Pallas kernels, attend(): pl.pallas_call(functools.partial(attend_kernel, tiles), grid=(pairs,), ou...  22.9 us
    pallas_call x1, Pallas kernels, attend_back(): pl.pallas_call(functools.partial(attend_back_kernel, tiles, scale), grid=...  18.3 us
  transfers between devices with their start and end apart: 10, of which 7 were waited for; matrix products, arithmetic and copies ran while one was open for 2% of the time, Pallas kernels for 15%

profile of v1, /device:TPU:0, one launch (start us, length us, event | category | flops | bytes accessed | tf_op | source)
XLA Modules:
  0.0 614.8 jit_solution(11129701236991469560)
XLA Ops:
  7.3 0.7 all-gather.8.cloned.1.call-update
  8.1 0.7 all-gather.10.cloned.1.call-update
  8.8 0.7 all-gather.16.cloned.1.call-update
  10.9 15.7 %all-gather.1 = bf16[8,1,1280]{2,1,0:T(2,128)(2,1)S(1)} all-gather(bf16[1,1,1280]{2,1,0:T(2,128)(2,1)S(1)} %reshape.127), channel_id=2, replica_groups=mesh['dp'=4,'fsdp'=8] {'fsdp'}, dimensions={0}, use_global_device_ids=true | all-gather | bytes 23040 | tf_op jit(solution)/shard_map/all_gather | solution.py:473
  26.9 0.7 reshape.106.gain_ref
  28.3 0.7 reshape.110.b_proj_ref
  28.9 0.7 reshape.111.gain_ref
  30.3 0.7 reshape.114.b_down_ref
  32.2 4.0 masks.1.bias_ref
  36.8 17.3 %all-gather.8.cloned.1.call-done.w_ref = bf16[768,2304]{1,0:T(8,128)(2,1)} async-done(((bf16[96,2304]{1,0:T(8,128)(2,1)}), bf16[768,2304]{1,0:T(8,128)(2,1)}) %all-gather.8.cloned.1.call-update) | async-done | bytes 3538960 | tf_op jit(solution)/shard_map/all_gather | solution.py:473
  54.1 7.7 %norm_qkv.1 = (bf16[960,768]{1,0:T(8,128)(2,1)}, bf16[960,768]{1,0:T(8,128)(2,1)}, bf16[960,768]{1,0:T(8,128)(2,1)}, bf16[960,768]{1,0:T(8,128)(2,1)}) custom-call(bf16[960,768]{1,0:T(8,128)(2,1)} %tok_ref.5, bf16[1,768]{1,0:T(2,128)(2,1)} %reshape.106.gain_ref, bf16[1,768]{1,0:T(2,128)(2,1)} %reshape.107.shift_ref, ...), custom_call_target="tpu_custom_call" | custom-call | tf_op jit(solution)/shard_map/norm_qkv/pallas_call | solution.py:131
  61.8 22.9 %attend.1 = (bf16[960,768]{1,0:T(8,128)(2,1)}, f32[6,8,256]{2,1,0:T(8,128)}) custom-call(f32[3072,128]{1,0:T(8,128)} %masks.1.bias_ref, bf16[960,768]{1,0:T(8,128)(2,1)} %get-tuple-element.47.q_ref, bf16[960,768]{1,0:T(8,128)(2,1)} %get-tuple-element.48.k_ref, bf16[960,768]{1,0:T(8,128)(2,1)} %get-tuple-element.49.v_ref), custom_call_target="tpu_custom_call" | custom-call | tf_op jit(solution)/shard_map/attend/pallas_call | solution.py:180
  84.8 19.0 %all-gather.16.cloned.1.call-done.w_head_ref = bf16[768,1024]{1,0:T(8,128)(2,1)} async-done(((bf16[96,1024]{1,0:T(8,128)(2,1)}), bf16[768,1024]{1,0:T(8,128)(2,1)}) %all-gather.16.cloned.1.call-update) | async-done | bytes 1572880 | tf_op jit(solution)/shard_map/all_gather | solution.py:473
  103.8 52.8 %all-gather.12.cloned.1.call-done.w_up_ref = bf16[768,3072]{1,0:T(8,128)(2,1)} async-done(((bf16[96,3072]{1,0:T(8,128)(2,1)}), bf16[768,3072]{1,0:T(8,128)(2,1)}) %all-gather.12.cloned.1.call-update) | async-done | bytes 4718608 | tf_op jit(solution)/shard_map/all_gather | solution.py:473
  156.6 52.0 %all-gather.14.cloned.1.call-done.w_down_ref = bf16[3072,768]{1,0:T(8,128)(2,1)} async-done(((bf16[384,768]{1,0:T(8,128)(2,1)}), bf16[3072,768]{1,0:T(8,128)(2,1)}) %all-gather.14.cloned.1.call-update) | async-done | bytes 4718608 | tf_op jit(solution)/shard_map/all_gather | solution.py:473
  208.6 35.8 %middle.1 = (bf16[960,768]{1,0:T(8,128)(2,1)}, bf16[960,1024]{1,0:T(8,128)(2,1)}, bf16[960,768]{1,0:T(8,128)(2,1)}, bf16[960,1024]{1,0:T(8,128)(2,1)}, bf16[960,...) custom-call(s32[1]{0:T(128)} %bitcast.seq_ref, ...), custom_call_target="tpu_custom_call" | custom-call | tf_op jit(solution)/shard_map/middle/pallas_call | solution.py:380
  244.4 4.5 grad_proj.1
  248.9 4.9 grad_head.1
  253.9 18.3 %attend_back.1 = (bf16[960,768]{1,0:T(8,128)(2,1)}, bf16[960,768]{1,0:T(8,128)(2,1)}, bf16[960,768]{1,0:T(8,128)(2,1)}, f32[2,768]{1,0:T(2,128)}) custom-call(f32[3072,128]{1,0:T(8,128)} %masks.1.bias_ref, bf16[960,768]{1,0:T(8,128)(2,1)} %get-tuple-element.47.q_ref, bf16[960,768]{1,0:T(8,128)(2,1)} %get-tuple-element.48.k_ref, ...), custom_call_target="tpu_custom_call" | custom-call | tf_op jit(solution)/shard_map/attend_back/pallas_call | solution.py:240
  272.2 3.8 pad_maximum_fusion.r_ref
  276.0 7.6 %grad_qkv.1 = bf16[768,2304]{1,0:T(8,128)(2,1)} custom-call(bf16[960,768]{1,0:T(8,128)(2,1)} %get-tuple-element.69.l_ref, bf16[960,2304]{1,0:T(8,128)(2,1)} %pad_maximum_fusion.r_ref), custom_call_target="tpu_custom_call" | custom-call | tf_op jit(solution)/shard_map/grad_qkv/pallas_call | solution.py:400
  283.7 9.9 %grad_down.1 = bf16[3072,768]{1,0:T(8,128)(2,1)} custom-call(bf16[960,3072]{1,0:T(8,128)(2,1)} %get-tuple-element.73.l_ref, bf16[960,768]{1,0:T(8,128)(2,1)} %get-tuple-element.74.r_ref), custom_call_target="tpu_custom_call" | custom-call | tf_op jit(solution)/shard_map/grad_down/pallas_call | solution.py:400
  293.7 9.9 %grad_up.1 = bf16[768,3072]{1,0:T(8,128)(2,1)} custom-call(bf16[960,768]{1,0:T(8,128)(2,1)} %get-tuple-element.71.l_ref, bf16[960,3072]{1,0:T(8,128)(2,1)} %get-tuple-element.72.r_ref), custom_call_target="tpu_custom_call" | custom-call | tf_op jit(solution)/shard_map/grad_up/pallas_call | solution.py:400
  304.9 9.5 %first_back.1 = (bf16[960,768]{1,0:T(8,128)(2,1)}, f32[1,768]{1,0:T(1,128)}, f32[1,768]{1,0:T(1,128)}) custom-call(bf16[960,768]{1,0:T(8,128)(2,1)} %tok_ref.5, f32[960,768]{1,0:T(8,128)} %get-tuple-element.53.dx_ref, bf16[960,768]{1,0:T(8,128)(2,1)} %get-tuple-element.56.dq_ref, bf16[960,768]{1,0:T(8,128)(2,1)} %get-tuple-element.57.dk_ref, ...), custom_call_target="tpu_custom_call" | custom-call | tf_op jit(solution)/shard_map/first_back/pallas_call | solution.py:438
  314.4 0.7 reduce
  315.1 0.7 reduce.1
  316.6 0.7 reduce.15
  317.8 28.6 %all-reduce = f32[8,1280]{1,0:T(8,128)S(1)} all-reduce(f32[8,1280]{1,0:T(8,128)S(1)} %concatenate.14), channel_id=3, replica_groups=mesh['dp'=4,'fsdp'=8] {'fsdp'}, use_global_device_ids=true, to_apply=%region_0.0.clone | all-reduce | flops 10240 | bytes 81920
  347.1 13.4 %reduce-scatter.6.cloned.1.call-done = bf16[96,2304]{1,0:T(8,128)(2,1)} async-done(((bf16[768,2304]{1,0:T(8,128)(2,1)}), bf16[96,2304]{1,0:T(8,128)(2,1)}) %reduce-scatter.6.cloned.1.call-update) | async-done | bytes 442384 | tf_op jit(solution)/shard_map/reduce_scatter | solution.py:510
  360.5 55.9 %reduce-scatter.12.cloned.1.call-done = bf16[384,768]{1,0:T(8,128)(2,1)} async-done(((bf16[3072,768]{1,0:T(8,128)(2,1)}), bf16[384,768]{1,0:T(8,128)(2,1)}) %reduce-scatter.12.cloned.1.call-update) | async-done | bytes 589840 | tf_op jit(solution)/shard_map/reduce_scatter | solution.py:510
  416.4 55.6 %reduce-scatter.10.cloned.1.call-done = bf16[96,3072]{1,0:T(8,128)(2,1)} async-done(((bf16[768,3072]{1,0:T(8,128)(2,1)}), bf16[96,3072]{1,0:T(8,128)(2,1)}) %reduce-scatter.10.cloned.1.call-update) | async-done | bytes 589840 | tf_op jit(solution)/shard_map/reduce_scatter | solution.py:510
  472.0 133.6 %all-reduce.3 = (f32[1,1280]{1,0:T(1,128)S(1)}, f32[96,2304]{1,0:T(8,128)}, f32[96,768]{1,0:T(8,128)}, f32[96,3072]{1,0:T(8,128)}, f32[384,768]{1,0:T(8,128)}, /*index=5*/f32[96,1024]{1,0:T(8,128)}) all-reduce(f32[1,1280]{1,0:T(1,128)S(1)} %constant_dynamic-slice_fusion, ...), channel_id=1, replica_groups=mesh['dp'=4,'fsdp'=8] {'dp'}, use_global_device_ids=true, to_apply=%region_1.0 | all-reduce | flops 984320 | bytes 5908480 | tf_op jit(solution)/shard_map/psum | solution.py:516
  (90 shorter events, 10.7 us)
Async XLA Ops:
  7.2 3.5 copy-start.7
  7.2 3.5 copy-start.9
  7.2 3.5 copy-start.10
  7.2 3.5 copy-start.11
  7.2 3.5 copy-start.12
  7.2 3.5 copy-start.13
  7.3 3.5 copy-start.8
  7.3 3.5 copy-start.14
  7.3 3.5 copy-start.15
  7.3 46.8 %all-gather.8.cloned.1.call-start = ((), (), s32[]{:S(2)}) async-start(), calls=%async_computation.5 | async-start | bytes 3981312 | tf_op jit(solution)/shard_map/all_gather | solution.py:473
  8.0 76.7 %all-gather.10.cloned.1.call-start = ((), (), s32[]{:S(2)}) async-start(), calls=%async_computation.6 | async-start | bytes 1327104 | tf_op jit(solution)/shard_map/all_gather | solution.py:473
  8.8 95.0 %all-gather.16.cloned.1.call-start = ((), (), s32[]{:S(2)}) async-start(), calls=%async_computation.9 | async-start | bytes 1769472 | tf_op jit(solution)/shard_map/all_gather | solution.py:473
  9.5 147.0 %all-gather.12.cloned.1.call-start = ((), (), s32[]{:S(2)}) async-start(), calls=%async_computation.7 | async-start | bytes 5308416 | tf_op jit(solution)/shard_map/all_gather | solution.py:473
  10.1 198.5 %all-gather.14.cloned.1.call-start = ((), (), s32[]{:S(2)}) async-start(), calls=%async_computation.8 | async-start | bytes 5308416 | tf_op jit(solution)/shard_map/all_gather | solution.py:473
  10.7 336.4 %reduce-scatter.8.cloned.1.call-start = ((), (), s32[]{:S(2)}) async-start(), calls=%async_computation.11 | async-start | bytes 1327104 | tf_op jit(solution)/shard_map/reduce_scatter | solution.py:510
  248.9 98.2 %reduce-scatter.14.cloned.1.call-start = ((), (), s32[]{:S(2)}) async-start(), calls=%async_computation.14 | async-start | bytes 1769472 | tf_op jit(solution)/shard_map/reduce_scatter | solution.py:510
  253.8 106.7 %reduce-scatter.6.cloned.1.call-start = ((), (), s32[]{:S(2)}) async-start(), calls=%async_computation.10 | async-start | bytes 3981312 | tf_op jit(solution)/shard_map/reduce_scatter | solution.py:510
  283.7 132.7 %reduce-scatter.12.cloned.1.call-start = ((), (), s32[]{:S(2)}) async-start(), calls=%async_computation.13 | async-start | bytes 5308416 | tf_op jit(solution)/shard_map/reduce_scatter | solution.py:510
  293.6 178.4 %reduce-scatter.10.cloned.1.call-start = ((), (), s32[]{:S(2)}) async-start(), calls=%async_computation.12 | async-start | bytes 5308416 | tf_op jit(solution)/shard_map/reduce_scatter | solution.py:510
  303.6 0.7 copy-start.16
  304.8 11.1 %copy-start.1 = (f32[2,768]{1,0:T(2,128)S(1)}, f32[2,768]{1,0:T(2,128)}, u32[]{:S(2)}) copy-start(f32[2,768]{1,0:T(2,128)} %get-tuple-element.62) | copy-start | bytes 18436
  304.8 11.8 %copy-start = (f32[1,3072]{1,0:T(1,128)S(1)}, f32[1,3072]{1,0:T(1,128)}, u32[]{:S(2)}) copy-start(f32[1,3072]{1,0:T(1,128)} %get-tuple-element.66) | copy-start | bytes 36868
  304.8 12.5 %copy-start.6 = (f32[1,768]{1,0:T(1,128)S(1)}, f32[1,768]{1,0:T(1,128)}, u32[]{:S(2)}) copy-start(f32[1,768]{1,0:T(1,128)} %get-tuple-element.63) | copy-start | bytes 9220
  304.8 12.6 %copy-start.5 = (f32[1,768]{1,0:T(1,128)S(1)}, f32[1,768]{1,0:T(1,128)}, u32[]{:S(2)}) copy-start(f32[1,768]{1,0:T(1,128)} %get-tuple-element.64) | copy-start | bytes 9220
  304.8 12.7 %copy-start.4 = (f32[1,768]{1,0:T(1,128)S(1)}, f32[1,768]{1,0:T(1,128)}, u32[]{:S(2)}) copy-start(f32[1,768]{1,0:T(1,128)} %get-tuple-element.65) | copy-start | bytes 9220
  304.8 12.7 %copy-start.3 = (f32[1,768]{1,0:T(1,128)S(1)}, f32[1,768]{1,0:T(1,128)}, u32[]{:S(2)}) copy-start(f32[1,768]{1,0:T(1,128)} %get-tuple-element.67) | copy-start | bytes 9220
  304.8 12.8 %copy-start.2 = (f32[1,1024]{1,0:T(1,128)S(1)}, f32[1,1024]{1,0:T(1,128)}, u32[]{:S(2)}) copy-start(f32[1,1024]{1,0:T(1,128)} %get-tuple-element.68) | copy-start | bytes 12292
Sparse Core Ops, SparseCore 0:
  9.8 44.2 all-gather.7
  55.7 21.4 all-gather.9
  78.9 24.8 all-gather.15
  105.3 51.2 all-gather.11
  158.0 50.5 all-gather.13
  249.0 31.6 reduce-scatter.7
  283.0 32.0 reduce-scatter.13
  317.5 42.9 reduce-scatter.5
  362.9 53.4 reduce-scatter.11
  418.7 53.2 reduce-scatter.9

commit v2 on v1

v2 whole, which is shorter than its diff:
```python
import functools
import math

import jax
import jax.numpy as jnp
from jax import lax
from jax.experimental import pallas as pl
from jax.experimental.pallas import tpu as pltpu
from jax.sharding import PartitionSpec as P

HEADS = 12
LONGEST = 157
EPSILON = 1e-06
MASKED = -1e30
VMEM_BYTES = 56 * 1024 * 1024
TILE = 128

f32 = jnp.float32
bf16 = jnp.bfloat16


def dot_nn(left, right):
    return lax.dot_general(left, right, (((1,), (0,)), ((), ())), preferred_element_type=f32)


def dot_nt(left, right):
    return lax.dot_general(left, right, (((1,), (1,)), ((), ())), preferred_element_type=f32)


def dot_tn(left, right):
    return lax.dot_general(left, right, (((0,), (0,)), ((), ())), preferred_element_type=f32)


def attention_tiles(rows):
    tiles, offset = [], 0
    reach = LONGEST - 1
    for start in range(0, rows, TILE):
        size = min(TILE, rows - start)
        low = max(0, (start - reach) // 16 * 16)
        high = min(rows, -(-(start + size + reach) // 16) * 16)
        tiles.append((start, size, low, high - low, offset))
        offset += high - low
    return tiles, offset


def row_tile(rows, most):
    for size in range(most, 15, -16):
        if rows % size == 0:
            return size
    return rows


LONG = pl.CostEstimate(flops=10**10, bytes_accessed=1, transcendentals=0)


def whole(shape):
    return pl.BlockSpec(shape, lambda *_: (0,) * len(shape), pipeline_mode=pl.Buffered(1))


def out_whole(shape):
    return pl.BlockSpec(shape, lambda *_: (0,) * len(shape))


SMEM = pl.BlockSpec(memory_space=pltpu.SMEM)
VMEM = pl.BlockSpec(memory_space=pltpu.VMEM)
ANY = pl.BlockSpec(memory_space=pl.ANY)


def shape_of(shape, dtype=bf16):
    return jax.ShapeDtypeStruct(tuple(shape), dtype)


class Order:
    def __init__(self, place):
        self.place, self.last = place, None

    def __call__(self, kernel, name, arrays, in_specs, outs, grid=(), scratch=(), into=(), after=()):
        in_specs, arrays = list(in_specs), list(arrays)
        seen = 1 + len(arrays)
        aliases = {seen + i: i for i in range(len(into))}
        extra = (list(into) or ([] if self.last is None else [self.last])) + list(after)
        in_specs += [ANY] * len(extra)
        arrays += extra

        def body(*refs):
            kernel(*refs[:seen], *refs[seen + len(extra) :])

        result = pl.pallas_call(
            body,
            grid_spec=pltpu.PrefetchScalarGridSpec(
                num_scalar_prefetch=1,
                grid=grid,
                in_specs=in_specs,
                out_specs=tuple(spec for spec, _ in outs),
                scratch_shapes=list(scratch),
            ),
            out_shape=tuple(shape for _, shape in outs),
            cost_estimate=LONG,
            input_output_aliases=aliases,
            compiler_params=pltpu.CompilerParams(vmem_limit_bytes=VMEM_BYTES),
            name=name,
        )(self.place, *arrays)
        self.last = result[0]
        return result


Z, CORE, Y, X, SEQ = range(5)


def position():
    dp, fsdp = lax.axis_index("dp"), lax.axis_index("fsdp")
    seq = dp * lax.axis_size("fsdp") + fsdp
    return jnp.stack([fsdp // 2, fsdp % 2, dp // 2, dp % 2, seq]).astype(jnp.int32)


def swap(value, name, dp=0, fsdp=0):
    m, n = lax.axis_size("dp"), lax.axis_size("fsdp")
    pairs = [(i * n + j, (i ^ dp) * n + (j ^ fsdp)) for i in range(m) for j in range(n)]
    with jax.named_scope(f"{name}_{dp}_{fsdp}"):
        return lax.ppermute(value, ("dp", "fsdp"), pairs)


class Weight:
    def __init__(self, arrays, column, shape):
        self.arrays, self.column, self.shape = list(arrays), column, tuple(shape)
        if len(self.arrays) == 1:
            self.scratch = self.shape
        else:
            levels, rows, _ = arrays[0].shape
            self.scratch = (levels, 2, rows, shape[1])

    def copies(self, place, refs, weight, sems, first):
        columns = pl.ds(self.column, self.shape[1])
        if len(refs) == 1:
            return [pltpu.make_async_copy(refs[0], weight, sems.at[first])]
        return [
            pltpu.make_async_copy(ref.at[:, :, columns], weight.at[:, place[CORE] ^ i], sems.at[first + i])
            for i, ref in enumerate(refs)
        ]


def matrix(ref, columns=slice(None)):
    if len(ref.shape) == 2:
        return ref[:, columns]
    value = ref[:, :, :, columns]
    return value.reshape(-1, value.shape[-1])


def fetch_all(place, weights, arrays, scratch, sems):
    copies = []
    for weight, refs, target in zip(weights, arrays, scratch):
        copies += weight.copies(place, refs, target, sems, len(copies))
    for copy in copies:
        copy.start()
    for copy in copies:
        copy.wait()


def split_refs(refs, weights):
    groups, at = [], 0
    for weight in weights:
        groups.append(refs[at : at + len(weight.arrays)])
        at += len(weight.arrays)
    return groups, refs[at:]


def weight_scratch(weights):
    scratch = [pltpu.VMEM(w.scratch, bf16) for w in weights]
    return scratch + [pltpu.SemaphoreType.DMA((sum(len(w.arrays) for w in weights),))]


def mask_kernel(tiles, place_ref, counts_ref, bias_ref, seg_ref):
    rows = seg_ref.shape[0]
    slots = counts_ref.shape[1]
    seq = place_ref[SEQ]
    ends, total = [], jnp.int32(0)
    for slot in range(slots):
        total = total + counts_ref[seq, slot]
        ends.append(total)
    places = lax.broadcasted_iota(jnp.int32, (rows, TILE), 0)
    seg = jnp.zeros((rows, TILE), jnp.int32)
    for end in ends:
        seg = seg + jnp.where(places >= end, 1, 0)
    seg_ref[...] = seg
    lanes = lax.broadcasted_iota(jnp.int32, (8, TILE), 1)
    for start, size, low, keys, offset in tiles:
        own = start + jnp.where(lanes >= size, lanes - size, lanes)
        seg_own = jnp.zeros((8, TILE), jnp.int32)
        for end in ends:
            seg_own = seg_own + jnp.where(own >= end, 1, 0)
        same = seg_ref[low : low + keys, :] == seg_own[0:1, :]
        bias_ref[offset : offset + keys, :] = jnp.where(same, 0.0, MASKED).astype(f32)


def make_masks(order, counts, rows):
    tiles, total = attention_tiles(rows)
    return order(
        functools.partial(mask_kernel, tiles),
        "masks",
        [counts],
        [SMEM],
        [(out_whole((total, TILE)), shape_of((total, TILE), f32))],
        scratch=[pltpu.VMEM((rows, TILE), jnp.int32)],
    )[0]


def normed(values):
    center = values - jnp.mean(values, axis=-1, keepdims=True)
    spread = jnp.mean(center * center, axis=-1, keepdims=True)
    inverse = lax.rsqrt(spread + EPSILON)
    return center * inverse, inverse


def qkv_kernel(scale, weight, place_ref, tok_ref, gain_ref, shift_ref, qb_ref, vb_ref, *refs):
    arrays, (h_ref, q_ref, k_ref, v_ref, w_ref, sems) = split_refs(refs, [weight])
    width = tok_ref.shape[1]

    @pl.when(pl.program_id(0) == 0)
    def _():
        fetch_all(place_ref, [weight], arrays, [w_ref], sems)

    n1, _ = normed(tok_ref[...].astype(f32))
    hidden = (n1 * gain_ref[...].astype(f32) + shift_ref[...].astype(f32)).astype(bf16)
    h_ref[...] = hidden
    q = dot_nn(hidden, matrix(w_ref, slice(0, width)))
    q_ref[...] = ((q + qb_ref[...].astype(f32)) * scale).astype(bf16)
    k = dot_nn(hidden, matrix(w_ref, slice(width, 2 * width)))
    k_ref[...] = k.astype(bf16)
    v = dot_nn(hidden, matrix(w_ref, slice(2 * width, 3 * width)))
    v_ref[...] = (v + vb_ref[...].astype(f32)).astype(bf16)


def project_qkv(order, tokens, gain, shift, b_q, b_v, weight):
    rows, width = tokens.shape
    scale = (width // HEADS) ** (-0.5)
    size = row_tile(rows, 320)
    rowwise = pl.BlockSpec((size, width), lambda i, p: (i, 0))
    return order(
        functools.partial(qkv_kernel, scale, weight),
        "norm_qkv",
        [tokens, gain, shift, b_q, b_v] + weight.arrays,
        [rowwise] + [whole(gain.shape)] * 4 + [ANY] * len(weight.arrays),
        [(rowwise, shape_of((rows, width)))] * 4,
        grid=(rows // size,),
        scratch=weight_scratch([weight]),
    )


def stack_heads(pair, size):
    lanes = lax.broadcasted_iota(jnp.int32, pair.shape, 1)
    half = pair.shape[1] // 2
    zero = jnp.zeros_like(pair)
    first = jnp.where(lanes < half, pair, zero)
    second = jnp.where(lanes < half, zero, pair)
    return jnp.concatenate([first, second], axis=0)


def both(bias, size):
    return bias if size < TILE else jnp.concatenate([bias, bias], axis=1)


def unstack(columns, size, half):
    return jnp.concatenate([columns[:half, :size], columns[half:, size:]], axis=0).T


def attend_kernel(tiles, place_ref, bias_ref, q_ref, k_ref, v_ref, o_ref, lse_ref):
    half = q_ref.shape[1] // 2
    for index, (start, size, low, keys, offset) in enumerate(tiles):
        stacked = stack_heads(q_ref[start : start + size, :], size)
        scores = dot_nt(k_ref[low : low + keys, :], stacked)
        scores = scores + both(bias_ref[offset : offset + keys, :], size)
        top = jnp.max(scores, axis=0, keepdims=True)
        weights = jnp.exp(scores - top)
        total = jnp.sum(weights, axis=0, keepdims=True)
        probs = (weights * (1.0 / total)).astype(bf16)
        columns = dot_tn(v_ref[low : low + keys, :], probs)
        o_ref[start : start + size, :] = unstack(columns, size, half).astype(bf16)
        lse_ref[0, index : index + 1, : 2 * size] = top + jnp.log(total)


def attend(order, bias, q, k, v):
    rows, width = q.shape
    tiles, total = attention_tiles(rows)
    span = 2 * (width // HEADS)
    pairs = HEADS // 2
    column = pl.BlockSpec((rows, span), lambda i, p: (0, i))
    return order(
        functools.partial(attend_kernel, tiles),
        "attend",
        [bias, q, k, v],
        [whole(bias.shape), column, column, column],
        [
            (column, shape_of((rows, width))),
            (
                pl.BlockSpec((1, len(tiles), 2 * TILE), lambda i, p: (i, 0, 0)),
                shape_of((pairs, len(tiles), 2 * TILE), f32),
            ),
        ],
        grid=(pairs,),
    )


def attend_back_kernel(
    tiles, scale, place_ref, bias_ref, q_ref, k_ref, v_ref, o_ref, do_ref, lse_ref, d_ref, dqv_ref, dk_sum, dv_sum
):
    half = q_ref.shape[1] // 2
    dk_sum[...] = jnp.zeros_like(dk_sum)
    dv_sum[...] = jnp.zeros_like(dv_sum)
    dq_total = jnp.zeros((1, 2 * half), f32)
    for index, (start, size, low, keys, offset) in enumerate(tiles):
        window = slice(low, low + keys)
        rows = slice(start, start + size)
        q2 = stack_heads(q_ref[rows, :], size)
        grads = do_ref[rows, :]
        do2 = stack_heads(grads, size)
        scores = dot_nt(k_ref[window, :], q2) + both(bias_ref[offset : offset + keys, :], size)
        probs = jnp.exp(scores - lse_ref[0, index : index + 1, : 2 * size])
        dprobs = dot_nt(v_ref[window, :], do2)
        meet = (grads.astype(f32) * o_ref[rows, :].astype(f32)).T
        delta = jnp.concatenate(
            [
                jnp.sum(meet[:half, :], axis=0, keepdims=True),
                jnp.sum(meet[half:, :], axis=0, keepdims=True),
            ],
            axis=1,
        )
        dv_sum[window, :] += dot_nn(probs.astype(bf16), do2)
        dscores = (probs * (dprobs - delta)).astype(bf16)
        dk_sum[window, :] += dot_nn(dscores, q2)
        columns = dot_tn(k_ref[window, :], dscores)
        dq = unstack(columns, size, half).astype(bf16) * bf16(scale)
        d_ref[0, rows, :] = dq
        dq_total = dq_total + jnp.sum(dq.astype(f32), axis=0, keepdims=True)
    d_ref[1, :, :] = dk_sum[...].astype(bf16)
    dv = dv_sum[...].astype(bf16)
    d_ref[2, :, :] = dv
    dqv_ref[0:1, :] = dq_total
    dqv_ref[1:2, :] = jnp.sum(dv.astype(f32), axis=0, keepdims=True)


def attend_back(order, bias, q, k, v, o, do, lse):
    rows, width = q.shape
    tiles, total = attention_tiles(rows)
    span = 2 * (width // HEADS)
    pairs = HEADS // 2
    scale = (width // HEADS) ** (-0.5)
    column = pl.BlockSpec((rows, span), lambda i, p: (0, i))
    return order(
        functools.partial(attend_back_kernel, tiles, scale),
        "attend_back",
        [bias, q, k, v, o, do, lse],
        [whole(bias.shape)]
        + [column] * 5
        + [pl.BlockSpec((1, len(tiles), 2 * TILE), lambda i, p: (i, 0, 0))],
        [
            (pl.BlockSpec((3, rows, span), lambda i, p: (0, 0, i)), shape_of((3, rows, width))),
            (pl.BlockSpec((2, span), lambda i, p: (0, i)), shape_of((2, width), f32)),
        ],
        grid=(pairs,),
        scratch=[pltpu.VMEM((rows, span), f32)] * 2,
    )


PARTS = 4


def middle_kernel(weights, place_ref, counts_ref, tok_ref, o_ref, cot_out_ref, cot_align_ref, *refs):
    b_proj_ref, gain_ref, shift_ref, b_up_ref, b_down_ref, b_head_ref = refs[:6]
    arrays, refs = split_refs(refs[6:], weights)
    out_ref, aligned_ref, z_ref, e_ref, h_ref, g_ref, du_ref, dm_ref, dx_ref, da_ref, do_ref = refs[:11]
    s_head_ref, s_down_ref, s_up_ref, s_gain_ref, s_shift_ref, s_proj_ref = refs[11:17]
    w_proj_ref, w_up_ref, w_down_ref, w_head_ref, sems = refs[17:]
    step = pl.program_id(0)
    size, width = tok_ref.shape
    hidden_units = w_up_ref.shape[-1]
    part = hidden_units // PARTS
    seq = place_ref[SEQ]
    total = jnp.int32(0)
    for slot in range(counts_ref.shape[1]):
        total = total + counts_ref[seq, slot]
    places = lax.broadcasted_iota(jnp.int32, (size, 1), 0) + step * size
    valid = jnp.where(places < total, 1.0, 0.0).astype(f32)

    @pl.when(step == 0)
    def _():
        fetch_all(place_ref, weights, arrays, [w_proj_ref, w_up_ref, w_down_ref, w_head_ref], sems)
        for ref in (s_head_ref, s_down_ref, s_up_ref, s_gain_ref, s_shift_ref, s_proj_ref):
            ref[...] = jnp.zeros_like(ref)

    x1 = tok_ref[...].astype(f32) + dot_nn(o_ref[...], matrix(w_proj_ref)) + b_proj_ref[...].astype(f32)
    n2, inverse = normed(x1)
    gain = gain_ref[...].astype(f32)
    h2 = (n2 * gain + shift_ref[...].astype(f32)).astype(bf16)
    h_ref[...] = h2

    e_al = (cot_align_ref[...].astype(f32) * valid).astype(bf16)
    e_ref[...] = e_al
    s_head_ref[...] += jnp.sum(e_al.astype(f32), axis=0, keepdims=True)
    dx2 = cot_out_ref[...].astype(f32) * valid + dot_nt(e_al, matrix(w_head_ref))
    dm = dx2.astype(bf16)
    dm_ref[...] = dm
    s_down_ref[...] += jnp.sum(dm.astype(f32), axis=0, keepdims=True)

    x2 = x1 + b_down_ref[...].astype(f32)
    dh2 = jnp.zeros((size, width), f32)
    for index in range(PARTS):
        span = slice(index * part, (index + 1) * part)
        u = dot_nn(h2, matrix(w_up_ref, span)) + b_up_ref[:, span].astype(f32)
        cdf = 0.5 * (1.0 + lax.erf(u * (1.0 / math.sqrt(2.0))))
        pdf = jnp.exp(-0.5 * u * u) * (1.0 / math.sqrt(2.0 * math.pi))
        g = (u * cdf).astype(bf16)
        g_ref[:, span] = g
        x2 = x2 + dot_nn(g, w_down_ref[span, :])
        du = (dot_nt(dm, w_down_ref[span, :]) * (cdf + u * pdf)).astype(bf16)
        du_ref[:, span] = du
        s_up_ref[:, span] += jnp.sum(du.astype(f32), axis=0, keepdims=True)
        dh2 = dh2 + dot_nt(du, matrix(w_up_ref, span))
    out_ref[...] = (x2 * valid).astype(bf16)
    z = x2.astype(bf16)
    z_ref[...] = z
    aligned_ref[...] = ((dot_nn(z, matrix(w_head_ref)) + b_head_ref[...].astype(f32)) * valid).astype(bf16)

    s_gain_ref[...] += jnp.sum(dh2 * n2, axis=0, keepdims=True)
    s_shift_ref[...] += jnp.sum(dh2, axis=0, keepdims=True)
    t = dh2 * gain
    inner = t - jnp.mean(t, axis=-1, keepdims=True) - n2 * jnp.mean(t * n2, axis=-1, keepdims=True)
    dx1 = dx2 + inverse * inner
    dx_ref[...] = dx1
    da = dx1.astype(bf16)
    da_ref[...] = da
    s_proj_ref[...] += jnp.sum(da.astype(f32), axis=0, keepdims=True)
    do_ref[...] = dot_nt(da, matrix(w_proj_ref)).astype(bf16)


def middle(order, counts, tokens, o, cot_out, cot_align, weights, small):
    rows, width = tokens.shape
    hidden, align = weights[1].shape[1], weights[3].shape[1]
    size = row_tile(rows, 240)

    def by_row(columns):
        return pl.BlockSpec((size, columns), lambda i, p: (i, 0))

    def row_shape(columns, dtype=bf16):
        return shape_of((rows, columns), dtype)

    outs = [
        (by_row(width), row_shape(width)),
        (by_row(align), row_shape(align)),
        (by_row(width), row_shape(width)),
        (by_row(align), row_shape(align)),
        (by_row(width), row_shape(width)),
        (by_row(hidden), row_shape(hidden)),
        (by_row(hidden), row_shape(hidden)),
        (by_row(width), row_shape(width)),
        (by_row(width), row_shape(width, f32)),
        (by_row(width), row_shape(width)),
        (by_row(width), row_shape(width)),
    ]
    for columns in (align, width, hidden, width, width, width):
        outs.append((out_whole((1, columns)), shape_of((1, columns), f32)))
    arrays = [array for weight in weights for array in weight.arrays]
    return order(
        functools.partial(middle_kernel, weights),
        "middle",
        [counts, tokens, o, cot_out, cot_align, *small, *arrays],
        [SMEM, by_row(width), by_row(width), by_row(width), by_row(align)]
        + [whole(s.shape) for s in small]
        + [ANY] * len(arrays),
        outs,
        grid=(rows // size,),
        scratch=weight_scratch(weights),
    )


def outer_kernel(place_ref, l_ref, r_ref, out_ref):
    out_ref[...] = dot_tn(l_ref[...], r_ref[...]).astype(out_ref.dtype)


def outer(order, left, right, rows_out, columns_out, name):
    rows, m = left.shape
    n = right.shape[1]
    tm, tn = min(rows_out, m), min(columns_out, n)
    return order(
        outer_kernel,
        name,
        [left, right],
        [pl.BlockSpec((rows, tm), lambda i, j, p: (0, i)), pl.BlockSpec((rows, tn), lambda i, j, p: (0, j))],
        [(pl.BlockSpec((tm, tn), lambda i, j, p: (i, j)), shape_of((m, n)))],
        grid=(m // tm, n // tn),
    )[0]


BAND = 96
HALF = BAND // 2
FEW = 16


def outer_split_kernel(place_ref, l_ref, r_ref, keep_ref, send_ref, l_scratch):
    levels, _, _, columns = keep_ref.shape

    @pl.when(pl.program_id(0) == 0)
    def _():
        l_scratch[...] = l_ref[...].T

    right = r_ref[0] if len(r_ref.shape) == 3 else r_ref[...]
    total = dot_nn(l_scratch[...], right).astype(bf16)
    shape = (2, HALF, columns)
    first = place_ref[CORE] == 0
    for z in range(levels):
        low = total[2 * z * BAND : (2 * z + 1) * BAND].reshape(shape)
        high = total[(2 * z + 1) * BAND : (2 * z + 2) * BAND].reshape(shape)
        level = place_ref[Z] ^ z
        keep_ref[level] = jnp.where(first, low, high)
        send_ref[level] = jnp.where(first, high, low)


def outer_split(order, left, right, levels, columns_out, total, at, into, name, after=()):
    rows, m = left.shape
    n = right.shape[-1] * (right.shape[0] if right.ndim == 3 else 1)
    if right.ndim == 3:
        columns_out = right.shape[-1]
        r_spec = pl.BlockSpec((1, rows, columns_out), lambda j, p: (j, 0, 0))
    else:
        r_spec = pl.BlockSpec((rows, columns_out), lambda j, p: (0, j))
    out = shape_of((levels, 2, HALF, total))
    out_spec = pl.BlockSpec((levels, 2, HALF, columns_out), lambda j, p: (0, 0, 0, at // columns_out + j))
    return order(
        outer_split_kernel,
        name,
        [left, right],
        [whole(left.shape), r_spec],
        [(out_spec, out)] * 2,
        grid=(n // columns_out,),
        scratch=[pltpu.VMEM((m, rows), bf16)],
        into=into,
        after=after,
    )


def split_kernel(sets, place_ref, *refs):
    pairs, outs = refs[: 2 * len(sets)], refs[2 * len(sets) :]
    for own in range(4):

        @pl.when(place_ref[Y] * 2 + place_ref[X] == own)
        def _():
            for quarter, out_ref in enumerate(outs):
                y, x = divmod(own ^ quarter, 2)
                at = 0
                for number, members in enumerate(sets):
                    keep_ref, got_ref = pairs[2 * number : 2 * number + 2]
                    first = 0
                    for columns in members:
                        half = columns // 2
                        part = slice(first + x * half, first + (x + 1) * half)
                        out_ref[:, :, at : at + half] = keep_ref[:, y, :, part] + got_ref[:, y, :, part]
                        at, first = at + half, first + columns


def split(order, sets, pairs, name, after):
    levels = pairs[0][0].shape[0]
    total = sum(keep.shape[3] for keep, _ in pairs)
    shape = (levels, HALF, total // 2)
    return order(
        functools.partial(split_kernel, sets),
        name,
        [array for pair in pairs for array in pair],
        [VMEM] * (2 * len(pairs)),
        [(VMEM, shape_of(shape))] * 4,
        after=after,
    )


def levels_kernel(*refs):
    ins, outs = refs[1:5], refs[5:]
    for level, out_ref in enumerate(outs):
        total = ins[0][level].astype(f32)
        for ref in ins[1:]:
            total = total + ref[level].astype(f32)
        out_ref[...] = total.astype(bf16)


def by_level(order, quarters, name, after):
    levels, height, columns = quarters[0].shape
    return order(
        levels_kernel,
        name,
        quarters,
        [VMEM] * 4,
        [(VMEM, shape_of((height, columns)))] * levels,
        after=after,
    )


def add_kernel(*refs):
    total = refs[1][...].astype(f32)
    for ref in refs[2:-1]:
        total = total + ref[...].astype(f32)
    refs[-1][...] = total.astype(bf16)


def add_up(order, arrays, name, after):
    return order(
        add_kernel,
        name,
        arrays,
        [VMEM] * len(arrays),
        [(VMEM, shape_of(arrays[0].shape))],
        after=after,
    )[0]


def join_kernel(members, lengths, widen, place_ref, *refs):
    quarters, narrow, outs, lines = refs[:4], refs[4 : 4 + widen], refs[4 + widen : -1], refs[-1]
    matrices = len(members) - (1 if lengths else 0)
    for ref, out_ref in zip(narrow, outs[matrices:]):
        out_ref[...] = ref[...].astype(f32)
    for x in (0, 1):

        @pl.when(place_ref[X] == x)
        def _():
            for quarter, ref in enumerate(quarters):
                y = place_ref[Y] ^ (quarter // 2)
                across = x ^ (quarter % 2)
                at = 0
                for number, columns in enumerate(members):
                    half = columns // 2
                    if number == matrices:
                        lines[2 * y + across] = ref[0:FEW, at : at + half].astype(f32)
                    else:
                        outs[number][y, :, across * half : (across + 1) * half] = ref[:, at : at + half].astype(f32)
                    at += half

    if lengths:
        each, line = keep_lines([n for part in lengths for n in part]), 0
        for part, out_ref in zip(lengths, outs[matrices + widen :]):
            rows = []
            for length in part:
                pieces = []
                for i in range(lines_of(length)):
                    quarter, row = divmod(line + i, each)
                    pieces.append(lines[quarter, row : row + 1, : min(TILE, length - i * TILE)])
                rows.append(jnp.concatenate(pieces, axis=1) if len(pieces) > 1 else pieces[0])
                line += lines_of(length)
            if len(rows) == 1:
                out_ref[...] = rows[0][0]
            else:
                for i, row in enumerate(rows):
                    out_ref[i : i + 1, :] = row


def join(order, quarters, members, lengths, widen, name):
    matrices = members[:-1] if lengths else members
    outs = [(VMEM, shape_of((2, HALF, columns), f32)) for columns in matrices]
    outs += [(VMEM, shape_of(array.shape, f32)) for array in widen]
    for part in lengths:
        outs.append((VMEM, shape_of((part[0],) if len(part) == 1 else (len(part), part[0]), f32)))
    results = order(
        functools.partial(join_kernel, members, lengths, len(widen)),
        name,
        list(quarters) + list(widen),
        [VMEM] * (4 + len(widen)),
        outs,
        scratch=[pltpu.VMEM((4, FEW, TILE), f32)],
    )
    return [r.reshape(BAND, -1) for r in results[: len(matrices)]] + list(results[len(matrices) :])


class Reduction:
    def __init__(self, order, name, lengths=()):
        self.order, self.name, self.lengths = order, name, lengths
        self.sets, self.pairs = [], []

    def add(self, keep, send, members):
        self.sets.append(members)
        self.pairs.append((keep, swap(send, self.name + "_core", fsdp=1)))

    def split(self, after=()):
        quarters = split(self.order, self.sets, self.pairs, self.name + "_split", after)
        self.quarters = [quarters[0]] + [swap(quarters[j], self.name + "_plane", dp=j) for j in (1, 2, 3)]

    def levels(self, after=()):
        parts = by_level(self.order, self.quarters, self.name + "_levels", after)
        self.parts = [parts[0]]
        self.parts += [swap(part, self.name + "_column", fsdp=2 * level) for level, part in enumerate(parts) if level]

    def total(self, after=()):
        near = add_up(self.order, self.parts, self.name + "_total", after)
        self.near = [near] + [swap(near, self.name + "_back", dp=j) for j in (1, 2, 3)]

    def join(self, widen=()):
        members = [columns for members in self.sets for columns in members]
        return join(self.order, self.near, members, self.lengths, widen, self.name + "_join")


def lines_of(length):
    return -(-length // TILE)


def keep_lines(lengths):
    return -(-sum(lines_of(n) for n in lengths) // 4)


def pack_kernel(lengths, place_ref, *refs):
    vectors, (keep_ref, send_ref) = refs[: len(lengths)], refs[len(lengths) :]
    levels = keep_ref.shape[0]
    first = place_ref[CORE] == 0
    each = keep_lines(lengths)
    values = [ref[...] for ref in vectors]

    def lines(shard):
        rows = []
        for value, length in zip(values, lengths):
            row = value[:, shard * length : (shard + 1) * length]
            if length % TILE:
                row = jnp.concatenate([row, jnp.zeros((1, -length % TILE), f32)], axis=1)
            rows += [row[:, at : at + TILE] for at in range(0, row.shape[1], TILE)]
        return rows

    keep_ref[...] = jnp.zeros_like(keep_ref)
    send_ref[...] = jnp.zeros_like(send_ref)
    for z in range(levels):
        level = place_ref[Z] ^ z
        low, high = lines(2 * z), lines(2 * z + 1)
        for quarter in range(4):
            y, x = divmod(quarter, 2)
            part = slice(quarter * each, (quarter + 1) * each)
            blank = [jnp.zeros((FEW - len(low[part]), TILE), f32)]
            a = jnp.concatenate(low[part] + blank, axis=0)
            b = jnp.concatenate(high[part] + blank, axis=0)
            columns = slice(x * TILE, (x + 1) * TILE)
            keep_ref[level, y, 0:FEW, columns] = jnp.where(first, a, b).astype(bf16)
            send_ref[level, y, 0:FEW, columns] = jnp.where(first, b, a).astype(bf16)


def pack_vectors(order, vectors, levels):
    lengths = [v.shape[1] // (2 * levels) for v in vectors]
    shape = (levels, 2, HALF, 2 * TILE)
    return order(
        functools.partial(pack_kernel, lengths),
        "pack_vectors",
        vectors,
        [VMEM] * len(vectors),
        [(VMEM, shape_of(shape))] * 2,
    )


def unpack_kernel(lengths, place_ref, own_ref, other_ref, *out_refs):
    levels = own_ref.shape[0]
    first = place_ref[CORE] == 0
    shards = []
    for z in range(levels):
        own = own_ref[z].astype(f32)
        other = other_ref[z].astype(f32)
        shards += [jnp.where(first, own, other), jnp.where(first, other, own)]
    at = 0
    for length, out_ref in zip(lengths, out_refs):
        pieces = []
        for shard in shards:
            for line in range(lines_of(length)):
                pieces.append(shard[at + line : at + line + 1, : min(TILE, length - line * TILE)])
        out_ref[...] = jnp.concatenate(pieces, axis=1).astype(bf16)
        at += lines_of(length)


def unpack_vectors(order, own, other, lengths):
    levels = own.shape[0]
    return order(
        functools.partial(unpack_kernel, lengths),
        "unpack_vectors",
        [own, other],
        [VMEM] * 2,
        [(VMEM, shape_of((1, 2 * levels * n))) for n in lengths],
    )


def start_kernel(lengths, groups, place_ref, *refs):
    count = sum(len(g) for g in groups)
    vectors = refs[: len(refs) - count - len(groups)]
    shards, outs = refs[len(vectors) : len(vectors) + count], refs[len(vectors) + count :]
    at = 0
    for group, out_ref in zip(groups, outs):
        column = 0
        for _ in group:
            half = shards[at].shape[1]
            out_ref[:, column : column + half] = shards[at][...]
            column += half
            at += 1
    values = []
    for ref in vectors:
        value = ref[...].astype(f32)
        values += [value[i] for i in range(value.shape[0])] if value.ndim == 2 else [value]
    lines = []
    for value, length in zip(values, lengths):
        if length % TILE:
            value = jnp.concatenate([value, jnp.zeros((-length % TILE,), f32)])
        lines += [value[at : at + TILE].reshape(1, TILE) for at in range(0, value.shape[0], TILE)]
    lines.append(jnp.zeros((HALF - len(lines), TILE), f32))
    outs[0][:, outs[0].shape[1] - TILE :] = jnp.concatenate(lines, axis=0).astype(bf16)


def start_gather(order, vectors, lengths, groups):
    shards = [w for group in groups for w in group]
    outs = []
    for number, group in enumerate(groups):
        shape = (HALF, sum(w.shape[1] // 2 for w in group) + (TILE if number == 0 else 0))
        outs.append((out_whole(shape), shape_of(shape)))
    return order(
        functools.partial(start_kernel, lengths, groups),
        "quarters",
        list(vectors) + shards,
        [whole(v.shape) for v in vectors]
        + [pl.BlockSpec((w.shape[0] // 2, w.shape[1] // 2), lambda i, p: (p[Y], p[X])) for w in shards],
        outs,
        grid=(1,),
    )


def near_kernel(levels, place_ref, *refs):
    got, out_ref, lines = refs[:levels], refs[levels], refs[levels + 1 :]
    columns = out_ref.shape[2]
    for level, ref in enumerate(got):
        if level:
            out_ref[level - 1] = ref[:, :columns]
        for lines_ref in lines:
            lines_ref[place_ref[Z] ^ level] = ref[0:FEW, columns:]


def near_levels(order, got, lines, name):
    levels, (height, columns) = len(got), got[0].shape
    columns -= TILE if lines else 0
    outs = [(VMEM, shape_of((levels - 1, height, columns)))]
    if lines:
        outs.append((VMEM, shape_of((levels, FEW, TILE))))
    return order(
        functools.partial(near_kernel, levels),
        name,
        got,
        [VMEM] * levels,
        outs,
    )


def assemble_kernel(halves, place_ref, *refs):
    shards, refs = refs[: len(halves)], refs[len(halves) :]
    quarters, out_ref = refs[:4], refs[4]
    z = place_ref[Z]
    column = 0
    for shard in shards:
        columns = shard.shape[1]
        for y in (0, 1):
            out_ref[z, y, :, column : column + columns] = shard[y * HALF : (y + 1) * HALF, :]
        column += columns
    for x in (0, 1):

        @pl.when(place_ref[X] == x)
        def _():
            for quarter, ref in enumerate(quarters):
                y = place_ref[Y] ^ (quarter // 2)
                across = x ^ (quarter % 2)
                for level in range(ref.shape[0]):
                    source, column = 0, 0
                    for half in halves:
                        target = column + across * half
                        out_ref[z ^ (level + 1), y, :, target : target + half] = ref[level, :, source : source + half]
                        source, column = source + half, column + 2 * half


def assemble(order, shards, quarters, name):
    levels = quarters[0].shape[0] + 1
    halves = [shard.shape[1] // 2 for shard in shards]
    return order(
        functools.partial(assemble_kernel, halves),
        name,
        list(shards) + list(quarters),
        [VMEM] * (len(shards) + 4),
        [(VMEM, shape_of((levels, 2, HALF, 2 * sum(halves))))],
    )[0].reshape(levels, BAND, -1)


def across_plane(near, name):
    return [near] + [swap(near, name + "_plane", dp=j) for j in (1, 2, 3)]


def first_back_kernel(weight, place_ref, tok_ref, dx_ref, d_ref, gain_ref, *refs):
    arrays, (out_ref, s_gain_ref, s_shift_ref, w_ref, sems) = split_refs(refs, [weight])
    width = tok_ref.shape[1]

    @pl.when(pl.program_id(0) == 0)
    def _():
        fetch_all(place_ref, [weight], arrays, [w_ref], sems)
        s_gain_ref[...] = jnp.zeros_like(s_gain_ref)
        s_shift_ref[...] = jnp.zeros_like(s_shift_ref)

    dh = dot_nt(d_ref[0], matrix(w_ref, slice(0, width)))
    dh = dh + dot_nt(d_ref[1], matrix(w_ref, slice(width, 2 * width)))
    dh = dh + dot_nt(d_ref[2], matrix(w_ref, slice(2 * width, 3 * width)))
    n1, inverse = normed(tok_ref[...].astype(f32))
    s_gain_ref[...] += jnp.sum(dh * n1, axis=0, keepdims=True)
    s_shift_ref[...] += jnp.sum(dh, axis=0, keepdims=True)
    t = dh * gain_ref[...].astype(f32)
    inner = t - jnp.mean(t, axis=-1, keepdims=True) - n1 * jnp.mean(t * n1, axis=-1, keepdims=True)
    out_ref[...] = (dx_ref[...] + inverse * inner).astype(bf16)


def first_back(order, tokens, dx1, dqkv, weight, gain, after):
    rows, width = tokens.shape
    size = row_tile(rows, 320)
    rowwise = pl.BlockSpec((size, width), lambda i, p: (i, 0))
    total = (out_whole((1, width)), shape_of((1, width), f32))
    return order(
        functools.partial(first_back_kernel, weight),
        "first_back",
        [tokens, dx1, dqkv, gain] + weight.arrays,
        [rowwise, rowwise, pl.BlockSpec((3, size, width), lambda i, p: (0, i, 0)), whole(gain.shape)]
        + [ANY] * len(weight.arrays),
        [(rowwise, shape_of((rows, width))), total, total],
        grid=(rows // size,),
        after=after,
        scratch=weight_scratch([weight]),
    )


def local(
    tokens,
    ln1_gain,
    ln1_bias,
    w_qkv,
    qv_bias,
    w_proj,
    proj_bias,
    ln2_gain,
    ln2_bias,
    w_up,
    up_bias,
    w_down,
    down_bias,
    w_head,
    head_bias,
    clip_counts,
    cot_out,
    cot_align,
):
    rows, width = tokens.shape
    shards = lax.axis_size("fsdp")
    levels = shards // 2
    order = Order(position())
    vectors = (ln1_gain, ln1_bias, qv_bias, proj_bias, ln2_gain, ln2_bias, up_bias, down_bias, head_bias)
    parts = [[v.shape[-1]] * (v.size // v.shape[-1]) for v in vectors]
    lengths = [length for part in parts for length in part]
    paired = (
        lax.axis_size("dp") == 4
        and shards % 2 == 0
        and levels in (2, 4, 8)
        and w_qkv.shape[0] == BAND
        and sum(lines_of(n) for n in lengths) <= FEW
    )

    def gather(value):
        return lax.all_gather(value, "fsdp", axis=0, tiled=True)

    def scatter(value):
        return lax.psum_scatter(value, "fsdp", scatter_dimension=0, tiled=True)

    if paired:
        wide = [w_up, w_head, w_proj]
        p_qkv, p_wide = start_gather(order, vectors, lengths, [[w_qkv], wide])
        got = [p_qkv] + [swap(p_qkv, "qkv_column", fsdp=2 * level) for level in range(1, levels)]
        got_wide = [swap(p_wide, "wide_column", fsdp=2 * level) for level in range(2, levels)]
        bias = make_masks(order, clip_counts, rows)
        near, lines = near_levels(order, got, True, "qkv_near")
        quarters = across_plane(near, "qkv")
        other_lines = swap(lines, "vectors_core", fsdp=1)
        own = assemble(order, [w_qkv], quarters, "qkv_assemble")
        full_qkv = Weight([own, swap(own, "qkv_core", fsdp=1)], 0, (width, w_qkv.shape[1]))
        later, own = lax.optimization_barrier((p_wide, own))
        got_wide = [p_wide, swap(later, "wide_column", fsdp=2)] + got_wide
        gathered = unpack_vectors(order, lines, other_lines, lengths)
        (near,) = near_levels(order, got_wide, False, "wide_near")
        quarters = across_plane(near, "wide")
        later, near = lax.optimization_barrier((w_down, near))
        full_down = gather(later)
    else:
        pieces = [piece for v in vectors for piece in ([v[0], v[1]] if v.ndim == 2 else [v])]
        joined = gather(jnp.concatenate(pieces)[None])
        gathered, at = [], 0
        for length in lengths:
            gathered.append(joined[:, at : at + length].reshape(1, -1))
            at += length
        full_qkv, full_proj, full_up, full_head = (
            Weight([full], 0, full.shape) for full in (gather(w) for w in (w_qkv, w_proj, w_up, w_head))
        )
        full_down = gather(w_down)
        bias = make_masks(order, clip_counts, rows)
    gain_one, shift_one, b_q, b_v, b_proj, gain_two, shift_two, b_up, b_down, b_head = gathered
    full_down = Weight([full_down], 0, full_down.shape)
    h1, q, k, v = project_qkv(order, tokens, gain_one, shift_one, b_q, b_v, full_qkv)
    o, lse = attend(order, bias, q, k, v)
    if paired:
        own = assemble(order, wide, quarters, "wide_assemble")
        both_cores = [own, swap(own, "wide_core", fsdp=1)]
        at = [0, w_up.shape[1], w_up.shape[1] + w_head.shape[1]]
        full_up, full_head, full_proj = (
            Weight(both_cores, column, (width, w.shape[1])) for column, w in zip(at, wide)
        )
    (block_out, aligned, z, e_al, h2, g, du, dm, dx1, da, do, s_head, s_down, s_up, s_gain, s_shift, s_proj) = middle(
        order,
        clip_counts,
        tokens,
        o,
        cot_out,
        cot_align,
        (full_proj, full_up, full_down, full_head),
        (b_proj, gain_two, shift_two, b_up, b_down, b_head),
    )
    d_down = scatter(outer(order, g, dm, 512, 768, "grad_down"))
    if paired:
        r_wide = Reduction(order, "wide")
        pair = outer_split(order, h2, du, levels, 768, w_up.shape[1], 0, (), "grad_up")
        r_wide.add(*pair, [w_up.shape[1]])
        members = [w_head.shape[1], w_proj.shape[1]]
        pair = outer_split(order, z, e_al, levels, 512, sum(members), 0, (), "grad_head")
        pair = outer_split(order, o, da, levels, 256, sum(members), members[0], pair, "grad_proj")
        r_wide.add(*pair, members)
        r_wide.split()
    dqkv, s_qv = attend_back(order, bias, q, k, v, o, do, lse)
    if paired:
        r_qkv = Reduction(order, "qkv", parts)
        n = w_qkv.shape[1]
        r_qkv.add(*outer_split(order, h1, dqkv, levels, width, n, 0, (), "grad_qkv"), [n])
    grad_tokens, s_gain_one, s_shift_one = first_back(order, tokens, dx1, dqkv, full_qkv, gain_one, [d_down])
    d_down = lax.psum(d_down, "dp")
    sums = (s_gain_one, s_shift_one, s_qv[0:1], s_qv[1:2], s_proj, s_gain, s_shift, s_up, s_down, s_head)
    if paired:
        r_qkv.add(*pack_vectors(order, sums, levels), [2 * TILE])
        r_wide.levels()
        r_qkv.split()
        r_wide.total()
        r_qkv.levels()
        r_qkv.total(after=[d_down])
        d_up, d_head, d_proj = r_wide.join()
        d_qkv, d_down, *mine = r_qkv.join([d_down])
    else:

        def reduce(value):
            return lax.psum(scatter(value), "dp").astype(f32)

        d_down = d_down.astype(f32)
        d_up = reduce(outer(order, h2, du, 768, 512, "grad_up"))
        d_head = reduce(outer(order, z, e_al, 768, 512, "grad_head"))
        d_proj = reduce(outer(order, o, da, 768, 384, "grad_proj"))
        d_qkv = reduce(outer(order, h1, jnp.concatenate([dqkv[0], dqkv[1], dqkv[2]], axis=1), 768, 768, "grad_qkv"))
        joined = jnp.concatenate([s.reshape(shards, -1) for s in sums], axis=1)
        joined = lax.psum(lax.psum_scatter(joined, "fsdp", scatter_dimension=0, tiled=True), "dp")[0]
        mine, at = [], 0
        for part in parts:
            size = sum(part)
            mine.append(joined[at : at + size].reshape((part[0],) if len(part) == 1 else (len(part), -1)))
            at += size
    d_gain_one, d_shift_one, d_qv, d_b_proj, d_gain_two, d_shift_two, d_b_up, d_b_down, d_b_head = mine
    return (
        block_out,
        aligned,
        grad_tokens,
        d_gain_one,
        d_shift_one,
        d_qkv,
        d_qv,
        d_proj,
        d_b_proj,
        d_gain_two,
        d_shift_two,
        d_up,
        d_b_up,
        d_down,
        d_b_down,
        d_head,
        d_b_head,
    )


def solution(mesh):
    rows = P(("dp", "fsdp"), None)
    matrix, vector, pair = P("fsdp", None), P("fsdp"), P(None, "fsdp")
    return jax.shard_map(
        local,
        mesh=mesh,
        in_specs=(
            rows,
            vector,
            vector,
            matrix,
            pair,
            matrix,
            vector,
            vector,
            vector,
            matrix,
            vector,
            matrix,
            vector,
            matrix,
            vector,
            P(),
            rows,
            rows,
        ),
        out_specs=(
            rows,
            rows,
            rows,
            vector,
            vector,
            matrix,
            pair,
            matrix,
            vector,
            vector,
            vector,
            matrix,
            vector,
            matrix,
            vector,
            matrix,
            vector,
        ),
        check_vma=False,
    )
```

time: 617 us -> 337 us (0.55)
  waiting for transfers between devices: 269 us -> 69.6 us
  blocking collectives: 178 us -> 0 us
  Pallas kernels: 135 us -> 196 us
  starting transfers between devices: 0.4 us -> 39.6 us
  other arithmetic: 7.1 us -> 0 us
    all_gather x5 -> x1, waiting for transfers between devices: 141 us -> 0.12 us  [gather(): return lax.all_gather(value, 'fsdp', axis=0, tiled=True)]
    psum x1 -> x0, blocking collectives: 134 us -> none  [local(): lax.psum(lax.psum_scatter(packed, 'fsdp', scatter_dimension=0, tiled=True...]
    reduce_scatter x5 -> x1, waiting for transfers between devices: 125 us -> 0.01 us  [scatter(): return lax.psum_scatter(value, 'fsdp', scatter_dimension=0, tiled=True)]
    pallas_call x11 -> x26, Pallas kernels: 135 us -> 196 us  [__call__(): pl.pallas_call(body, grid_spec=pltpu.PrefetchScalarGridSpec(num_scalar_pr...]
    ppermute x0 -> x37, waiting for transfers between devices: none -> 52.3 us  [swap(): return lax.ppermute(value, ('dp', 'fsdp'), pairs)]
    ppermute x0 -> x37, starting transfers between devices: none -> 39.5 us  [swap(): return lax.ppermute(value, ('dp', 'fsdp'), pairs)]
    unnamed x1 -> x0, blocking collectives: 28.6 us -> none
    psum x0 -> x1, waiting for transfers between devices: none -> 17.1 us  [local(): d_down = lax.psum(d_down, 'dp')]
  transfers between devices with their start and end apart: 10 -> 40, of which waited for: 7 -> 14; matrix products, arithmetic and copies ran while one was open for 2% -> 0% of each run, Pallas kernels for 15% -> 42%
where the time goes in v2:
time: 337 us; the launch traced here: 336 us
  Pallas kernels  196 us (58%)
  waiting for transfers between devices  69.6 us (21%)
  starting transfers between devices  39.6 us (12%)
  local copies, waits for them, and re-layouts  16 us (5%)
  between operations  14.1 us (4%)
    pallas_call x26, Pallas kernels, __call__(): pl.pallas_call(body, grid_spec=pltpu.PrefetchScalarGridSpec(num_scalar_pr...  196 us
    ppermute x37, waiting for transfers between devices, swap(): return lax.ppermute(value, ('dp', 'fsdp'), pairs)  52.3 us
    ppermute x37, starting transfers between devices, swap(): return lax.ppermute(value, ('dp', 'fsdp'), pairs)  39.5 us
    psum x1, waiting for transfers between devices, local(): d_down = lax.psum(d_down, 'dp')  17.1 us
    unnamed x74, local copies, waits for them, and re-layouts  14.8 us
  transfers between devices with their start and end apart: 40, of which 14 were waited for; matrix products, arithmetic and copies ran while one was open for 0% of the time, Pallas kernels for 42%

profile of v2, /device:TPU:0, one launch (start us, length us, event | category | flops | bytes accessed | tf_op | source)
XLA Modules:
  0.0 335.5 jit_solution(14889585020510455359)
XLA Ops:
  10.4 5.0 %collective-permute-start.2 = (bf16[48,1280]{1,0:T(8,128)(2,1)}, bf16[48,1280]{1,0:T(8,128)(2,1)S(1)}, u32[]{:S(2)}, u32[]{:S(2)}) collective-permute-start(bf16[48,1280]{1,0:T(8,128)(2,1)} %get-tuple-element.101.refs_2_.refs_1_), channel_id=1, source_target_pairs={{0,6},{1,7},{2,4},{3,5},{4,2},{5,3},{6,0},{7,1},{8,14},{9,15},{10,... | collective-permute-start | bytes 368648 | tf_op jit(solution)/shard_map/qkv_column_0_6/ppermute | solution.py:120
  16.1 4.6 %masks.1.refs_5_.refs_1_ = f32[3072,128]{1,0:T(8,128)} custom-call(s32[5]{0:T(128)} %stack.23.refs_0_, s32[32,32]{1,0:T(8,128)} %refs_1_.12, bf16[48,1280]{1,0:T(8,128)(2,1)} %get-tuple-element.101.refs_2_.refs_1_), custom_call_target="tpu_custom_call" | custom-call | flops 10000000000 | bytes 1 | tf_op jit(solution)/shard_map/masks/pallas_call | solution.py:88
  20.7 5.3 %collective-permute-done.1.refs_3_ = bf16[48,1280]{1,0:T(8,128)(2,1)S(1)} collective-permute-done((bf16[48,1280]{1,0:T(8,128)(2,1)}, bf16[48,1280]{1,0:T(8,128)(2,1)S(1)}, u32[]{:S(2)}, u32[]{:S(2)}) %collective-permute-start.1) | collective-permute-done | bytes 122912 | tf_op jit(solution)/shard_map/qkv_column_0_4/ppermute | solution.py:120
  35.8 5.9 %collective-permute-done.6.refs_5_ = bf16[3,48,1152]{2,1,0:T(8,128)(2,1)S(1)} collective-permute-done((bf16[3,48,1152]{2,1,0:T(8,128)(2,1)}, bf16[3,48,1152]{2,1,0:T(8,128)(2,1)S(1)}, u32[]{:S(2)}, u32[]{:S(2)}) %collective-permute-start.6) | collective-permute-done | bytes 331808 | tf_op jit(solution)/shard_map/qkv_plane_3_0/ppermute | solution.py:120
  41.7 5.2 %collective-permute-done.5.refs_4_ = bf16[3,48,1152]{2,1,0:T(8,128)(2,1)S(1)} collective-permute-done((bf16[3,48,1152]{2,1,0:T(8,128)(2,1)}, bf16[3,48,1152]{2,1,0:T(8,128)(2,1)S(1)}, u32[]{:S(2)}, u32[]{:S(2)}) %collective-permute-start.5) | collective-permute-done | bytes 331808 | tf_op jit(solution)/shard_map/qkv_plane_2_0/ppermute | solution.py:120
  48.3 3.4 %qkv_assemble.1.refs_3_ = bf16[4,2,48,2304]{3,2,1,0:T(8,128)(2,1)} custom-call(s32[5]{0:T(128)} %stack.23.refs_0_, bf16[96,2304]{1,0:T(8,128)(2,1)} %refs_1_.9, bf16[3,48,1152]{2,1,0:T(8,128)(2,1)} %get-tuple-element.103.refs_2_.refs_6_, bf16[3,48,1152]{2,1,0:T(8,128)(2,1)} %copy-done.14, bf16[3,48,1152]{2,1,0:T(8,128)(2,1)} %copy-done.13, ...), custom_call_target="tpu_custom_call" | custom-call | flops 10000000000 | bytes 1 | tf_op jit(solution)/shard_map/qkv_assemble/pallas_call | solution.py:88
  54.5 5.3 %collective-permute-done.8.refs_2_ = bf16[48,2432]{1,0:T(8,128)(2,1)S(1)} collective-permute-done((bf16[48,2432]{1,0:T(8,128)(2,1)S(1)}, bf16[48,2432]{1,0:T(8,128)(2,1)S(1)}, u32[]{:S(2)}, u32[]{:S(2)}) %collective-permute-start.8) | collective-permute-done | bytes 233504 | tf_op jit(solution)/shard_map/wide_column_0_2/ppermute | solution.py:120
  60.5 2.8 wide_near.1.refs_8_.refs_4_
  68.3 9.8 %norm_qkv.1 = (bf16[960,768]{1,0:T(8,128)(2,1)}, bf16[960,768]{1,0:T(8,128)(2,1)}, bf16[960,768]{1,0:T(8,128)(2,1)}, bf16[960,768]{1,0:T(8,128)(2,1)}) custom-call(s32[5]{0:T(128)} %stack.23.refs_0_, bf16[960,768]{1,0:T(8,128)(2,1)} %refs_1_.13, bf16[1,768]{1,0:T(2,128)(2,1)} %get-tuple-element.104.refs_5_.refs_2_.refs_4_, ...), custom_call_target="tpu_custom_call" | custom-call | flops 10000000000 | bytes 1 | tf_op jit(solution)/shard_map/norm_qkv/pallas_call | solution.py:88
  78.1 23.5 %attend.1 = (bf16[960,768]{1,0:T(8,128)(2,1)}, f32[6,8,256]{2,1,0:T(8,128)}) custom-call(s32[5]{0:T(128)} %stack.23.refs_0_, f32[3072,128]{1,0:T(8,128)} %masks.1.refs_5_.refs_1_, bf16[960,768]{1,0:T(8,128)(2,1)} %get-tuple-element.110.refs_2_, bf16[960,768]{1,0:T(8,128)(2,1)} %get-tuple-element.111.refs_3_, bf16[960,768]{1,0:T(8,128)(2,1)} %get-tuple-element.112.refs_4_, ...), custom_call_target="tpu_custom_call" | custom-call | flops 10000000000 | bytes 1 | tf_op jit(solution)/shard_map/attend/pallas_call | solution.py:88
  102.9 5.1 %wide_assemble.1.refs_19_ = bf16[4,2,48,4864]{3,2,1,0:T(8,128)(2,1)} custom-call(s32[5]{0:T(128)} %stack.23.refs_0_, bf16[96,3072]{1,0:T(8,128)(2,1)} %refs_1_.11, bf16[96,1024]{1,0:T(8,128)(2,1)} %refs_2_.4, bf16[96,768]{1,0:T(8,128)(2,1)} %refs_3_.3, bf16[3,48,2432]{2,1,0:T(8,128)(2,1)} %wide_near.1.refs_8_.refs_4_, bf16[3,48,2432]{2,1,0:T(8,128)(2,1)} %copy-done.8, ...), custom_call_target="tpu_custom_call" | custom-call | flops 10000000000 | bytes 1 | tf_op jit(solution)/shard_map/wide_assemble/pallas_call | solution.py:88
  107.9 6.8 %collective-permute-done.14.refs_13_.refs_15_.refs_18_ = bf16[4,96,4864]{2,1,0:T(8,128)(2,1)} collective-permute-done((bf16[4,96,4864]{2,1,0:T(8,128)(2,1)}, bf16[4,96,4864]{2,1,0:T(8,128)(2,1)}, u32[]{:S(2)}, u32[]{:S(2)}) %collective-permute-start.14) | collective-permute-done | bytes 3735584 | tf_op jit(solution)/shard_map/wide_core_0_1/ppermute | solution.py:120
  114.9 36.8 %middle.1 = (bf16[960,768]{1,0:T(8,128)(2,1)}, bf16[960,1024]{1,0:T(8,128)(2,1)}, bf16[960,768]{1,0:T(8,128)(2,1)}, bf16[960,1024]{1,0:T(8,128)(2,1)}, bf16[960,...) custom-call(s32[5]{0:T(128)} %stack.23.refs_0_, ...), custom_call_target="tpu_custom_call" | custom-call | flops 10000000000 | bytes 1 | tf_op jit(solution)/shard_map/middle/pallas_call | solution.py:88
  151.7 10.6 %grad_down.1.refs_3_ = bf16[3072,768]{1,0:T(8,128)(2,1)} custom-call(s32[5]{0:T(128)} %stack.23.refs_0_, bf16[960,3072]{1,0:T(8,128)(2,1)} %get-tuple-element.129.refs_1_, bf16[960,768]{1,0:T(8,128)(2,1)} %get-tuple-element.130.refs_2_, bf16[960,768]{1,0:T(8,128)(2,1)} %get-tuple-element.84.refs_3_), custom_call_target="tpu_custom_call" | custom-call | flops 10000000000 | bytes 1 | tf_op jit(solution)/shard_map/grad_down/pallas_call | solution.py:88
  162.2 10.3 %grad_up.1 = (bf16[4,2,48,3072]{3,2,1,0:T(8,128)(2,1)}, bf16[4,2,48,3072]{3,2,1,0:T(8,128)(2,1)}) custom-call(s32[5]{0:T(128)} %stack.23.refs_0_, bf16[960,768]{1,0:T(8,128)(2,1)} %get-tuple-element.127.refs_1_, bf16[960,3072]{1,0:T(8,128)(2,1)} %get-tuple-element.128.refs_2_, bf16[3072,768]{1,0:T(8,128)(2,1)} %grad_down.1.refs_3_), custom_call_target="tpu_custom_call" | custom-call | flops 10000000000 | bytes 1 | tf_op jit(solution)/shard_map/grad_up/pallas_call | solution.py:88
  172.8 5.8 %grad_head.1 = (bf16[4,2,48,1792]{3,2,1,0:T(8,128)(2,1)}, bf16[4,2,48,1792]{3,2,1,0:T(8,128)(2,1)}) custom-call(s32[5]{0:T(128)} %stack.23.refs_0_, bf16[960,768]{1,0:T(8,128)(2,1)} %get-tuple-element.134.refs_1_, bf16[960,1024]{1,0:T(8,128)(2,1)} %get-tuple-element.135.refs_2_, bf16[4,2,48,3072]{3,2,1,0:T(8,128)(2,1)} %get-tuple-element.131.refs_3_.refs_1_), custom_call_target="tpu_custom_call" | custom-call | flops 10000000000 | bytes 1 | tf_op jit(solution)/shard_map/grad_head/pallas_call | solution.py:88
  178.6 5.9 %grad_proj.1 = (bf16[4,2,48,1792]{3,2,1,0:T(8,128)(2,1)}, bf16[4,2,48,1792]{3,2,1,0:T(8,128)(2,1)}) custom-call(s32[5]{0:T(128)} %stack.23.refs_0_, bf16[960,768]{1,0:T(8,128)(2,1)} %get-tuple-element.114.refs_8_.refs_3_.refs_1_.refs_5_, bf16[960,768]{1,0:T(8,128)(2,1)} %get-tuple-element.133.refs_2_, ...), custom_call_target="tpu_custom_call", output_to_operand_aliasing={{0}: (3, {}), {1}: (4, {})} | custom-call | flops 10000000000 | bytes 1 | tf_op jit(solution)/shard_map/grad_proj/pallas_call | solution.py:88
  184.8 3.1 collective-permute-done.16.refs_4_
  189.7 6.5 %wide_split.1 = (bf16[4,48,2432]{2,1,0:T(8,128)(2,1)}, bf16[4,48,2432]{2,1,0:T(8,128)(2,1)}, bf16[4,48,2432]{2,1,0:T(8,128)(2,1)}, bf16[4,48,2432]{2,1,0:T(8,128)(2,1)}) custom-call(s32[5]{0:T(128)} %stack.23.refs_0_, bf16[4,2,48,3072]{3,2,1,0:T(8,128)(2,1)} %get-tuple-element.131.refs_3_.refs_1_, bf16[4,2,48,3072]{3,2,1,0:T(8,128)(2,1)} %copy-done.1, ...), custom_call_target="tpu_custom_call" | custom-call | flops 10000000000 | bytes 1 | tf_op jit(solution)/shard_map/wide_split/pallas_call | solution.py:88
  199.7 19.2 %attend_back.1 = (bf16[3,960,768]{2,1,0:T(8,128)(2,1)}, f32[2,768]{1,0:T(2,128)}) custom-call(s32[5]{0:T(128)} %stack.23.refs_0_, f32[3072,128]{1,0:T(8,128)} %masks.1.refs_5_.refs_1_, bf16[960,768]{1,0:T(8,128)(2,1)} %get-tuple-element.110.refs_2_, bf16[960,768]{1,0:T(8,128)(2,1)} %get-tuple-element.111.refs_3_, ...), custom_call_target="tpu_custom_call" | custom-call | flops 10000000000 | bytes 1 | tf_op jit(solution)/shard_map/attend_back/pallas_call | solution.py:88
  218.9 8.8 %grad_qkv.1 = (bf16[4,2,48,2304]{3,2,1,0:T(8,128)(2,1)}, bf16[4,2,48,2304]{3,2,1,0:T(8,128)(2,1)}) custom-call(s32[5]{0:T(128)} %stack.23.refs_0_, bf16[960,768]{1,0:T(8,128)(2,1)} %get-tuple-element.113.refs_5_.refs_1_, bf16[3,960,768]{2,1,0:T(8,128)(2,1)} %get-tuple-element.141.refs_2_.refs_3_, bf16[3,960,768]{2,1,0:T(8,128)(2,1)} %get-tuple-element.141.refs_2_.refs_3_), custom_call_target="tpu_custom_call" | custom-call | flops 10000000000 | bytes 1 | tf_op jit(solution)/shard_map/grad_qkv/pallas_call | solution.py:88
  228.3 10.8 %first_back.1 = (bf16[960,768]{1,0:T(8,128)(2,1)}, f32[1,768]{1,0:T(1,128)}, f32[1,768]{1,0:T(1,128)}) custom-call(s32[5]{0:T(128)} %stack.23.refs_0_, bf16[960,768]{1,0:T(8,128)(2,1)} %refs_1_.13, f32[960,768]{1,0:T(8,128)} %get-tuple-element.124.refs_2_, bf16[3,960,768]{2,1,0:T(8,128)(2,1)} %get-tuple-element.141.refs_2_.refs_3_, ...), custom_call_target="tpu_custom_call" | custom-call | flops 10000000000 | bytes 1 | tf_op jit(solution)/shard_map/first_back/pallas_call | solution.py:88
  242.9 3.8 %wide_levels.1 = (bf16[48,2432]{1,0:T(8,128)(2,1)}, bf16[48,2432]{1,0:T(8,128)(2,1)}, bf16[48,2432]{1,0:T(8,128)(2,1)}, bf16[48,2432]{1,0:T(8,128)(2,1)}) custom-call(s32[5]{0:T(128)} %stack.23.refs_0_, bf16[4,48,2432]{2,1,0:T(8,128)(2,1)} %get-tuple-element.140.refs_8_.refs_1_, bf16[4,48,2432]{2,1,0:T(8,128)(2,1)} %copy-done.5, ...), custom_call_target="tpu_custom_call" | custom-call | flops 10000000000 | bytes 1 | tf_op jit(solution)/shard_map/wide_levels/pallas_call | solution.py:88
  252.4 4.3 %qkv_split.1 = (bf16[4,48,1280]{2,1,0:T(8,128)(2,1)}, bf16[4,48,1280]{2,1,0:T(8,128)(2,1)}, bf16[4,48,1280]{2,1,0:T(8,128)(2,1)}, bf16[4,48,1280]{2,1,0:T(8,128)(2,1)}) custom-call(s32[5]{0:T(128)} %stack.23.refs_0_, bf16[4,2,48,2304]{3,2,1,0:T(8,128)(2,1)} %get-tuple-element.142.refs_7_.refs_1_, bf16[4,2,48,2304]{3,2,1,0:T(8,128)(2,1)} %copy-done.3, ...), custom_call_target="tpu_custom_call" | custom-call | flops 10000000000 | bytes 1 | tf_op jit(solution)/shard_map/qkv_split/pallas_call | solution.py:88
  260.8 5.8 %collective-permute-done.26.refs_3_ = bf16[48,2432]{1,0:T(8,128)(2,1)S(1)} collective-permute-done((bf16[48,2432]{1,0:T(8,128)(2,1)}, bf16[48,2432]{1,0:T(8,128)(2,1)S(1)}, u32[]{:S(2)}, u32[]{:S(2)}) %collective-permute-start.26) | collective-permute-done | bytes 233504 | tf_op jit(solution)/shard_map/wide_column_0_4/ppermute | solution.py:120
  267.5 2.8 wide_total.1.refs_5_.refs_1_
  272.0 12.3 %collective-permute-done.24.refs_4_ = bf16[4,48,1280]{2,1,0:T(8,128)(2,1)S(1)} collective-permute-done((bf16[4,48,1280]{2,1,0:T(8,128)(2,1)}, bf16[4,48,1280]{2,1,0:T(8,128)(2,1)S(1)}, u32[]{:S(2)}, u32[]{:S(2)}) %collective-permute-start.24) | collective-permute-done | bytes 491552 | tf_op jit(solution)/shard_map/qkv_plane_3_0/ppermute | solution.py:120
  285.1 3.0 qkv_levels.1
  288.6 3.1 collective-permute-start.29
  296.0 17.1 %all-reduce.2.cloned.1.call-done.refs_6_.refs_5_ = bf16[384,768]{1,0:T(8,128)(2,1)} async-done(((bf16[384,768]{1,0:T(8,128)(2,1)}), bf16[384,768]{1,0:T(8,128)(2,1)}) %all-reduce.2.cloned.1.call-update) | async-done | bytes 589840 | tf_op jit(solution)/shard_map/psum | solution.py:1031
  321.1 3.3 wide_join.1
  325.6 3.4 %qkv_join.1 = (f32[2,48,2304]{2,1,0:T(8,128)}, f32[384,768]{1,0:T(8,128)}, f32[96]{0:T(128)}, f32[96]{0:T(128)}, f32[2,96]{1,0:T(2,128)}, /*index=5*/f32[96]{0:T...) custom-call(s32[5]{0:T(128)} %stack.23.refs_0_, ...), custom_call_target="tpu_custom_call" | custom-call | flops 10000000000 | bytes 1 | tf_op jit(solution)/shard_map/qkv_join/pallas_call | solution.py:88
  (153 shorter events, 62.0 us)
Async XLA Ops:
  7.2 107.7 %all-gather.2.cloned.1.call-start = ((), (), s32[]{:S(2)}) async-start(), calls=%async_computation.1 | async-start | bytes 5308416 | tf_op jit(solution)/shard_map/all_gather | solution.py:959
  10.4 10.3 %collective-permute-start.2 = (bf16[48,1280]{1,0:T(8,128)(2,1)}, bf16[48,1280]{1,0:T(8,128)(2,1)S(1)}, u32[]{:S(2)}, u32[]{:S(2)}) collective-permute-start(bf16[48,1280]{1,0:T(8,128)(2,1)} %get-tuple-element.101.refs_2_.refs_1_), channel_id=1, source_target_pairs={{0,6},{1,7},{2,4},{3,5},{4,2},{5,3},{6,0},{7,1},{8,14},{9,15},{10,... | collective-permute-start | bytes 368648 | tf_op jit(solution)/shard_map/qkv_column_0_6/ppermute | solution.py:120
  15.4 10.6 %collective-permute-start.1 = (bf16[48,1280]{1,0:T(8,128)(2,1)}, bf16[48,1280]{1,0:T(8,128)(2,1)S(1)}, u32[]{:S(2)}, u32[]{:S(2)}) collective-permute-start(bf16[48,1280]{1,0:T(8,128)(2,1)} %get-tuple-element.101.refs_2_.refs_1_), channel_id=1, source_target_pairs={{0,4},{1,5},{2,6},{3,7},{4,0},{5,1},{6,2},{7,3},{8,12},{9,13},{10,... | collective-permute-start | bytes 368648 | tf_op jit(solution)/shard_map/qkv_column_0_4/ppermute | solution.py:120
  15.4 10.6 %collective-permute-start = (bf16[48,1280]{1,0:T(8,128)(2,1)}, bf16[48,1280]{1,0:T(8,128)(2,1)S(1)}, u32[]{:S(2)}, u32[]{:S(2)}) collective-permute-start(bf16[48,1280]{1,0:T(8,128)(2,1)} %get-tuple-element.101.refs_2_.refs_1_), channel_id=1, source_target_pairs={{0,2},{1,3},{2,0},{3,1},{4,6},{5,7},{6,4},{7,5},{8,10},{9,11},{10,... | collective-permute-start | bytes 368648 | tf_op jit(solution)/shard_map/qkv_column_0_2/ppermute | solution.py:120
  29.8 11.9 %collective-permute-start.6 = (bf16[3,48,1152]{2,1,0:T(8,128)(2,1)}, bf16[3,48,1152]{2,1,0:T(8,128)(2,1)S(1)}, u32[]{:S(2)}, u32[]{:S(2)}) collective-permute-start(bf16[3,48,1152]{2,1,0:T(8,128)(2,1)} %get-tuple-element.103.refs_2_.refs_6_), channel_id=1, source_target_pairs={{0,24},{1,25},{2,26},{3,27},{4,28},{5,29},{6,30},{7,31},{8,16},{9,... | collective-permute-start | bytes 995336 | tf_op jit(solution)/shard_map/qkv_plane_3_0/ppermute | solution.py:120
  32.3 14.6 %collective-permute-start.5 = (bf16[3,48,1152]{2,1,0:T(8,128)(2,1)}, bf16[3,48,1152]{2,1,0:T(8,128)(2,1)S(1)}, u32[]{:S(2)}, u32[]{:S(2)}) collective-permute-start(bf16[3,48,1152]{2,1,0:T(8,128)(2,1)} %get-tuple-element.103.refs_2_.refs_6_), channel_id=1, source_target_pairs={{0,16},{1,17},{2,18},{3,19},{4,20},{5,21},{6,22},{7,23},{8,24},{9,... | collective-permute-start | bytes 995336 | tf_op jit(solution)/shard_map/qkv_plane_2_0/ppermute | solution.py:120
  32.8 14.2 %collective-permute-start.4 = (bf16[3,48,1152]{2,1,0:T(8,128)(2,1)}, bf16[3,48,1152]{2,1,0:T(8,128)(2,1)S(1)}, u32[]{:S(2)}, u32[]{:S(2)}) collective-permute-start(bf16[3,48,1152]{2,1,0:T(8,128)(2,1)} %get-tuple-element.103.refs_2_.refs_6_), channel_id=1, source_target_pairs={{0,8},{1,9},{2,10},{3,11},{4,12},{5,13},{6,14},{7,15},{8,0},{9,1},... | collective-permute-start | bytes 995336 | tf_op jit(solution)/shard_map/qkv_plane_1_0/ppermute | solution.py:120
  33.3 21.2 %collective-permute-start.10 = (bf16[48,2432]{1,0:T(8,128)(2,1)S(1)}, bf16[48,2432]{1,0:T(8,128)(2,1)S(1)}, u32[]{:S(2)}, u32[]{:S(2)}) collective-permute-start(bf16[48,2432]{1,0:T(8,128)(2,1)S(1)} %copy-done.15), channel_id=1, source_target_pairs={{0,6},{1,7},{2,4},{3,5},{4,2},{5,3},{6,0},{7,1},{8,14},{9,15},{10,... | collective-permute-start | bytes 700424 | tf_op jit(solution)/shard_map/wide_column_0_6/ppermute | solution.py:120
  35.8 18.7 %collective-permute-start.9 = (bf16[48,2432]{1,0:T(8,128)(2,1)S(1)}, bf16[48,2432]{1,0:T(8,128)(2,1)S(1)}, u32[]{:S(2)}, u32[]{:S(2)}) collective-permute-start(bf16[48,2432]{1,0:T(8,128)(2,1)S(1)} %copy-done.15), channel_id=1, source_target_pairs={{0,4},{1,5},{2,6},{3,7},{4,0},{5,1},{6,2},{7,3},{8,12},{9,13},{10,... | collective-permute-start | bytes 700424 | tf_op jit(solution)/shard_map/wide_column_0_4/ppermute | solution.py:120
  41.7 10.1 %collective-permute-start.3 = (bf16[4,16,128]{2,1,0:T(8,128)(2,1)}, bf16[4,16,128]{2,1,0:T(8,128)(2,1)S(1)}, u32[]{:S(2)}, u32[]{:S(2)}) collective-permute-start(bf16[4,16,128]{2,1,0:T(8,128)(2,1)} %get-tuple-element.102.refs_1_), channel_id=1, source_target_pairs={{0,1},{1,0},{2,3},{3,2},{4,5},{5,4},{6,7},{7,6},{8,9},{9,8},{10,11... | collective-permute-start | bytes 49160 | tf_op jit(solution)/shard_map/vectors_core_0_1/ppermute | solution.py:120
  51.8 15.3 %collective-permute-start.7 = (bf16[4,96,2304]{2,1,0:T(8,128)(2,1)}, bf16[4,96,2304]{2,1,0:T(8,128)(2,1)S(1)}, u32[]{:S(2)}, u32[]{:S(2)}) collective-permute-start(bf16[4,96,2304]{2,1,0:T(8,128)(2,1)} %bitcast.15), channel_id=1, source_target_pairs={{0,1},{1,0},{2,3},{3,2},{4,5},{5,4},{6,7},{7,6},{8,9},{9,8},{10,11... | collective-permute-start | bytes 5308424 | tf_op jit(solution)/shard_map/qkv_core_0_1/ppermute | solution.py:120
  63.4 164.9 %reduce-scatter.2.cloned.1.call-start = ((), (), s32[]{:S(2)}) async-start(), calls=%async_computation.2 | async-start | bytes 5308416 | tf_op jit(solution)/shard_map/reduce_scatter | solution.py:962
  63.5 38.1 %collective-permute-start.13 = (bf16[3,48,2432]{2,1,0:T(8,128)(2,1)}, bf16[3,48,2432]{2,1,0:T(8,128)(2,1)S(1)}, u32[]{:S(2)}, u32[]{:S(2)}) collective-permute-start(bf16[3,48,2432]{2,1,0:T(8,128)(2,1)} %wide_near.1.refs_8_.refs_4_), channel_id=1, source_target_pairs={{0,24},{1,25},{2,26},{3,27},{4,28},{5,29},{6,30},{7,31},{8,16},{9,... | collective-permute-start | bytes 2101256 | tf_op jit(solution)/shard_map/wide_plane_3_0/ppermute | solution.py:120
  65.3 36.3 %collective-permute-start.12 = (bf16[3,48,2432]{2,1,0:T(8,128)(2,1)}, bf16[3,48,2432]{2,1,0:T(8,128)(2,1)S(1)}, u32[]{:S(2)}, u32[]{:S(2)}) collective-permute-start(bf16[3,48,2432]{2,1,0:T(8,128)(2,1)} %wide_near.1.refs_8_.refs_4_), channel_id=1, source_target_pairs={{0,16},{1,17},{2,18},{3,19},{4,20},{5,21},{6,22},{7,23},{8,24},{9,... | collective-permute-start | bytes 2101256 | tf_op jit(solution)/shard_map/wide_plane_2_0/ppermute | solution.py:120
  66.5 35.1 %collective-permute-start.11 = (bf16[3,48,2432]{2,1,0:T(8,128)(2,1)}, bf16[3,48,2432]{2,1,0:T(8,128)(2,1)S(1)}, u32[]{:S(2)}, u32[]{:S(2)}) collective-permute-start(bf16[3,48,2432]{2,1,0:T(8,128)(2,1)} %wide_near.1.refs_8_.refs_4_), channel_id=1, source_target_pairs={{0,8},{1,9},{2,10},{3,11},{4,12},{5,13},{6,14},{7,15},{8,0},{9,1},... | collective-permute-start | bytes 2101256 | tf_op jit(solution)/shard_map/wide_plane_1_0/ppermute | solution.py:120
  172.6 15.3 %collective-permute-start.15 = (bf16[4,2,48,3072]{3,2,1,0:T(8,128)(2,1)}, bf16[4,2,48,3072]{3,2,1,0:T(8,128)(2,1)S(1)}, u32[]{:S(2)}, u32[]{:S(2)}) collective-permute-start(bf16[4,2,48,3072]{3,2,1,0:T(8,128)(2,1)} %get-tuple-element.132), channel_id=1, source_target_pairs={{0,1},{1,0},{2,3},{3,2},{4,5},{5,4},{6,7},{7,6},{8,9},{9,8},{10,11... | collective-permute-start | bytes 7077896 | tf_op jit(solution)/shard_map/wide_core_0_1/ppermute | solution.py:120
  196.2 45.8 %collective-permute-start.19 = (bf16[4,48,2432]{2,1,0:T(8,128)(2,1)}, bf16[4,48,2432]{2,1,0:T(8,128)(2,1)S(1)}, u32[]{:S(2)}, u32[]{:S(2)}) collective-permute-start(bf16[4,48,2432]{2,1,0:T(8,128)(2,1)} %get-tuple-element.156), channel_id=1, source_target_pairs={{0,8},{1,9},{2,10},{3,11},{4,12},{5,13},{6,14},{7,15},{8,0},{9,1},... | collective-permute-start | bytes 2801672 | tf_op jit(solution)/shard_map/wide_plane_1_0/ppermute | solution.py:120
  197.6 44.4 %collective-permute-start.20 = (bf16[4,48,2432]{2,1,0:T(8,128)(2,1)}, bf16[4,48,2432]{2,1,0:T(8,128)(2,1)}, u32[]{:S(2)}, u32[]{:S(2)}) collective-permute-start(bf16[4,48,2432]{2,1,0:T(8,128)(2,1)} %get-tuple-element.157), channel_id=1, source_target_pairs={{0,16},{1,17},{2,18},{3,19},{4,20},{5,21},{6,22},{7,23},{8,24},{9,... | collective-permute-start | bytes 2801672 | tf_op jit(solution)/shard_map/wide_plane_2_0/ppermute | solution.py:120
  198.6 43.4 %collective-permute-start.21 = (bf16[4,48,2432]{2,1,0:T(8,128)(2,1)}, bf16[4,48,2432]{2,1,0:T(8,128)(2,1)}, u32[]{:S(2)}, u32[]{:S(2)}) collective-permute-start(bf16[4,48,2432]{2,1,0:T(8,128)(2,1)} %get-tuple-element.158), channel_id=1, source_target_pairs={{0,24},{1,25},{2,26},{3,27},{4,28},{5,29},{6,30},{7,31},{8,16},{9,... | collective-permute-start | bytes 2801672 | tf_op jit(solution)/shard_map/wide_plane_3_0/ppermute | solution.py:120
  227.7 23.5 %collective-permute-start.17 = (bf16[4,2,48,2304]{3,2,1,0:T(8,128)(2,1)}, bf16[4,2,48,2304]{3,2,1,0:T(8,128)(2,1)S(1)}, u32[]{:S(2)}, u32[]{:S(2)}) collective-permute-start(bf16[4,2,48,2304]{3,2,1,0:T(8,128)(2,1)} %get-tuple-element.144), channel_id=1, source_target_pairs={{0,1},{1,0},{2,3},{3,2},{4,5},{5,4},{6,7},{7,6},{8,9},{9,8},{10,11... | collective-permute-start | bytes 5308424 | tf_op jit(solution)/shard_map/qkv_core_0_1/ppermute | solution.py:120
  239.1 74.0 %all-reduce.2.cloned.1.call-start = ((), (), s32[]{:S(2)}) async-start(), calls=%async_computation.3 | async-start | bytes 1179648 | tf_op jit(solution)/shard_map/psum | solution.py:1031
  246.7 12.4 %collective-permute-start.25 = (bf16[48,2432]{1,0:T(8,128)(2,1)}, bf16[48,2432]{1,0:T(8,128)(2,1)S(1)}, u32[]{:S(2)}, u32[]{:S(2)}) collective-permute-start(bf16[48,2432]{1,0:T(8,128)(2,1)} %get-tuple-element.164), channel_id=1, source_target_pairs={{0,2},{1,3},{2,0},{3,1},{4,6},{5,7},{6,4},{7,5},{8,10},{9,11},{10,... | collective-permute-start | bytes 700424 | tf_op jit(solution)/shard_map/wide_column_0_2/ppermute | solution.py:120
  247.0 19.7 %collective-permute-start.26 = (bf16[48,2432]{1,0:T(8,128)(2,1)}, bf16[48,2432]{1,0:T(8,128)(2,1)S(1)}, u32[]{:S(2)}, u32[]{:S(2)}) collective-permute-start(bf16[48,2432]{1,0:T(8,128)(2,1)} %get-tuple-element.165), channel_id=1, source_target_pairs={{0,4},{1,5},{2,6},{3,7},{4,0},{5,1},{6,2},{7,3},{8,12},{9,13},{10,... | collective-permute-start | bytes 700424 | tf_op jit(solution)/shard_map/wide_column_0_4/ppermute | solution.py:120
  249.4 17.3 %collective-permute-start.27 = (bf16[48,2432]{1,0:T(8,128)(2,1)}, bf16[48,2432]{1,0:T(8,128)(2,1)S(1)}, u32[]{:S(2)}, u32[]{:S(2)}) collective-permute-start(bf16[48,2432]{1,0:T(8,128)(2,1)} %get-tuple-element.166), channel_id=1, source_target_pairs={{0,6},{1,7},{2,4},{3,5},{4,2},{5,3},{6,0},{7,1},{8,14},{9,15},{10,... | collective-permute-start | bytes 700424 | tf_op jit(solution)/shard_map/wide_column_0_6/ppermute | solution.py:120
  256.7 15.2 %collective-permute-start.22 = (bf16[4,48,1280]{2,1,0:T(8,128)(2,1)}, bf16[4,48,1280]{2,1,0:T(8,128)(2,1)S(1)}, u32[]{:S(2)}, u32[]{:S(2)}) collective-permute-start(bf16[4,48,1280]{2,1,0:T(8,128)(2,1)} %get-tuple-element.161), channel_id=1, source_target_pairs={{0,8},{1,9},{2,10},{3,11},{4,12},{5,13},{6,14},{7,15},{8,0},{9,1},... | collective-permute-start | bytes 1474568 | tf_op jit(solution)/shard_map/qkv_plane_1_0/ppermute | solution.py:120
  258.1 13.9 %collective-permute-start.23 = (bf16[4,48,1280]{2,1,0:T(8,128)(2,1)}, bf16[4,48,1280]{2,1,0:T(8,128)(2,1)S(1)}, u32[]{:S(2)}, u32[]{:S(2)}) collective-permute-start(bf16[4,48,1280]{2,1,0:T(8,128)(2,1)} %get-tuple-element.162), channel_id=1, source_target_pairs={{0,16},{1,17},{2,18},{3,19},{4,20},{5,21},{6,22},{7,23},{8,24},{9,... | collective-permute-start | bytes 1474568 | tf_op jit(solution)/shard_map/qkv_plane_2_0/ppermute | solution.py:120
  259.1 25.2 %collective-permute-start.24 = (bf16[4,48,1280]{2,1,0:T(8,128)(2,1)}, bf16[4,48,1280]{2,1,0:T(8,128)(2,1)S(1)}, u32[]{:S(2)}, u32[]{:S(2)}) collective-permute-start(bf16[4,48,1280]{2,1,0:T(8,128)(2,1)} %get-tuple-element.163), channel_id=1, source_target_pairs={{0,24},{1,25},{2,26},{3,27},{4,28},{5,29},{6,30},{7,31},{8,16},{9,... | collective-permute-start | bytes 1474568 | tf_op jit(solution)/shard_map/qkv_plane_3_0/ppermute | solution.py:120
  288.6 24.5 %collective-permute-start.29 = (bf16[48,1280]{1,0:T(8,128)(2,1)}, bf16[48,1280]{1,0:T(8,128)(2,1)S(1)}, u32[]{:S(2)}, u32[]{:S(2)}) collective-permute-start(bf16[48,1280]{1,0:T(8,128)(2,1)} %get-tuple-element.169), channel_id=1, source_target_pairs={{0,4},{1,5},{2,6},{3,7},{4,0},{5,1},{6,2},{7,3},{8,12},{9,13},{10,... | collective-permute-start | bytes 368648 | tf_op jit(solution)/shard_map/qkv_column_0_4/ppermute | solution.py:120
  291.6 21.5 %collective-permute-start.30 = (bf16[48,1280]{1,0:T(8,128)(2,1)}, bf16[48,1280]{1,0:T(8,128)(2,1)S(1)}, u32[]{:S(2)}, u32[]{:S(2)}) collective-permute-start(bf16[48,1280]{1,0:T(8,128)(2,1)} %get-tuple-element.170), channel_id=1, source_target_pairs={{0,6},{1,7},{2,4},{3,5},{4,2},{5,3},{6,0},{7,1},{8,14},{9,15},{10,... | collective-permute-start | bytes 368648 | tf_op jit(solution)/shard_map/qkv_column_0_6/ppermute | solution.py:120
  292.5 26.7 %collective-permute-start.36 = (bf16[48,2432]{1,0:T(8,128)(2,1)S(1)}, bf16[48,2432]{1,0:T(8,128)(2,1)S(1)}, u32[]{:S(2)}, u32[]{:S(2)}) collective-permute-start(bf16[48,2432]{1,0:T(8,128)(2,1)S(1)} %copy-done.16), channel_id=1, source_target_pairs={{0,24},{1,25},{2,26},{3,27},{4,28},{5,29},{6,30},{7,31},{8,16},{9,... | collective-permute-start | bytes 700424 | tf_op jit(solution)/shard_map/wide_back_3_0/ppermute | solution.py:120
  292.9 26.8 %collective-permute-start.35 = (bf16[48,2432]{1,0:T(8,128)(2,1)S(1)}, bf16[48,2432]{1,0:T(8,128)(2,1)S(1)}, u32[]{:S(2)}, u32[]{:S(2)}) collective-permute-start(bf16[48,2432]{1,0:T(8,128)(2,1)S(1)} %copy-done.16), channel_id=1, source_target_pairs={{0,16},{1,17},{2,18},{3,19},{4,20},{5,21},{6,22},{7,23},{8,24},{9,... | collective-permute-start | bytes 700424 | tf_op jit(solution)/shard_map/wide_back_2_0/ppermute | solution.py:120
  294.7 25.0 %collective-permute-start.34 = (bf16[48,2432]{1,0:T(8,128)(2,1)S(1)}, bf16[48,2432]{1,0:T(8,128)(2,1)S(1)}, u32[]{:S(2)}, u32[]{:S(2)}) collective-permute-start(bf16[48,2432]{1,0:T(8,128)(2,1)S(1)} %copy-done.16), channel_id=1, source_target_pairs={{0,8},{1,9},{2,10},{3,11},{4,12},{5,13},{6,14},{7,15},{8,0},{9,1},... | collective-permute-start | bytes 700424 | tf_op jit(solution)/shard_map/wide_back_1_0/ppermute | solution.py:120
  (45 other events, 193.9 us)
Sparse Core Ops, SparseCore 0:
  63.5 51.3 all-gather.1
  162.4 53.8 reduce-scatter.1
  251.3 61.7 all-reduce.1

commit v3 on v2

--- a/solution.py
+++ b/solution.py
@@ -12,7 +12,6 @@
 LONGEST = 157
 EPSILON = 1e-06
 MASKED = -1e30
-VMEM_BYTES = 56 * 1024 * 1024
 TILE = 128
 
 f32 = jnp.float32
@@ -50,7 +49,15 @@
     return rows
 
 
-LONG = pl.CostEstimate(flops=10**10, bytes_accessed=1, transcendentals=0)
+USUAL = 10
+TIMES = {
+    "attend_back": 20,
+    "first_back": 20,
+}
+
+
+def duration(name):
+    return pl.CostEstimate(flops=TIMES.get(name, USUAL) * 10**9, bytes_accessed=1, transcendentals=0)
 
 
 def whole(shape):
@@ -74,7 +81,7 @@
     def __init__(self, place):
         self.place, self.last = place, None
 
-    def __call__(self, kernel, name, arrays, in_specs, outs, grid=(), scratch=(), into=(), after=()):
+    def __call__(self, kernel, name, arrays, in_specs, outs, grid=(), scratch=(), into=(), after=(), vmem=32):
         in_specs, arrays = list(in_specs), list(arrays)
         seen = 1 + len(arrays)
         aliases = {seen + i: i for i in range(len(into))}
@@ -95,9 +102,9 @@
                 scratch_shapes=list(scratch),
             ),
             out_shape=tuple(shape for _, shape in outs),
-            cost_estimate=LONG,
+            cost_estimate=duration(name),
             input_output_aliases=aliases,
-            compiler_params=pltpu.CompilerParams(vmem_limit_bytes=VMEM_BYTES),
+            compiler_params=pltpu.CompilerParams(vmem_limit_bytes=vmem << 20),
             name=name,
         )(self.place, *arrays)
         self.last = result[0]
@@ -167,6 +174,14 @@
 def weight_scratch(weights):
     scratch = [pltpu.VMEM(w.scratch, bf16) for w in weights]
     return scratch + [pltpu.SemaphoreType.DMA((sum(len(w.arrays) for w in weights),))]
+
+
+GAIN_ONE, SHIFT_ONE, B_Q, B_V, B_PROJ, GAIN_TWO, SHIFT_TWO, B_UP, B_DOWN, B_HEAD = range(10)
+ROWS = 16
+
+
+def row(vectors_ref, index, length):
+    return vectors_ref[index : index + 1, :length].astype(f32)
 
 
 def mask_kernel(tiles, place_ref, counts_ref, bias_ref, seg_ref):
@@ -211,7 +226,7 @@
     return center * inverse, inverse
 
 
-def qkv_kernel(scale, weight, place_ref, tok_ref, gain_ref, shift_ref, qb_ref, vb_ref, *refs):
+def qkv_kernel(scale, weight, place_ref, tok_ref, vec_ref, *refs):
     arrays, (h_ref, q_ref, k_ref, v_ref, w_ref, sems) = split_refs(refs, [weight])
     width = tok_ref.shape[1]
 
@@ -220,17 +235,17 @@
         fetch_all(place_ref, [weight], arrays, [w_ref], sems)
 
     n1, _ = normed(tok_ref[...].astype(f32))
-    hidden = (n1 * gain_ref[...].astype(f32) + shift_ref[...].astype(f32)).astype(bf16)
+    hidden = (n1 * row(vec_ref, GAIN_ONE, width) + row(vec_ref, SHIFT_ONE, width)).astype(bf16)
     h_ref[...] = hidden
     q = dot_nn(hidden, matrix(w_ref, slice(0, width)))
-    q_ref[...] = ((q + qb_ref[...].astype(f32)) * scale).astype(bf16)
+    q_ref[...] = ((q + row(vec_ref, B_Q, width)) * scale).astype(bf16)
     k = dot_nn(hidden, matrix(w_ref, slice(width, 2 * width)))
     k_ref[...] = k.astype(bf16)
     v = dot_nn(hidden, matrix(w_ref, slice(2 * width, 3 * width)))
-    v_ref[...] = (v + vb_ref[...].astype(f32)).astype(bf16)
-
-
-def project_qkv(order, tokens, gain, shift, b_q, b_v, weight):
+    v_ref[...] = (v + row(vec_ref, B_V, width)).astype(bf16)
+
+
+def project_qkv(order, tokens, vectors, weight):
     rows, width = tokens.shape
     scale = (width // HEADS) ** (-0.5)
     size = row_tile(rows, 320)
@@ -238,8 +253,8 @@
     return order(
         functools.partial(qkv_kernel, scale, weight),
         "norm_qkv",
-        [tokens, gain, shift, b_q, b_v] + weight.arrays,
-        [rowwise] + [whole(gain.shape)] * 4 + [ANY] * len(weight.arrays),
+        [tokens, vectors] + weight.arrays,
+        [rowwise, whole(vectors.shape)] + [ANY] * len(weight.arrays),
         [(rowwise, shape_of((rows, width)))] * 4,
         grid=(rows // size,),
         scratch=weight_scratch([weight]),
@@ -265,15 +280,19 @@
 
 def attend_kernel(tiles, place_ref, bias_ref, q_ref, k_ref, v_ref, o_ref, lse_ref):
     half = q_ref.shape[1] // 2
-    for index, (start, size, low, keys, offset) in enumerate(tiles):
+    scores = []
+    for start, size, low, keys, offset in tiles:
         stacked = stack_heads(q_ref[start : start + size, :], size)
-        scores = dot_nt(k_ref[low : low + keys, :], stacked)
-        scores = scores + both(bias_ref[offset : offset + keys, :], size)
-        top = jnp.max(scores, axis=0, keepdims=True)
-        weights = jnp.exp(scores - top)
-        total = jnp.sum(weights, axis=0, keepdims=True)
-        probs = (weights * (1.0 / total)).astype(bf16)
-        columns = dot_tn(v_ref[low : low + keys, :], probs)
+        value = dot_nt(k_ref[low : low + keys, :], stacked)
+        scores.append(value + both(bias_ref[offset : offset + keys, :], size))
+    parts = []
+    for value in scores:
+        top = jnp.max(value, axis=0, keepdims=True)
+        weights = jnp.exp(value - top)
+        parts.append((weights.astype(bf16), top, jnp.sum(weights, axis=0, keepdims=True)))
+    for index, (start, size, low, keys, _) in enumerate(tiles):
+        weights, top, total = parts[index]
+        columns = dot_tn(v_ref[low : low + keys, :], weights) * (1.0 / total)
         o_ref[start : start + size, :] = unstack(columns, size, half).astype(bf16)
         lse_ref[0, index : index + 1, : 2 * size] = top + jnp.log(total)
 
@@ -307,30 +326,37 @@
     dk_sum[...] = jnp.zeros_like(dk_sum)
     dv_sum[...] = jnp.zeros_like(dv_sum)
     dq_total = jnp.zeros((1, 2 * half), f32)
-    for index, (start, size, low, keys, offset) in enumerate(tiles):
-        window = slice(low, low + keys)
-        rows = slice(start, start + size)
-        q2 = stack_heads(q_ref[rows, :], size)
-        grads = do_ref[rows, :]
-        do2 = stack_heads(grads, size)
-        scores = dot_nt(k_ref[window, :], q2) + both(bias_ref[offset : offset + keys, :], size)
-        probs = jnp.exp(scores - lse_ref[0, index : index + 1, : 2 * size])
-        dprobs = dot_nt(v_ref[window, :], do2)
-        meet = (grads.astype(f32) * o_ref[rows, :].astype(f32)).T
-        delta = jnp.concatenate(
-            [
-                jnp.sum(meet[:half, :], axis=0, keepdims=True),
-                jnp.sum(meet[half:, :], axis=0, keepdims=True),
-            ],
-            axis=1,
-        )
-        dv_sum[window, :] += dot_nn(probs.astype(bf16), do2)
-        dscores = (probs * (dprobs - delta)).astype(bf16)
-        dk_sum[window, :] += dot_nn(dscores, q2)
-        columns = dot_tn(k_ref[window, :], dscores)
-        dq = unstack(columns, size, half).astype(bf16) * bf16(scale)
-        d_ref[0, rows, :] = dq
-        dq_total = dq_total + jnp.sum(dq.astype(f32), axis=0, keepdims=True)
+    for pair in range(0, len(tiles), 2):
+        group = list(enumerate(tiles))[pair : pair + 2]
+        held = []
+        for index, (start, size, low, keys, offset) in group:
+            window, rows = slice(low, low + keys), slice(start, start + size)
+            q2 = stack_heads(q_ref[rows, :], size)
+            grads = do_ref[rows, :]
+            do2 = stack_heads(grads, size)
+            scores = dot_nt(k_ref[window, :], q2) + both(bias_ref[offset : offset + keys, :], size)
+            dprobs = dot_nt(v_ref[window, :], do2)
+            meet = (grads.astype(f32) * o_ref[rows, :].astype(f32)).T
+            delta = jnp.concatenate(
+                [
+                    jnp.sum(meet[:half, :], axis=0, keepdims=True),
+                    jnp.sum(meet[half:, :], axis=0, keepdims=True),
+                ],
+                axis=1,
+            )
+            held.append((q2, do2, scores, dprobs, delta))
+        lows = []
+        for (index, (start, size, *_)), (q2, do2, scores, dprobs, delta) in zip(group, held):
+            probs = jnp.exp(scores - lse_ref[0, index : index + 1, : 2 * size])
+            lows.append((probs.astype(bf16), (probs * (dprobs - delta)).astype(bf16)))
+        for (index, (start, size, low, keys, _)), (q2, do2, *_), (probs, dscores) in zip(group, held, lows):
+            window, rows = slice(low, low + keys), slice(start, start + size)
+            dv_sum[window, :] += dot_nn(probs, do2)
+            dk_sum[window, :] += dot_nn(dscores, q2)
+            columns = dot_tn(k_ref[window, :], dscores)
+            dq = unstack(columns, size, half).astype(bf16) * bf16(scale)
+            d_ref[0, rows, :] = dq
+            dq_total = dq_total + jnp.sum(dq.astype(f32), axis=0, keepdims=True)
     d_ref[1, :, :] = dk_sum[...].astype(bf16)
     dv = dv_sum[...].astype(bf16)
     d_ref[2, :, :] = dv
@@ -364,12 +390,10 @@
 PARTS = 4
 
 
-def middle_kernel(weights, place_ref, counts_ref, tok_ref, o_ref, cot_out_ref, cot_align_ref, *refs):
-    b_proj_ref, gain_ref, shift_ref, b_up_ref, b_down_ref, b_head_ref = refs[:6]
-    arrays, refs = split_refs(refs[6:], weights)
+def middle_kernel(weights, place_ref, counts_ref, tok_ref, o_ref, cot_out_ref, cot_align_ref, vec_ref, *refs):
+    arrays, refs = split_refs(refs, weights)
     out_ref, aligned_ref, z_ref, e_ref, h_ref, g_ref, du_ref, dm_ref, dx_ref, da_ref, do_ref = refs[:11]
-    s_head_ref, s_down_ref, s_up_ref, s_gain_ref, s_shift_ref, s_proj_ref = refs[11:17]
-    w_proj_ref, w_up_ref, w_down_ref, w_head_ref, sems = refs[17:]
+    sums_ref, w_proj_ref, w_up_ref, w_down_ref, w_head_ref, sems = refs[11:]
     step = pl.program_id(0)
     size, width = tok_ref.shape
     hidden_units = w_up_ref.shape[-1]
@@ -384,28 +408,31 @@
     @pl.when(step == 0)
     def _():
         fetch_all(place_ref, weights, arrays, [w_proj_ref, w_up_ref, w_down_ref, w_head_ref], sems)
-        for ref in (s_head_ref, s_down_ref, s_up_ref, s_gain_ref, s_shift_ref, s_proj_ref):
-            ref[...] = jnp.zeros_like(ref)
-
-    x1 = tok_ref[...].astype(f32) + dot_nn(o_ref[...], matrix(w_proj_ref)) + b_proj_ref[...].astype(f32)
+        sums_ref[...] = jnp.zeros_like(sums_ref)
+
+    def add_sum(index, first, value):
+        columns = slice(first, first + value.shape[1])
+        sums_ref[index : index + 1, columns] += jnp.sum(value.astype(f32), axis=0, keepdims=True)
+
+    x1 = tok_ref[...].astype(f32) + dot_nn(o_ref[...], matrix(w_proj_ref)) + row(vec_ref, B_PROJ, width)
     n2, inverse = normed(x1)
-    gain = gain_ref[...].astype(f32)
-    h2 = (n2 * gain + shift_ref[...].astype(f32)).astype(bf16)
+    gain = row(vec_ref, GAIN_TWO, width)
+    h2 = (n2 * gain + row(vec_ref, SHIFT_TWO, width)).astype(bf16)
     h_ref[...] = h2
 
     e_al = (cot_align_ref[...].astype(f32) * valid).astype(bf16)
     e_ref[...] = e_al
-    s_head_ref[...] += jnp.sum(e_al.astype(f32), axis=0, keepdims=True)
+    add_sum(B_HEAD, 0, e_al)
     dx2 = cot_out_ref[...].astype(f32) * valid + dot_nt(e_al, matrix(w_head_ref))
     dm = dx2.astype(bf16)
     dm_ref[...] = dm
-    s_down_ref[...] += jnp.sum(dm.astype(f32), axis=0, keepdims=True)
-
-    x2 = x1 + b_down_ref[...].astype(f32)
+    add_sum(B_DOWN, 0, dm)
+
+    x2 = x1 + row(vec_ref, B_DOWN, width)
     dh2 = jnp.zeros((size, width), f32)
     for index in range(PARTS):
         span = slice(index * part, (index + 1) * part)
-        u = dot_nn(h2, matrix(w_up_ref, span)) + b_up_ref[:, span].astype(f32)
+        u = dot_nn(h2, matrix(w_up_ref, span)) + vec_ref[B_UP : B_UP + 1, span].astype(f32)
         cdf = 0.5 * (1.0 + lax.erf(u * (1.0 / math.sqrt(2.0))))
         pdf = jnp.exp(-0.5 * u * u) * (1.0 / math.sqrt(2.0 * math.pi))
         g = (u * cdf).astype(bf16)
@@ -413,29 +440,29 @@
         x2 = x2 + dot_nn(g, w_down_ref[span, :])
         du = (dot_nt(dm, w_down_ref[span, :]) * (cdf + u * pdf)).astype(bf16)
         du_ref[:, span] = du
-        s_up_ref[:, span] += jnp.sum(du.astype(f32), axis=0, keepdims=True)
+        add_sum(B_UP, index * part, du)
         dh2 = dh2 + dot_nt(du, matrix(w_up_ref, span))
     out_ref[...] = (x2 * valid).astype(bf16)
     z = x2.astype(bf16)
     z_ref[...] = z
-    aligned_ref[...] = ((dot_nn(z, matrix(w_head_ref)) + b_head_ref[...].astype(f32)) * valid).astype(bf16)
-
-    s_gain_ref[...] += jnp.sum(dh2 * n2, axis=0, keepdims=True)
-    s_shift_ref[...] += jnp.sum(dh2, axis=0, keepdims=True)
+    aligned_ref[...] = ((dot_nn(z, matrix(w_head_ref)) + row(vec_ref, B_HEAD, cot_align_ref.shape[1])) * valid).astype(bf16)
+
+    add_sum(GAIN_TWO, 0, dh2 * n2)
+    add_sum(SHIFT_TWO, 0, dh2)
     t = dh2 * gain
     inner = t - jnp.mean(t, axis=-1, keepdims=True) - n2 * jnp.mean(t * n2, axis=-1, keepdims=True)
     dx1 = dx2 + inverse * inner
     dx_ref[...] = dx1
     da = dx1.astype(bf16)
     da_ref[...] = da
-    s_proj_ref[...] += jnp.sum(da.astype(f32), axis=0, keepdims=True)
+    add_sum(B_PROJ, 0, da)
     do_ref[...] = dot_nt(da, matrix(w_proj_ref)).astype(bf16)
 
 
-def middle(order, counts, tokens, o, cot_out, cot_align, weights, small):
+def middle(order, counts, tokens, o, cot_out, cot_align, weights, vectors):
     rows, width = tokens.shape
     hidden, align = weights[1].shape[1], weights[3].shape[1]
-    size = row_tile(rows, 240)
+    size = row_tile(rows, 320)
 
     def by_row(columns):
         return pl.BlockSpec((size, columns), lambda i, p: (i, 0))
@@ -456,18 +483,17 @@
         (by_row(width), row_shape(width)),
         (by_row(width), row_shape(width)),
     ]
-    for columns in (align, width, hidden, width, width, width):
-        outs.append((out_whole((1, columns)), shape_of((1, columns), f32)))
+    outs.append((out_whole(vectors.shape), shape_of(vectors.shape, f32)))
     arrays = [array for weight in weights for array in weight.arrays]
     return order(
         functools.partial(middle_kernel, weights),
         "middle",
-        [counts, tokens, o, cot_out, cot_align, *small, *arrays],
-        [SMEM, by_row(width), by_row(width), by_row(width), by_row(align)]
-        + [whole(s.shape) for s in small]
+        [counts, tokens, o, cot_out, cot_align, vectors, *arrays],
+        [SMEM, by_row(width), by_row(width), by_row(width), by_row(align), whole(vectors.shape)]
         + [ANY] * len(arrays),
         outs,
         grid=(rows // size,),
+        vmem=54,
         scratch=weight_scratch(weights),
     )
 
@@ -487,6 +513,7 @@
         [pl.BlockSpec((rows, tm), lambda i, j, p: (0, i)), pl.BlockSpec((rows, tn), lambda i, j, p: (0, j))],
         [(pl.BlockSpec((tm, tn), lambda i, j, p: (i, j)), shape_of((m, n)))],
         grid=(m // tm, n // tn),
+        vmem=56,
     )[0]
 
 
@@ -533,6 +560,7 @@
         grid=(n // columns_out,),
         scratch=[pltpu.VMEM((m, rows), bf16)],
         into=into,
+        vmem=56,
         after=after,
     )
 
@@ -556,7 +584,7 @@
                         at, first = at + half, first + columns
 
 
-def split(order, sets, pairs, name, after):
+def split(order, sets, pairs, name):
     levels = pairs[0][0].shape[0]
     total = sum(keep.shape[3] for keep, _ in pairs)
     shape = (levels, HALF, total // 2)
@@ -566,54 +594,62 @@
         [array for pair in pairs for array in pair],
         [VMEM] * (2 * len(pairs)),
         [(VMEM, shape_of(shape))] * 4,
-        after=after,
-    )
-
-
-def levels_kernel(*refs):
-    ins, outs = refs[1:5], refs[5:]
+    )
+
+
+def levels_kernel(levels, place_ref, *refs):
+    ins, lines, outs = refs[:4], refs[4:-levels], refs[-levels:]
+    columns = ins[0].shape[2]
     for level, out_ref in enumerate(outs):
         total = ins[0][level].astype(f32)
         for ref in ins[1:]:
             total = total + ref[level].astype(f32)
-        out_ref[...] = total.astype(bf16)
-
-
-def by_level(order, quarters, name, after):
+        out_ref[:, :columns] = total.astype(bf16)
+        if lines:
+            out_ref[0:FEW, columns:] = lines[0][level] + lines[1][level]
+            out_ref[FEW:, columns:] = jnp.zeros((HALF - FEW, TILE), bf16)
+
+
+def by_level(order, quarters, lines, name):
     levels, height, columns = quarters[0].shape
-    return order(
-        levels_kernel,
+    columns += TILE if lines else 0
+    return order(
+        functools.partial(levels_kernel, levels),
         name,
-        quarters,
-        [VMEM] * 4,
+        list(quarters) + list(lines),
+        [VMEM] * (4 + len(lines)),
         [(VMEM, shape_of((height, columns)))] * levels,
-        after=after,
-    )
-
-
-def add_kernel(*refs):
-    total = refs[1][...].astype(f32)
-    for ref in refs[2:-1]:
+    )
+
+
+def add_kernel(parts, place_ref, *refs):
+    ins, beside, out_ref = refs[:parts], refs[parts:-1], refs[-1]
+    columns = ins[0].shape[1]
+    total = ins[0][...].astype(f32)
+    for ref in ins[1:]:
         total = total + ref[...].astype(f32)
-    refs[-1][...] = total.astype(bf16)
-
-
-def add_up(order, arrays, name, after):
-    return order(
-        add_kernel,
+    out_ref[:, :columns] = total.astype(bf16)
+    for ref in beside:
+        width = ref.shape[1]
+        for band in range(ref.shape[0] // HALF):
+            out_ref[:, columns : columns + width] = ref[band * HALF : (band + 1) * HALF, :]
+            columns += width
+
+
+def add_up(order, arrays, beside, name):
+    height, columns = arrays[0].shape
+    columns += sum(b.size // height for b in beside)
+    return order(
+        functools.partial(add_kernel, len(arrays)),
         name,
-        arrays,
-        [VMEM] * len(arrays),
-        [(VMEM, shape_of(arrays[0].shape))],
-        after=after,
+        list(arrays) + list(beside),
+        [VMEM] * (len(arrays) + len(beside)),
+        [(VMEM, shape_of((height, columns)))],
     )[0]
 
 
-def join_kernel(members, lengths, widen, place_ref, *refs):
-    quarters, narrow, outs, lines = refs[:4], refs[4 : 4 + widen], refs[4 + widen : -1], refs[-1]
-    matrices = len(members) - (1 if lengths else 0)
-    for ref, out_ref in zip(narrow, outs[matrices:]):
-        out_ref[...] = ref[...].astype(f32)
+def join_kernel(members, lengths, beside, place_ref, *refs):
+    quarters, outs = refs[:4], refs[4:]
     for x in (0, 1):
 
         @pl.when(place_ref[X] == x)
@@ -624,127 +660,125 @@
                 at = 0
                 for number, columns in enumerate(members):
                     half = columns // 2
-                    if number == matrices:
-                        lines[2 * y + across] = ref[0:FEW, at : at + half].astype(f32)
-                    else:
-                        outs[number][y, :, across * half : (across + 1) * half] = ref[:, at : at + half].astype(f32)
+                    outs[number][y, :, across * half : (across + 1) * half] = ref[:, at : at + half].astype(f32)
                     at += half
 
+    at = sum(members) // 2
+    if beside:
+        out_ref = outs[len(members)]
+        width = out_ref.shape[3]
+        for quarter, ref in enumerate(quarters):
+            owner = (place_ref[Y] * 2 + place_ref[X]) ^ quarter
+            for band in range(out_ref.shape[1]):
+                columns = slice(at + band * width, at + (band + 1) * width)
+                out_ref[owner, band] = ref[:, columns].astype(f32)
+
     if lengths:
-        each, line = keep_lines([n for part in lengths for n in part]), 0
-        for part, out_ref in zip(lengths, outs[matrices + widen :]):
+        lines = quarters[0][0:FEW, at : at + TILE].astype(f32)
+        for ref in quarters[1:]:
+            lines = lines + ref[0:FEW, at : at + TILE].astype(f32)
+        line = 0
+        for part, out_ref in zip(lengths, outs[len(members) :]):
             rows = []
             for length in part:
                 pieces = []
                 for i in range(lines_of(length)):
-                    quarter, row = divmod(line + i, each)
-                    pieces.append(lines[quarter, row : row + 1, : min(TILE, length - i * TILE)])
+                    pieces.append(lines[line + i : line + i + 1, : min(TILE, length - i * TILE)])
                 rows.append(jnp.concatenate(pieces, axis=1) if len(pieces) > 1 else pieces[0])
                 line += lines_of(length)
             if len(rows) == 1:
                 out_ref[...] = rows[0][0]
             else:
-                for i, row in enumerate(rows):
-                    out_ref[i : i + 1, :] = row
-
-
-def join(order, quarters, members, lengths, widen, name):
-    matrices = members[:-1] if lengths else members
-    outs = [(VMEM, shape_of((2, HALF, columns), f32)) for columns in matrices]
-    outs += [(VMEM, shape_of(array.shape, f32)) for array in widen]
+                for i, value in enumerate(rows):
+                    out_ref[i : i + 1, :] = value
+
+
+def join(order, quarters, members, lengths, beside, name):
+    outs = [(VMEM, shape_of((2, HALF, columns), f32)) for columns in members]
+    if beside:
+        rows, columns = beside
+        outs.append((VMEM, shape_of((4, rows // (4 * HALF), HALF, columns), f32)))
     for part in lengths:
         outs.append((VMEM, shape_of((part[0],) if len(part) == 1 else (len(part), part[0]), f32)))
     results = order(
-        functools.partial(join_kernel, members, lengths, len(widen)),
+        functools.partial(join_kernel, members, lengths, beside),
         name,
-        list(quarters) + list(widen),
-        [VMEM] * (4 + len(widen)),
+        quarters,
+        [VMEM] * 4,
         outs,
-        scratch=[pltpu.VMEM((4, FEW, TILE), f32)],
-    )
-    return [r.reshape(BAND, -1) for r in results[: len(matrices)]] + list(results[len(matrices) :])
+    )
+    matrices = len(members) + (1 if beside else 0)
+    return [r.reshape(-1, r.shape[-1]) for r in results[:matrices]] + list(results[matrices:])
 
 
 class Reduction:
-    def __init__(self, order, name, lengths=()):
-        self.order, self.name, self.lengths = order, name, lengths
+    def __init__(self, order, name):
+        self.order, self.name = order, name
         self.sets, self.pairs = [], []
 
     def add(self, keep, send, members):
         self.sets.append(members)
         self.pairs.append((keep, swap(send, self.name + "_core", fsdp=1)))
 
-    def split(self, after=()):
-        quarters = split(self.order, self.sets, self.pairs, self.name + "_split", after)
+    def split(self):
+        quarters = split(self.order, self.sets, self.pairs, self.name + "_split")
         self.quarters = [quarters[0]] + [swap(quarters[j], self.name + "_plane", dp=j) for j in (1, 2, 3)]
 
-    def levels(self, after=()):
-        parts = by_level(self.order, self.quarters, self.name + "_levels", after)
+    def levels(self, lines=()):
+        parts = by_level(self.order, self.quarters, lines, self.name + "_levels")
         self.parts = [parts[0]]
         self.parts += [swap(part, self.name + "_column", fsdp=2 * level) for level, part in enumerate(parts) if level]
 
-    def total(self, after=()):
-        near = add_up(self.order, self.parts, self.name + "_total", after)
+    def total(self, beside=()):
+        near = add_up(self.order, self.parts, beside, self.name + "_total")
         self.near = [near] + [swap(near, self.name + "_back", dp=j) for j in (1, 2, 3)]
 
-    def join(self, widen=()):
+    def join(self, lengths=(), beside=()):
         members = [columns for members in self.sets for columns in members]
-        return join(self.order, self.near, members, self.lengths, widen, self.name + "_join")
+        return join(self.order, self.near, members, lengths, beside, self.name + "_join")
 
 
 def lines_of(length):
     return -(-length // TILE)
 
 
-def keep_lines(lengths):
-    return -(-sum(lines_of(n) for n in lengths) // 4)
-
-
-def pack_kernel(lengths, place_ref, *refs):
-    vectors, (keep_ref, send_ref) = refs[: len(lengths)], refs[len(lengths) :]
+def pack_kernel(lengths, place_ref, sums_ref, first_ref, qv_ref, keep_ref, send_ref):
     levels = keep_ref.shape[0]
     first = place_ref[CORE] == 0
-    each = keep_lines(lengths)
-    values = [ref[...] for ref in vectors]
+    late = {GAIN_ONE: (first_ref, 0), SHIFT_ONE: (first_ref, 1), B_Q: (qv_ref, 0), B_V: (qv_ref, 1)}
+    values = []
+    for index, length in enumerate(lengths):
+        ref, line = late.get(index, (sums_ref, index))
+        values.append(ref[line : line + 1, : 2 * levels * length])
 
     def lines(shard):
         rows = []
         for value, length in zip(values, lengths):
-            row = value[:, shard * length : (shard + 1) * length]
+            part = value[:, shard * length : (shard + 1) * length]
             if length % TILE:
-                row = jnp.concatenate([row, jnp.zeros((1, -length % TILE), f32)], axis=1)
-            rows += [row[:, at : at + TILE] for at in range(0, row.shape[1], TILE)]
-        return rows
-
-    keep_ref[...] = jnp.zeros_like(keep_ref)
-    send_ref[...] = jnp.zeros_like(send_ref)
+                part = jnp.concatenate([part, jnp.zeros((1, -length % TILE), f32)], axis=1)
+            rows += [part[:, at : at + TILE] for at in range(0, part.shape[1], TILE)]
+        return jnp.concatenate(rows + [jnp.zeros((FEW - len(rows), TILE), f32)], axis=0)
+
     for z in range(levels):
         level = place_ref[Z] ^ z
         low, high = lines(2 * z), lines(2 * z + 1)
-        for quarter in range(4):
-            y, x = divmod(quarter, 2)
-            part = slice(quarter * each, (quarter + 1) * each)
-            blank = [jnp.zeros((FEW - len(low[part]), TILE), f32)]
-            a = jnp.concatenate(low[part] + blank, axis=0)
-            b = jnp.concatenate(high[part] + blank, axis=0)
-            columns = slice(x * TILE, (x + 1) * TILE)
-            keep_ref[level, y, 0:FEW, columns] = jnp.where(first, a, b).astype(bf16)
-            send_ref[level, y, 0:FEW, columns] = jnp.where(first, b, a).astype(bf16)
-
-
-def pack_vectors(order, vectors, levels):
-    lengths = [v.shape[1] // (2 * levels) for v in vectors]
-    shape = (levels, 2, HALF, 2 * TILE)
+        keep_ref[level] = jnp.where(first, low, high).astype(bf16)
+        send_ref[level] = jnp.where(first, high, low).astype(bf16)
+
+
+def pack_vectors(order, sums, lengths, levels):
+    shape = (levels, FEW, TILE)
     return order(
         functools.partial(pack_kernel, lengths),
         "pack_vectors",
-        vectors,
-        [VMEM] * len(vectors),
+        sums,
+        [VMEM] * len(sums),
         [(VMEM, shape_of(shape))] * 2,
     )
 
 
-def unpack_kernel(lengths, place_ref, own_ref, other_ref, *out_refs):
+def unpack_kernel(lengths, place_ref, own_ref, other_ref, out_ref):
     levels = own_ref.shape[0]
     first = place_ref[CORE] == 0
     shards = []
@@ -753,12 +787,12 @@
         other = other_ref[z].astype(f32)
         shards += [jnp.where(first, own, other), jnp.where(first, other, own)]
     at = 0
-    for length, out_ref in zip(lengths, out_refs):
+    for index, length in enumerate(lengths):
         pieces = []
         for shard in shards:
             for line in range(lines_of(length)):
                 pieces.append(shard[at + line : at + line + 1, : min(TILE, length - line * TILE)])
-        out_ref[...] = jnp.concatenate(pieces, axis=1).astype(bf16)
+        out_ref[index : index + 1, : length * len(shards)] = jnp.concatenate(pieces, axis=1).astype(bf16)
         at += lines_of(length)
 
 
@@ -769,8 +803,8 @@
         "unpack_vectors",
         [own, other],
         [VMEM] * 2,
-        [(VMEM, shape_of((1, 2 * levels * n))) for n in lengths],
-    )
+        [(VMEM, shape_of((ROWS, 2 * levels * max(lengths))))],
+    )[0]
 
 
 def start_kernel(lengths, groups, place_ref, *refs):
@@ -812,6 +846,7 @@
         + [pl.BlockSpec((w.shape[0] // 2, w.shape[1] // 2), lambda i, p: (p[Y], p[X])) for w in shards],
         outs,
         grid=(1,),
+        vmem=56,
     )
 
 
@@ -881,42 +916,41 @@
     return [near] + [swap(near, name + "_plane", dp=j) for j in (1, 2, 3)]
 
 
-def first_back_kernel(weight, place_ref, tok_ref, dx_ref, d_ref, gain_ref, *refs):
-    arrays, (out_ref, s_gain_ref, s_shift_ref, w_ref, sems) = split_refs(refs, [weight])
+def first_back_kernel(weight, place_ref, tok_ref, dx_ref, d_ref, vec_ref, *refs):
+    arrays, (out_ref, sums_ref, w_ref, sems) = split_refs(refs, [weight])
     width = tok_ref.shape[1]
 
     @pl.when(pl.program_id(0) == 0)
     def _():
         fetch_all(place_ref, [weight], arrays, [w_ref], sems)
-        s_gain_ref[...] = jnp.zeros_like(s_gain_ref)
-        s_shift_ref[...] = jnp.zeros_like(s_shift_ref)
+        sums_ref[...] = jnp.zeros_like(sums_ref)
 
     dh = dot_nt(d_ref[0], matrix(w_ref, slice(0, width)))
     dh = dh + dot_nt(d_ref[1], matrix(w_ref, slice(width, 2 * width)))
     dh = dh + dot_nt(d_ref[2], matrix(w_ref, slice(2 * width, 3 * width)))
     n1, inverse = normed(tok_ref[...].astype(f32))
-    s_gain_ref[...] += jnp.sum(dh * n1, axis=0, keepdims=True)
-    s_shift_ref[...] += jnp.sum(dh, axis=0, keepdims=True)
-    t = dh * gain_ref[...].astype(f32)
+    sums_ref[0:1, :] += jnp.sum(dh * n1, axis=0, keepdims=True)
+    sums_ref[1:2, :] += jnp.sum(dh, axis=0, keepdims=True)
+    t = dh * row(vec_ref, GAIN_ONE, width)
     inner = t - jnp.mean(t, axis=-1, keepdims=True) - n1 * jnp.mean(t * n1, axis=-1, keepdims=True)
     out_ref[...] = (dx_ref[...] + inverse * inner).astype(bf16)
 
 
-def first_back(order, tokens, dx1, dqkv, weight, gain, after):
+def first_back(order, tokens, dx1, dqkv, weight, vectors, after):
     rows, width = tokens.shape
     size = row_tile(rows, 320)
     rowwise = pl.BlockSpec((size, width), lambda i, p: (i, 0))
-    total = (out_whole((1, width)), shape_of((1, width), f32))
     return order(
         functools.partial(first_back_kernel, weight),
         "first_back",
-        [tokens, dx1, dqkv, gain] + weight.arrays,
-        [rowwise, rowwise, pl.BlockSpec((3, size, width), lambda i, p: (0, i, 0)), whole(gain.shape)]
+        [tokens, dx1, dqkv, vectors] + weight.arrays,
+        [rowwise, rowwise, pl.BlockSpec((3, size, width), lambda i, p: (0, i, 0)), whole(vectors.shape)]
         + [ANY] * len(weight.arrays),
-        [(rowwise, shape_of((rows, width))), total, total],
+        [(rowwise, shape_of((rows, width))), (out_whole((2, width)), shape_of((2, width), f32))],
         grid=(rows // size,),
         after=after,
         scratch=weight_scratch([weight]),
+        vmem=56,
     )
 
 
@@ -944,8 +978,8 @@
     shards = lax.axis_size("fsdp")
     levels = shards // 2
     order = Order(position())
-    vectors = (ln1_gain, ln1_bias, qv_bias, proj_bias, ln2_gain, ln2_bias, up_bias, down_bias, head_bias)
-    parts = [[v.shape[-1]] * (v.size // v.shape[-1]) for v in vectors]
+    own_vectors = (ln1_gain, ln1_bias, qv_bias, proj_bias, ln2_gain, ln2_bias, up_bias, down_bias, head_bias)
+    parts = [[v.shape[-1]] * (v.size // v.shape[-1]) for v in own_vectors]
     lengths = [length for part in parts for length in part]
     paired = (
         lax.axis_size("dp") == 4
@@ -963,7 +997,7 @@
 
     if paired:
         wide = [w_up, w_head, w_proj]
-        p_qkv, p_wide = start_gather(order, vectors, lengths, [[w_qkv], wide])
+        p_qkv, p_wide = start_gather(order, own_vectors, lengths, [[w_qkv], wide])
         got = [p_qkv] + [swap(p_qkv, "qkv_column", fsdp=2 * level) for level in range(1, levels)]
         got_wide = [swap(p_wide, "wide_column", fsdp=2 * level) for level in range(2, levels)]
         bias = make_masks(order, clip_counts, rows)
@@ -974,26 +1008,27 @@
         full_qkv = Weight([own, swap(own, "qkv_core", fsdp=1)], 0, (width, w_qkv.shape[1]))
         later, own = lax.optimization_barrier((p_wide, own))
         got_wide = [p_wide, swap(later, "wide_column", fsdp=2)] + got_wide
-        gathered = unpack_vectors(order, lines, other_lines, lengths)
+        vectors = unpack_vectors(order, lines, other_lines, lengths)
         (near,) = near_levels(order, got_wide, False, "wide_near")
         quarters = across_plane(near, "wide")
         later, near = lax.optimization_barrier((w_down, near))
         full_down = gather(later)
     else:
-        pieces = [piece for v in vectors for piece in ([v[0], v[1]] if v.ndim == 2 else [v])]
+        pieces = [piece for v in own_vectors for piece in ([v[0], v[1]] if v.ndim == 2 else [v])]
         joined = gather(jnp.concatenate(pieces)[None])
-        gathered, at = [], 0
+        lines, at = [], 0
         for length in lengths:
-            gathered.append(joined[:, at : at + length].reshape(1, -1))
+            line = joined[:, at : at + length].reshape(1, -1)
+            lines.append(jnp.pad(line, ((0, 0), (0, shards * max(lengths) - line.shape[1]))))
             at += length
+        vectors = jnp.pad(jnp.concatenate(lines), ((0, ROWS - len(lines)), (0, 0)))
         full_qkv, full_proj, full_up, full_head = (
             Weight([full], 0, full.shape) for full in (gather(w) for w in (w_qkv, w_proj, w_up, w_head))
         )
         full_down = gather(w_down)
         bias = make_masks(order, clip_counts, rows)
-    gain_one, shift_one, b_q, b_v, b_proj, gain_two, shift_two, b_up, b_down, b_head = gathered
     full_down = Weight([full_down], 0, full_down.shape)
-    h1, q, k, v = project_qkv(order, tokens, gain_one, shift_one, b_q, b_v, full_qkv)
+    h1, q, k, v = project_qkv(order, tokens, vectors, full_qkv)
     o, lse = attend(order, bias, q, k, v)
     if paired:
         own = assemble(order, wide, quarters, "wide_assemble")
@@ -1002,7 +1037,7 @@
         full_up, full_head, full_proj = (
             Weight(both_cores, column, (width, w.shape[1])) for column, w in zip(at, wide)
         )
-    (block_out, aligned, z, e_al, h2, g, du, dm, dx1, da, do, s_head, s_down, s_up, s_gain, s_shift, s_proj) = middle(
+    block_out, aligned, z, e_al, h2, g, du, dm, dx1, da, do, sums = middle(
         order,
         clip_counts,
         tokens,
@@ -1010,7 +1045,7 @@
         cot_out,
         cot_align,
         (full_proj, full_up, full_down, full_head),
-        (b_proj, gain_two, shift_two, b_up, b_down, b_head),
+        vectors,
     )
     d_down = scatter(outer(order, g, dm, 512, 768, "grad_down"))
     if paired:
@@ -1024,32 +1059,34 @@
         r_wide.split()
     dqkv, s_qv = attend_back(order, bias, q, k, v, o, do, lse)
     if paired:
-        r_qkv = Reduction(order, "qkv", parts)
+        r_qkv = Reduction(order, "qkv")
         n = w_qkv.shape[1]
         r_qkv.add(*outer_split(order, h1, dqkv, levels, width, n, 0, (), "grad_qkv"), [n])
-    grad_tokens, s_gain_one, s_shift_one = first_back(order, tokens, dx1, dqkv, full_qkv, gain_one, [d_down])
-    d_down = lax.psum(d_down, "dp")
-    sums = (s_gain_one, s_shift_one, s_qv[0:1], s_qv[1:2], s_proj, s_gain, s_shift, s_up, s_down, s_head)
+    grad_tokens, s_first = first_back(order, tokens, dx1, dqkv, full_qkv, vectors, [d_down])
     if paired:
-        r_qkv.add(*pack_vectors(order, sums, levels), [2 * TILE])
+        d_down = lax.psum_scatter(d_down, "dp", scatter_dimension=0, tiled=True)
+        r_qkv.split()
+        lines, send = pack_vectors(order, [sums, s_first, s_qv], lengths, levels)
+        lines = [lines, swap(send, "vectors_core", fsdp=1)]
         r_wide.levels()
-        r_qkv.split()
-        r_wide.total()
-        r_qkv.levels()
-        r_qkv.total(after=[d_down])
-        d_up, d_head, d_proj = r_wide.join()
-        d_qkv, d_down, *mine = r_qkv.join([d_down])
+        r_qkv.levels(lines)
+        r_wide.total([d_down])
+        r_qkv.total()
+        d_up, d_head, d_proj, d_down = r_wide.join(beside=w_down.shape)
+        d_qkv, *mine = r_qkv.join(lengths=parts)
     else:
 
         def reduce(value):
             return lax.psum(scatter(value), "dp").astype(f32)
 
-        d_down = d_down.astype(f32)
+        d_down = lax.psum(d_down, "dp").astype(f32)
         d_up = reduce(outer(order, h2, du, 768, 512, "grad_up"))
         d_head = reduce(outer(order, z, e_al, 768, 512, "grad_head"))
         d_proj = reduce(outer(order, o, da, 768, 384, "grad_proj"))
         d_qkv = reduce(outer(order, h1, jnp.concatenate([dqkv[0], dqkv[1], dqkv[2]], axis=1), 768, 768, "grad_qkv"))
-        joined = jnp.concatenate([s.reshape(shards, -1) for s in sums], axis=1)
+        late = {GAIN_ONE: s_first[0], SHIFT_ONE: s_first[1], B_Q: s_qv[0], B_V: s_qv[1]}
+        lines = [late.get(i, sums[i])[: shards * n].reshape(shards, n) for i, n in enumerate(lengths)]
+        joined = jnp.concatenate(lines, axis=1)
         joined = lax.psum(lax.psum_scatter(joined, "fsdp", scatter_dimension=0, tiled=True), "dp")[0]
         mine, at = [], 0
         for part in parts:

time: 337 us -> 303 us (0.90)
  Pallas kernels: 196 us -> 144 us
  waiting for transfers between devices: 69.6 us -> 91.1 us
    pallas_call x26, Pallas kernels: 196 us -> 144 us  [__call__(): pl.pallas_call(body, grid_spec=pltpu.PrefetchScalarGridSpec(num_scalar_pr...]
    ppermute x37, waiting for transfers between devices: 52.3 us -> 79.8 us  [swap(): return lax.ppermute(value, ('dp', 'fsdp'), pairs)]
    psum x1 -> x0, waiting for transfers between devices: 17.1 us -> none  [local(): d_down = lax.psum(d_down, 'dp')]
    all_gather x1, waiting for transfers between devices: 0.12 us -> 7.96 us  [gather(): return lax.all_gather(value, 'fsdp', axis=0, tiled=True)]
    unnamed x74 -> x88, local copies, waits for them, and re-layouts: 14.8 us -> 13.3 us
  transfers between devices with their start and end apart: 40 -> 40, of which waited for: 14 -> 17; matrix products, arithmetic and copies ran while one was open for 0% -> 0% of each run, Pallas kernels for 42% -> 31%
where the time goes in v3:
time: 303 us; the launch traced here: 302 us
  Pallas kernels  144 us (48%)
  waiting for transfers between devices  91.1 us (30%)
  starting transfers between devices  37.9 us (13%)
  between operations  14.4 us (5%)
  local copies, waits for them, and re-layouts  13.9 us (5%)
    pallas_call x26, Pallas kernels, __call__(): pl.pallas_call(body, grid_spec=pltpu.PrefetchScalarGridSpec(num_scalar_pr...  144 us
    ppermute x37, waiting for transfers between devices, swap(): return lax.ppermute(value, ('dp', 'fsdp'), pairs)  79.8 us
    ppermute x37, starting transfers between devices, swap(): return lax.ppermute(value, ('dp', 'fsdp'), pairs)  37.6 us
    unnamed x88, local copies, waits for them, and re-layouts  13.3 us
    all_gather x1, waiting for transfers between devices, gather(): return lax.all_gather(value, 'fsdp', axis=0, tiled=True)  7.96 us
  transfers between devices with their start and end apart: 40, of which 17 were waited for; matrix products, arithmetic and copies ran while one was open for 0% of the time, Pallas kernels for 31%

profile of v3, /device:TPU:0, one launch (start us, length us, event | category | flops | bytes accessed | tf_op | source)
XLA Modules:
  0.0 301.5 jit_solution(4011626666560741686)
XLA Ops:
  7.9 2.6 quarters.1
  10.5 5.0 %collective-permute-start.2 = (bf16[48,1280]{1,0:T(8,128)(2,1)}, bf16[48,1280]{1,0:T(8,128)(2,1)S(1)}, u32[]{:S(2)}, u32[]{:S(2)}) collective-permute-start(bf16[48,1280]{1,0:T(8,128)(2,1)} %get-tuple-element.85.refs_2_.refs_1_), channel_id=1, source_target_pairs={{0,6},{1,7},{2,4},{3,5},{4,2},{5,3},{6,0},{7,1},{8,14},{9,15},{10,... | collective-permute-start | bytes 368648 | tf_op jit(solution)/shard_map/qkv_column_0_6/ppermute | solution.py:127
  17.1 3.2 %masks.1.refs_5_.refs_1_ = f32[3072,128]{1,0:T(8,128)S(1)} custom-call(s32[5]{0:T(128)S(1)} %copy-done.6, s32[32,32]{1,0:T(8,128)S(1)} %copy-done.5, bf16[48,1280]{1,0:T(8,128)(2,1)S(1)} %copy-done.22), custom_call_target="tpu_custom_call" | custom-call | flops 10000000000 | bytes 1 | tf_op jit(solution)/shard_map/masks/pallas_call | solution.py:95
  20.4 5.8 %collective-permute-done.1.refs_3_ = bf16[48,1280]{1,0:T(8,128)(2,1)S(1)} collective-permute-done((bf16[48,1280]{1,0:T(8,128)(2,1)}, bf16[48,1280]{1,0:T(8,128)(2,1)S(1)}, u32[]{:S(2)}, u32[]{:S(2)}) %collective-permute-start.1) | collective-permute-done | bytes 122912 | tf_op jit(solution)/shard_map/qkv_column_0_4/ppermute | solution.py:127
  26.7 2.5 collective-permute-start.6
  30.3 2.5 collective-permute-start.10
  32.8 5.7 %collective-permute-done.6.refs_5_ = bf16[3,48,1152]{2,1,0:T(8,128)(2,1)S(1)} collective-permute-done((bf16[3,48,1152]{2,1,0:T(8,128)(2,1)S(1)}, bf16[3,48,1152]{2,1,0:T(8,128)(2,1)S(1)}, u32[]{:S(2)}, u32[]{:S(2)}) %collective-permute-start.6) | collective-permute-done | bytes 331808 | tf_op jit(solution)/shard_map/qkv_plane_3_0/ppermute | solution.py:127
  38.5 5.2 %collective-permute-done.5.refs_4_ = bf16[3,48,1152]{2,1,0:T(8,128)(2,1)S(1)} collective-permute-done((bf16[3,48,1152]{2,1,0:T(8,128)(2,1)S(1)}, bf16[3,48,1152]{2,1,0:T(8,128)(2,1)S(1)}, u32[]{:S(2)}, u32[]{:S(2)}) %collective-permute-start.5) | collective-permute-done | bytes 331808 | tf_op jit(solution)/shard_map/qkv_plane_2_0/ppermute | solution.py:127
  45.3 5.3 %collective-permute-done.9.refs_3_ = bf16[48,2432]{1,0:T(8,128)(2,1)S(1)} collective-permute-done((bf16[48,2432]{1,0:T(8,128)(2,1)S(1)}, bf16[48,2432]{1,0:T(8,128)(2,1)S(1)}, u32[]{:S(2)}, u32[]{:S(2)}) %collective-permute-start.9) | collective-permute-done | bytes 233504 | tf_op jit(solution)/shard_map/wide_column_0_4/ppermute | solution.py:127
  50.6 4.8 %collective-permute-done.8.refs_2_ = bf16[48,2432]{1,0:T(8,128)(2,1)S(1)} collective-permute-done((bf16[48,2432]{1,0:T(8,128)(2,1)S(1)}, bf16[48,2432]{1,0:T(8,128)(2,1)S(1)}, u32[]{:S(2)}, u32[]{:S(2)}) %collective-permute-start.8) | collective-permute-done | bytes 233504 | tf_op jit(solution)/shard_map/wide_column_0_2/ppermute | solution.py:127
  61.6 7.1 %norm_qkv.1 = (bf16[960,768]{1,0:T(8,128)(2,1)S(1)}, bf16[960,768]{1,0:T(8,128)(2,1)S(1)}, bf16[960,768]{1,0:T(8,128)(2,1)S(1)}, bf16[960,768]{1,0:T(8,128)(2,1)S(1)}) custom-call(s32[5]{0:T(128)S(1)} %copy-done.6, bf16[960,768]{1,0:T(8,128)(2,1)S(1)} %copy-done.1, bf16[16,3072]{1,0:T(8,128)(2,1)S(1)} %unpack_vectors.1.refs_5_.refs_2_.refs_6_.refs_4_, ...), custom_call_target="tpu_custom_call" | custom-call | flops 10000000000 | bytes 1 | tf_op jit(solution)/shard_map/norm_qkv/pallas_call | solution.py:95
  68.7 10.0 %attend.1 = (bf16[960,768]{1,0:T(8,128)(2,1)S(1)}, f32[6,8,256]{2,1,0:T(8,128)S(1)}) custom-call(s32[5]{0:T(128)S(1)} %copy-done.6, f32[3072,128]{1,0:T(8,128)S(1)} %copy-done.30, bf16[960,768]{1,0:T(8,128)(2,1)S(1)} %get-tuple-element.90.refs_2_, bf16[960,768]{1,0:T(8,128)(2,1)S(1)} %get-tuple-element.91.refs_3_, ...), custom_call_target="tpu_custom_call" | custom-call | flops 10000000000 | bytes 1 | tf_op jit(solution)/shard_map/attend/pallas_call | solution.py:95
  78.8 11.7 %collective-permute-done.12.refs_6_ = bf16[3,48,2432]{2,1,0:T(8,128)(2,1)S(1)} collective-permute-done((bf16[3,48,2432]{2,1,0:T(8,128)(2,1)}, bf16[3,48,2432]{2,1,0:T(8,128)(2,1)S(1)}, u32[]{:S(2)}, u32[]{:S(2)}) %collective-permute-start.12) | collective-permute-done | bytes 700448 | tf_op jit(solution)/shard_map/wide_plane_2_0/ppermute | solution.py:127
  93.6 6.7 %collective-permute-done.14.refs_8_.refs_10_.refs_13_ = bf16[4,96,4864]{2,1,0:T(8,128)(2,1)} collective-permute-done((bf16[4,96,4864]{2,1,0:T(8,128)(2,1)S(1)}, bf16[4,96,4864]{2,1,0:T(8,128)(2,1)}, u32[]{:S(2)}, u32[]{:S(2)}) %collective-permute-start.14) | collective-permute-done | bytes 3735584 | tf_op jit(solution)/shard_map/wide_core_0_1/ppermute | solution.py:127
  100.3 8.0 %all-gather.2.cloned.1.call-done.refs_11_ = bf16[3072,768]{1,0:T(8,128)(2,1)} async-done(((bf16[384,768]{1,0:T(8,128)(2,1)}), bf16[3072,768]{1,0:T(8,128)(2,1)}) %all-gather.2.cloned.1.call-update) | async-done | bytes 4718608 | tf_op jit(solution)/shard_map/all_gather | solution.py:993
  108.2 36.5 %middle.1 = (bf16[960,768]{1,0:T(8,128)(2,1)}, bf16[960,1024]{1,0:T(8,128)(2,1)}, bf16[960,768]{1,0:T(8,128)(2,1)}, bf16[960,1024]{1,0:T(8,128)(2,1)}, bf16[960,...) custom-call(s32[5]{0:T(128)} %stack.23.refs_0_, ...), custom_call_target="tpu_custom_call" | custom-call | flops 10000000000 | bytes 1 | tf_op jit(solution)/shard_map/middle/pallas_call | solution.py:95
  144.8 10.5 %grad_down.1.refs_3_ = bf16[3072,768]{1,0:T(8,128)(2,1)} custom-call(s32[5]{0:T(128)} %stack.23.refs_0_, bf16[960,3072]{1,0:T(8,128)(2,1)} %get-tuple-element.103.refs_1_, bf16[960,768]{1,0:T(8,128)(2,1)} %get-tuple-element.104.refs_2_, bf16[960,768]{1,0:T(8,128)(2,1)} %get-tuple-element.68.refs_3_), custom_call_target="tpu_custom_call" | custom-call | flops 10000000000 | bytes 1 | tf_op jit(solution)/shard_map/grad_down/pallas_call | solution.py:95
  155.6 10.2 %grad_up.1 = (bf16[4,2,48,3072]{3,2,1,0:T(8,128)(2,1)}, bf16[4,2,48,3072]{3,2,1,0:T(8,128)(2,1)}) custom-call(s32[5]{0:T(128)} %stack.23.refs_0_, bf16[960,768]{1,0:T(8,128)(2,1)} %get-tuple-element.101.refs_1_, bf16[960,3072]{1,0:T(8,128)(2,1)} %get-tuple-element.102.refs_2_, bf16[3072,768]{1,0:T(8,128)(2,1)} %grad_down.1.refs_3_), custom_call_target="tpu_custom_call" | custom-call | flops 10000000000 | bytes 1 | tf_op jit(solution)/shard_map/grad_up/pallas_call | solution.py:95
  166.1 5.8 %grad_head.1 = (bf16[4,2,48,1792]{3,2,1,0:T(8,128)(2,1)}, bf16[4,2,48,1792]{3,2,1,0:T(8,128)(2,1)}) custom-call(s32[5]{0:T(128)} %stack.23.refs_0_, bf16[960,768]{1,0:T(8,128)(2,1)} %get-tuple-element.108.refs_1_, bf16[960,1024]{1,0:T(8,128)(2,1)} %get-tuple-element.109.refs_2_, bf16[4,2,48,3072]{3,2,1,0:T(8,128)(2,1)} %get-tuple-element.105.refs_3_.refs_1_), custom_call_target="tpu_custom_call" | custom-call | flops 10000000000 | bytes 1 | tf_op jit(solution)/shard_map/grad_head/pallas_call | solution.py:95
  171.9 6.0 %grad_proj.1 = (bf16[4,2,48,1792]{3,2,1,0:T(8,128)(2,1)}, bf16[4,2,48,1792]{3,2,1,0:T(8,128)(2,1)}) custom-call(s32[5]{0:T(128)} %stack.23.refs_0_, bf16[960,768]{1,0:T(8,128)(2,1)} %copy-done.2, bf16[960,768]{1,0:T(8,128)(2,1)} %get-tuple-element.107.refs_2_, ...), custom_call_target="tpu_custom_call", output_to_operand_aliasing={{0}: (3, {}), {1}: (4, {})} | custom-call | flops 10000000000 | bytes 1 | tf_op jit(solution)/shard_map/grad_proj/pallas_call | solution.py:95
  178.2 3.2 %collective-permute-done.16.refs_4_ = bf16[4,2,48,1792]{3,2,1,0:T(8,128)(2,1)S(1)} collective-permute-done((bf16[4,2,48,1792]{3,2,1,0:T(8,128)(2,1)}, bf16[4,2,48,1792]{3,2,1,0:T(8,128)(2,1)S(1)}, u32[]{:S(2)}, u32[]{:S(2)}) %collective-permute-start.16) | collective-permute-done | bytes 1376288 | tf_op jit(solution)/shard_map/wide_core_0_1/ppermute | solution.py:127
  182.8 2.6 wide_split.1
  188.9 15.4 %attend_back.1 = (bf16[3,960,768]{2,1,0:T(8,128)(2,1)S(1)}, f32[2,768]{1,0:T(2,128)S(1)}) custom-call(s32[5]{0:T(128)S(1)} %copy-done.7, f32[3072,128]{1,0:T(8,128)S(1)} %copy-done.31, bf16[960,768]{1,0:T(8,128)(2,1)S(1)} %copy-done.34, bf16[960,768]{1,0:T(8,128)(2,1)S(1)} %copy-done.36, bf16[960,768]{1,0:T(8,128)(2,1)S(1)} %copy-done.38, ...), custom_call_target="tpu_custom_call" | custom-call | flops 20000000000 | bytes 1 | tf_op jit(solution)/shard_map/attend_back/pallas_call | solution.py:95
  206.4 8.7 %grad_qkv.1 = (bf16[4,2,48,2304]{3,2,1,0:T(8,128)(2,1)}, bf16[4,2,48,2304]{3,2,1,0:T(8,128)(2,1)}) custom-call(s32[5]{0:T(128)} %stack.23.refs_0_, bf16[960,768]{1,0:T(8,128)(2,1)} %copy-done.28, bf16[3,960,768]{2,1,0:T(8,128)(2,1)} %copy-done.25, bf16[3,960,768]{2,1,0:T(8,128)(2,1)} %copy-done.25), custom_call_target="tpu_custom_call" | custom-call | flops 10000000000 | bytes 1 | tf_op jit(solution)/shard_map/grad_qkv/pallas_call | solution.py:95
  215.2 11.0 %first_back.1 = (bf16[960,768]{1,0:T(8,128)(2,1)}, f32[2,768]{1,0:T(2,128)}) custom-call(s32[5]{0:T(128)} %stack.23.refs_0_, bf16[960,768]{1,0:T(8,128)(2,1)} %refs_1_.13, f32[960,768]{1,0:T(8,128)} %get-tuple-element.98.refs_2_, bf16[3,960,768]{2,1,0:T(8,128)(2,1)} %copy-done.25, bf16[16,3072]{1,0:T(8,128)(2,1)} %copy-done.4, ...), custom_call_target="tpu_custom_call" | custom-call | flops 20000000000 | bytes 1 | tf_op jit(solution)/shard_map/first_back/pallas_call | solution.py:95
  235.7 2.5 wide_levels.1
  239.7 7.6 %collective-permute-done.18.refs_2_ = bf16[4,48,1152]{2,1,0:T(8,128)(2,1)S(1)} collective-permute-done((bf16[4,48,1152]{2,1,0:T(8,128)(2,1)}, bf16[4,48,1152]{2,1,0:T(8,128)(2,1)S(1)}, u32[]{:S(2)}, u32[]{:S(2)}) %collective-permute-start.18) | collective-permute-done | bytes 442400 | tf_op jit(solution)/shard_map/qkv_plane_1_0/ppermute | solution.py:127
  247.4 9.7 %collective-permute-done.19.refs_3_ = bf16[4,48,1152]{2,1,0:T(8,128)(2,1)S(1)} collective-permute-done((bf16[4,48,1152]{2,1,0:T(8,128)(2,1)}, bf16[4,48,1152]{2,1,0:T(8,128)(2,1)S(1)}, u32[]{:S(2)}, u32[]{:S(2)}) %collective-permute-start.19) | collective-permute-done | bytes 442400 | tf_op jit(solution)/shard_map/qkv_plane_2_0/ppermute | solution.py:127
  259.8 2.6 collective-permute-start.27
  262.4 3.4 %reduce-scatter.5.cloned.1.call-done.refs_5_ = bf16[96,768]{1,0:T(8,128)(2,1)} async-done(((bf16[384,768]{1,0:T(8,128)(2,1)}), bf16[96,768]{1,0:T(8,128)(2,1)}) %reduce-scatter.5.cloned.1.call-update) | async-done | bytes 147472 | tf_op jit(solution)/shard_map/reduce_scatter | solution.py:1067
  274.5 5.6 %collective-permute-done.36.refs_4_ = bf16[48,3968]{1,0:T(8,128)(2,1)S(1)} collective-permute-done((bf16[48,3968]{1,0:T(8,128)(2,1)S(1)}, bf16[48,3968]{1,0:T(8,128)(2,1)S(1)}, u32[]{:S(2)}, u32[]{:S(2)}) %collective-permute-start.36) | collective-permute-done | bytes 380960 | tf_op jit(solution)/shard_map/wide_back_3_0/ppermute | solution.py:127
  281.5 6.8 %collective-permute-done.35.refs_3_ = bf16[48,3968]{1,0:T(8,128)(2,1)S(1)} collective-permute-done((bf16[48,3968]{1,0:T(8,128)(2,1)S(1)}, bf16[48,3968]{1,0:T(8,128)(2,1)S(1)}, u32[]{:S(2)}, u32[]{:S(2)}) %collective-permute-start.35) | collective-permute-done | bytes 380960 | tf_op jit(solution)/shard_map/wide_back_2_0/ppermute | solution.py:127
  (166 shorter events, 52.9 us)
Async XLA Ops:
  7.2 101.1 %all-gather.2.cloned.1.call-start = ((), (), s32[]{:S(2)}) async-start(), calls=%async_computation.2 | async-start | bytes 5308416 | tf_op jit(solution)/shard_map/all_gather | solution.py:993
  26.7 11.7 %collective-permute-start.6 = (bf16[3,48,1152]{2,1,0:T(8,128)(2,1)S(1)}, bf16[3,48,1152]{2,1,0:T(8,128)(2,1)S(1)}, u32[]{:S(2)}, u32[]{:S(2)}) collective-permute-start(bf16[3,48,1152]{2,1,0:T(8,128)(2,1)S(1)} %get-tuple-element.87.refs_2_.refs_6_), channel_id=1, source_target_pairs={{0,24},{1,25},{2,26},{3,27},{4,28},{5,29},{6,30},{7,31},{8,16},{9,... | collective-permute-start | bytes 995336 | tf_op jit(solution)/shard_map/qkv_plane_3_0/ppermute | solution.py:127
  29.3 14.4 %collective-permute-start.5 = (bf16[3,48,1152]{2,1,0:T(8,128)(2,1)S(1)}, bf16[3,48,1152]{2,1,0:T(8,128)(2,1)S(1)}, u32[]{:S(2)}, u32[]{:S(2)}) collective-permute-start(bf16[3,48,1152]{2,1,0:T(8,128)(2,1)S(1)} %get-tuple-element.87.refs_2_.refs_6_), channel_id=1, source_target_pairs={{0,16},{1,17},{2,18},{3,19},{4,20},{5,21},{6,22},{7,23},{8,24},{9,... | collective-permute-start | bytes 995336 | tf_op jit(solution)/shard_map/qkv_plane_2_0/ppermute | solution.py:127
  29.8 14.0 %collective-permute-start.4 = (bf16[3,48,1152]{2,1,0:T(8,128)(2,1)S(1)}, bf16[3,48,1152]{2,1,0:T(8,128)(2,1)S(1)}, u32[]{:S(2)}, u32[]{:S(2)}) collective-permute-start(bf16[3,48,1152]{2,1,0:T(8,128)(2,1)S(1)} %get-tuple-element.87.refs_2_.refs_6_), channel_id=1, source_target_pairs={{0,8},{1,9},{2,10},{3,11},{4,12},{5,13},{6,14},{7,15},{8,0},{9,1},... | collective-permute-start | bytes 995336 | tf_op jit(solution)/shard_map/qkv_plane_1_0/ppermute | solution.py:127
  30.3 15.0 %collective-permute-start.10 = (bf16[48,2432]{1,0:T(8,128)(2,1)S(1)}, bf16[48,2432]{1,0:T(8,128)(2,1)S(1)}, u32[]{:S(2)}, u32[]{:S(2)}) collective-permute-start(bf16[48,2432]{1,0:T(8,128)(2,1)S(1)} %copy-done.17), channel_id=1, source_target_pairs={{0,6},{1,7},{2,4},{3,5},{4,2},{5,3},{6,0},{7,1},{8,14},{9,15},{10,... | collective-permute-start | bytes 700424 | tf_op jit(solution)/shard_map/wide_column_0_6/ppermute | solution.py:127
  32.8 17.8 %collective-permute-start.9 = (bf16[48,2432]{1,0:T(8,128)(2,1)S(1)}, bf16[48,2432]{1,0:T(8,128)(2,1)S(1)}, u32[]{:S(2)}, u32[]{:S(2)}) collective-permute-start(bf16[48,2432]{1,0:T(8,128)(2,1)S(1)} %copy-done.17), channel_id=1, source_target_pairs={{0,4},{1,5},{2,6},{3,7},{4,0},{5,1},{6,2},{7,3},{8,12},{9,13},{10,... | collective-permute-start | bytes 700424 | tf_op jit(solution)/shard_map/wide_column_0_4/ppermute | solution.py:127
  44.5 16.0 %collective-permute-start.7 = (bf16[4,96,2304]{2,1,0:T(8,128)(2,1)S(1)}, bf16[4,96,2304]{2,1,0:T(8,128)(2,1)}, u32[]{:S(2)}, u32[]{:S(2)}) collective-permute-start(bf16[4,96,2304]{2,1,0:T(8,128)(2,1)S(1)} %bitcast.16), channel_id=1, source_target_pairs={{0,1},{1,0},{2,3},{3,2},{4,5},{5,4},{6,7},{7,6},{8,9},{9,8},{10,11... | collective-permute-start | bytes 5308424 | tf_op jit(solution)/shard_map/qkv_core_0_1/ppermute | solution.py:127
  56.8 158.3 %reduce-scatter.3.cloned.1.call-start = ((), (), s32[]{:S(2)}) async-start(), calls=%async_computation.3 | async-start | bytes 5308416 | tf_op jit(solution)/shard_map/reduce_scatter | solution.py:996
  56.9 21.9 %collective-permute-start.13 = (bf16[3,48,2432]{2,1,0:T(8,128)(2,1)}, bf16[3,48,2432]{2,1,0:T(8,128)(2,1)S(1)}, u32[]{:S(2)}, u32[]{:S(2)}) collective-permute-start(bf16[3,48,2432]{2,1,0:T(8,128)(2,1)} %copy-done.11), channel_id=1, source_target_pairs={{0,24},{1,25},{2,26},{3,27},{4,28},{5,29},{6,30},{7,31},{8,16},{9,... | collective-permute-start | bytes 2101256 | tf_op jit(solution)/shard_map/wide_plane_3_0/ppermute | solution.py:127
  59.0 31.5 %collective-permute-start.12 = (bf16[3,48,2432]{2,1,0:T(8,128)(2,1)}, bf16[3,48,2432]{2,1,0:T(8,128)(2,1)S(1)}, u32[]{:S(2)}, u32[]{:S(2)}) collective-permute-start(bf16[3,48,2432]{2,1,0:T(8,128)(2,1)} %copy-done.11), channel_id=1, source_target_pairs={{0,16},{1,17},{2,18},{3,19},{4,20},{5,21},{6,22},{7,23},{8,24},{9,... | collective-permute-start | bytes 2101256 | tf_op jit(solution)/shard_map/wide_plane_2_0/ppermute | solution.py:127
  59.9 30.6 %collective-permute-start.11 = (bf16[3,48,2432]{2,1,0:T(8,128)(2,1)}, bf16[3,48,2432]{2,1,0:T(8,128)(2,1)S(1)}, u32[]{:S(2)}, u32[]{:S(2)}) collective-permute-start(bf16[3,48,2432]{2,1,0:T(8,128)(2,1)} %copy-done.11), channel_id=1, source_target_pairs={{0,8},{1,9},{2,10},{3,11},{4,12},{5,13},{6,14},{7,15},{8,0},{9,1},... | collective-permute-start | bytes 2101256 | tf_op jit(solution)/shard_map/wide_plane_1_0/ppermute | solution.py:127
  155.4 110.4 %reduce-scatter.5.cloned.1.call-start = ((), (), s32[]{:S(2)}) async-start(), calls=%async_computation.4 | async-start | bytes 737280 | tf_op jit(solution)/shard_map/reduce_scatter | solution.py:1067
  165.8 15.6 %collective-permute-start.15 = (bf16[4,2,48,3072]{3,2,1,0:T(8,128)(2,1)}, bf16[4,2,48,3072]{3,2,1,0:T(8,128)(2,1)S(1)}, u32[]{:S(2)}, u32[]{:S(2)}) collective-permute-start(bf16[4,2,48,3072]{3,2,1,0:T(8,128)(2,1)} %get-tuple-element.106), channel_id=1, source_target_pairs={{0,1},{1,0},{2,3},{3,2},{4,5},{5,4},{6,7},{7,6},{8,9},{9,8},{10,11... | collective-permute-start | bytes 7077896 | tf_op jit(solution)/shard_map/wide_core_0_1/ppermute | solution.py:127
  185.4 47.0 %collective-permute-start.22 = (bf16[4,48,2432]{2,1,0:T(8,128)(2,1)}, bf16[4,48,2432]{2,1,0:T(8,128)(2,1)S(1)}, u32[]{:S(2)}, u32[]{:S(2)}) collective-permute-start(bf16[4,48,2432]{2,1,0:T(8,128)(2,1)} %get-tuple-element.128), channel_id=1, source_target_pairs={{0,8},{1,9},{2,10},{3,11},{4,12},{5,13},{6,14},{7,15},{8,0},{9,1},... | collective-permute-start | bytes 2801672 | tf_op jit(solution)/shard_map/wide_plane_1_0/ppermute | solution.py:127
  186.9 47.0 %collective-permute-start.23 = (bf16[4,48,2432]{2,1,0:T(8,128)(2,1)}, bf16[4,48,2432]{2,1,0:T(8,128)(2,1)}, u32[]{:S(2)}, u32[]{:S(2)}) collective-permute-start(bf16[4,48,2432]{2,1,0:T(8,128)(2,1)} %get-tuple-element.129), channel_id=1, source_target_pairs={{0,16},{1,17},{2,18},{3,19},{4,20},{5,21},{6,22},{7,23},{8,24},{9,... | collective-permute-start | bytes 2801672 | tf_op jit(solution)/shard_map/wide_plane_2_0/ppermute | solution.py:127
  188.3 46.2 %collective-permute-start.24 = (bf16[4,48,2432]{2,1,0:T(8,128)(2,1)}, bf16[4,48,2432]{2,1,0:T(8,128)(2,1)}, u32[]{:S(2)}, u32[]{:S(2)}) collective-permute-start(bf16[4,48,2432]{2,1,0:T(8,128)(2,1)} %get-tuple-element.130), channel_id=1, source_target_pairs={{0,24},{1,25},{2,26},{3,27},{4,28},{5,29},{6,30},{7,31},{8,16},{9,... | collective-permute-start | bytes 2801672 | tf_op jit(solution)/shard_map/wide_plane_3_0/ppermute | solution.py:127
  215.2 11.0 %collective-permute-start.17 = (bf16[4,2,48,2304]{3,2,1,0:T(8,128)(2,1)}, bf16[4,2,48,2304]{3,2,1,0:T(8,128)(2,1)S(1)}, u32[]{:S(2)}, u32[]{:S(2)}) collective-permute-start(bf16[4,2,48,2304]{3,2,1,0:T(8,128)(2,1)} %get-tuple-element.118), channel_id=1, source_target_pairs={{0,1},{1,0},{2,3},{3,2},{4,5},{5,4},{6,7},{7,6},{8,9},{9,8},{10,11... | collective-permute-start | bytes 5308424 | tf_op jit(solution)/shard_map/qkv_core_0_1/ppermute | solution.py:127
  230.9 16.4 %collective-permute-start.18 = (bf16[4,48,1152]{2,1,0:T(8,128)(2,1)}, bf16[4,48,1152]{2,1,0:T(8,128)(2,1)S(1)}, u32[]{:S(2)}, u32[]{:S(2)}) collective-permute-start(bf16[4,48,1152]{2,1,0:T(8,128)(2,1)} %get-tuple-element.120), channel_id=1, source_target_pairs={{0,8},{1,9},{2,10},{3,11},{4,12},{5,13},{6,14},{7,15},{8,0},{9,1},... | collective-permute-start | bytes 1327112 | tf_op jit(solution)/shard_map/qkv_plane_1_0/ppermute | solution.py:127
  232.4 24.7 %collective-permute-start.19 = (bf16[4,48,1152]{2,1,0:T(8,128)(2,1)}, bf16[4,48,1152]{2,1,0:T(8,128)(2,1)S(1)}, u32[]{:S(2)}, u32[]{:S(2)}) collective-permute-start(bf16[4,48,1152]{2,1,0:T(8,128)(2,1)} %copy-done.16), channel_id=1, source_target_pairs={{0,16},{1,17},{2,18},{3,19},{4,20},{5,21},{6,22},{7,23},{8,24},{9,... | collective-permute-start | bytes 1327112 | tf_op jit(solution)/shard_map/qkv_plane_2_0/ppermute | solution.py:127
  233.9 23.2 %collective-permute-start.20 = (bf16[4,48,1152]{2,1,0:T(8,128)(2,1)S(1)}, bf16[4,48,1152]{2,1,0:T(8,128)(2,1)S(1)}, u32[]{:S(2)}, u32[]{:S(2)}) collective-permute-start(bf16[4,48,1152]{2,1,0:T(8,128)(2,1)S(1)} %get-tuple-element.122), channel_id=1, source_target_pairs={{0,24},{1,25},{2,26},{3,27},{4,28},{5,29},{6,30},{7,31},{8,16},{9,... | collective-permute-start | bytes 1327112 | tf_op jit(solution)/shard_map/qkv_plane_3_0/ppermute | solution.py:127
  238.2 21.5 %collective-permute-start.28 = (bf16[48,2432]{1,0:T(8,128)(2,1)S(1)}, bf16[48,2432]{1,0:T(8,128)(2,1)S(1)}, u32[]{:S(2)}, u32[]{:S(2)}) collective-permute-start(bf16[48,2432]{1,0:T(8,128)(2,1)S(1)} %get-tuple-element.136), channel_id=1, source_target_pairs={{0,2},{1,3},{2,0},{3,1},{4,6},{5,7},{6,4},{7,5},{8,10},{9,11},{10,... | collective-permute-start | bytes 700424 | tf_op jit(solution)/shard_map/wide_column_0_2/ppermute | solution.py:127
  238.3 24.1 %collective-permute-start.29 = (bf16[48,2432]{1,0:T(8,128)(2,1)S(1)}, bf16[48,2432]{1,0:T(8,128)(2,1)S(1)}, u32[]{:S(2)}, u32[]{:S(2)}) collective-permute-start(bf16[48,2432]{1,0:T(8,128)(2,1)S(1)} %get-tuple-element.137), channel_id=1, source_target_pairs={{0,4},{1,5},{2,6},{3,7},{4,0},{5,1},{6,2},{7,3},{8,12},{9,13},{10,... | collective-permute-start | bytes 700424 | tf_op jit(solution)/shard_map/wide_column_0_4/ppermute | solution.py:127
  247.3 15.1 %collective-permute-start.30 = (bf16[48,2432]{1,0:T(8,128)(2,1)S(1)}, bf16[48,2432]{1,0:T(8,128)(2,1)S(1)}, u32[]{:S(2)}, u32[]{:S(2)}) collective-permute-start(bf16[48,2432]{1,0:T(8,128)(2,1)S(1)} %get-tuple-element.138), channel_id=1, source_target_pairs={{0,6},{1,7},{2,4},{3,5},{4,2},{5,3},{6,0},{7,1},{8,14},{9,15},{10,... | collective-permute-start | bytes 700424 | tf_op jit(solution)/shard_map/wide_column_0_6/ppermute | solution.py:127
  257.9 12.4 %collective-permute-start.25 = (bf16[48,1280]{1,0:T(8,128)(2,1)S(1)}, bf16[48,1280]{1,0:T(8,128)(2,1)S(1)}, u32[]{:S(2)}, u32[]{:S(2)}) collective-permute-start(bf16[48,1280]{1,0:T(8,128)(2,1)S(1)} %get-tuple-element.133), channel_id=1, source_target_pairs={{0,2},{1,3},{2,0},{3,1},{4,6},{5,7},{6,4},{7,5},{8,10},{9,11},{10,... | collective-permute-start | bytes 368648 | tf_op jit(solution)/shard_map/qkv_column_0_2/ppermute | solution.py:127
  258.0 12.8 %collective-permute-start.26 = (bf16[48,1280]{1,0:T(8,128)(2,1)S(1)}, bf16[48,1280]{1,0:T(8,128)(2,1)S(1)}, u32[]{:S(2)}, u32[]{:S(2)}) collective-permute-start(bf16[48,1280]{1,0:T(8,128)(2,1)S(1)} %get-tuple-element.134), channel_id=1, source_target_pairs={{0,4},{1,5},{2,6},{3,7},{4,0},{5,1},{6,2},{7,3},{8,12},{9,13},{10,... | collective-permute-start | bytes 368648 | tf_op jit(solution)/shard_map/qkv_column_0_4/ppermute | solution.py:127
  259.8 11.1 %collective-permute-start.27 = (bf16[48,1280]{1,0:T(8,128)(2,1)S(1)}, bf16[48,1280]{1,0:T(8,128)(2,1)S(1)}, u32[]{:S(2)}, u32[]{:S(2)}) collective-permute-start(bf16[48,1280]{1,0:T(8,128)(2,1)S(1)} %get-tuple-element.135), channel_id=1, source_target_pairs={{0,6},{1,7},{2,4},{3,5},{4,2},{5,3},{6,0},{7,1},{8,14},{9,15},{10,... | collective-permute-start | bytes 368648 | tf_op jit(solution)/shard_map/qkv_column_0_6/ppermute | solution.py:127
  267.3 12.8 %collective-permute-start.36 = (bf16[48,3968]{1,0:T(8,128)(2,1)S(1)}, bf16[48,3968]{1,0:T(8,128)(2,1)S(1)}, u32[]{:S(2)}, u32[]{:S(2)}) collective-permute-start(bf16[48,3968]{1,0:T(8,128)(2,1)S(1)} %wide_total.1.refs_5_.refs_1_), channel_id=1, source_target_pairs={{0,24},{1,25},{2,26},{3,27},{4,28},{5,29},{6,30},{7,31},{8,16},{9,... | collective-permute-start | bytes 1142792 | tf_op jit(solution)/shard_map/wide_back_3_0/ppermute | solution.py:127
  268.9 19.5 %collective-permute-start.35 = (bf16[48,3968]{1,0:T(8,128)(2,1)S(1)}, bf16[48,3968]{1,0:T(8,128)(2,1)S(1)}, u32[]{:S(2)}, u32[]{:S(2)}) collective-permute-start(bf16[48,3968]{1,0:T(8,128)(2,1)S(1)} %wide_total.1.refs_5_.refs_1_), channel_id=1, source_target_pairs={{0,16},{1,17},{2,18},{3,19},{4,20},{5,21},{6,22},{7,23},{8,24},{9,... | collective-permute-start | bytes 1142792 | tf_op jit(solution)/shard_map/wide_back_2_0/ppermute | solution.py:127
  270.3 18.0 %collective-permute-start.34 = (bf16[48,3968]{1,0:T(8,128)(2,1)S(1)}, bf16[48,3968]{1,0:T(8,128)(2,1)S(1)}, u32[]{:S(2)}, u32[]{:S(2)}) collective-permute-start(bf16[48,3968]{1,0:T(8,128)(2,1)S(1)} %wide_total.1.refs_5_.refs_1_), channel_id=1, source_target_pairs={{0,8},{1,9},{2,10},{3,11},{4,12},{5,13},{6,14},{7,15},{8,0},{9,1},... | collective-permute-start | bytes 1142792 | tf_op jit(solution)/shard_map/wide_back_1_0/ppermute | solution.py:127
  271.5 19.4 %collective-permute-start.33 = (bf16[48,1280]{1,0:T(8,128)(2,1)S(1)}, bf16[48,1280]{1,0:T(8,128)(2,1)S(1)}, u32[]{:S(2)}, u32[]{:S(2)}) collective-permute-start(bf16[48,1280]{1,0:T(8,128)(2,1)S(1)} %qkv_total.1.refs_5_.refs_1_), channel_id=1, source_target_pairs={{0,24},{1,25},{2,26},{3,27},{4,28},{5,29},{6,30},{7,31},{8,16},{9,... | collective-permute-start | bytes 368648 | tf_op jit(solution)/shard_map/qkv_back_3_0/ppermute | solution.py:127
  273.0 19.2 %collective-permute-start.32 = (bf16[48,1280]{1,0:T(8,128)(2,1)S(1)}, bf16[48,1280]{1,0:T(8,128)(2,1)S(1)}, u32[]{:S(2)}, u32[]{:S(2)}) collective-permute-start(bf16[48,1280]{1,0:T(8,128)(2,1)S(1)} %qkv_total.1.refs_5_.refs_1_), channel_id=1, source_target_pairs={{0,16},{1,17},{2,18},{3,19},{4,20},{5,21},{6,22},{7,23},{8,24},{9,... | collective-permute-start | bytes 368648 | tf_op jit(solution)/shard_map/qkv_back_2_0/ppermute | solution.py:127
  280.1 12.1 %collective-permute-start.31 = (bf16[48,1280]{1,0:T(8,128)(2,1)S(1)}, bf16[48,1280]{1,0:T(8,128)(2,1)S(1)}, u32[]{:S(2)}, u32[]{:S(2)}) collective-permute-start(bf16[48,1280]{1,0:T(8,128)(2,1)S(1)} %qkv_total.1.refs_5_.refs_1_), channel_id=1, source_target_pairs={{0,8},{1,9},{2,10},{3,11},{4,12},{5,13},{6,14},{7,15},{8,0},{9,1},... | collective-permute-start | bytes 368648 | tf_op jit(solution)/shard_map/qkv_back_1_0/ppermute | solution.py:127
  (52 other events, 453.6 us)
Sparse Core Ops, SparseCore 0:
  57.0 51.2 all-gather.1
  155.5 53.7 reduce-scatter.2
  232.5 33.1 reduce-scatter.4

commit v4 on v3

--- a/solution.py
+++ b/solution.py
@@ -51,8 +51,16 @@
 
 USUAL = 10
 TIMES = {
-    "attend_back": 20,
-    "first_back": 20,
+    "attend_back": 60,
+    "grad_down": 30,
+    "pack_early": 30,
+    "qkv_split": 1,
+    "pack_late": 1,
+    "wide_half_4": 1,
+    "qkv_levels": 1,
+    "wide_half_2": 1,
+    "qkv_total": 1,
+    "wide_total": 1,
 }
 
 
@@ -384,6 +392,7 @@
         ],
         grid=(pairs,),
         scratch=[pltpu.VMEM((rows, span), f32)] * 2,
+        vmem=56,
     )
 
 
@@ -392,8 +401,8 @@
 
 def middle_kernel(weights, place_ref, counts_ref, tok_ref, o_ref, cot_out_ref, cot_align_ref, vec_ref, *refs):
     arrays, refs = split_refs(refs, weights)
-    out_ref, aligned_ref, z_ref, e_ref, h_ref, g_ref, du_ref, dm_ref, dx_ref, da_ref, do_ref = refs[:11]
-    sums_ref, w_proj_ref, w_up_ref, w_down_ref, w_head_ref, sems = refs[11:]
+    out_ref, aligned_ref, z_ref, e_ref, h_ref, g_ref, du_ref, dm_ref, da_ref, do_ref = refs[:10]
+    sums_ref, w_proj_ref, w_up_ref, w_down_ref, w_head_ref, sems = refs[10:]
     step = pl.program_id(0)
     size, width = tok_ref.shape
     hidden_units = w_up_ref.shape[-1]
@@ -452,7 +461,6 @@
     t = dh2 * gain
     inner = t - jnp.mean(t, axis=-1, keepdims=True) - n2 * jnp.mean(t * n2, axis=-1, keepdims=True)
     dx1 = dx2 + inverse * inner
-    dx_ref[...] = dx1
     da = dx1.astype(bf16)
     da_ref[...] = da
     add_sum(B_PROJ, 0, da)
@@ -479,7 +487,6 @@
         (by_row(hidden), row_shape(hidden)),
         (by_row(hidden), row_shape(hidden)),
         (by_row(width), row_shape(width)),
-        (by_row(width), row_shape(width, f32)),
         (by_row(width), row_shape(width)),
         (by_row(width), row_shape(width)),
     ]
@@ -563,6 +570,74 @@
         vmem=56,
         after=after,
     )
+
+
+def outer_group_kernel(steps, place_ref, *refs):
+    count = len(steps)
+    lefts, rights, outs = refs[:count], refs[count : 2 * count], refs[2 * count : 4 * count]
+    turned, held, sems = refs[4 * count], refs[4 * count + 1 : 5 * count], refs[5 * count]
+    step = pl.program_id(0)
+    first = place_ref[CORE] == 0
+    copies = [pltpu.make_async_copy(lefts[i], held[i - 1], sems.at[i - 1]) for i in range(1, count)]
+
+    @pl.when(step == 0)
+    def _():
+        for copy in copies:
+            copy.start()
+
+    begin = 0
+    for i, length in enumerate(steps):
+        keep_ref, send_ref = outs[2 * i], outs[2 * i + 1]
+
+        @pl.when(step == begin)
+        def _():
+            if i:
+                copies[i - 1].wait()
+                turned[...] = held[i - 1][...].T
+            else:
+                turned[...] = lefts[0][...].T
+
+        @pl.when((step >= begin) & (step < begin + length))
+        def _():
+            total = dot_nn(turned[...], rights[i][...]).astype(bf16)
+            levels, _, _, columns = keep_ref.shape
+            shape = (2, HALF, columns)
+            for z in range(levels):
+                low = total[2 * z * BAND : (2 * z + 1) * BAND].reshape(shape)
+                high = total[(2 * z + 1) * BAND : (2 * z + 2) * BAND].reshape(shape)
+                level = place_ref[Z] ^ z
+                keep_ref[level] = jnp.where(first, low, high)
+                send_ref[level] = jnp.where(first, high, low)
+
+        begin += length
+
+
+def outer_group(order, pairs, columns_out, levels, name):
+    rows, m = pairs[0][0].shape
+    steps = [right.shape[1] // columns for (_, right), columns in zip(pairs, columns_out)]
+    rights, outs, begin = [], [], 0
+    for (_, right), columns, length in zip(pairs, columns_out, steps):
+
+        def at(j, begin=begin, length=length):
+            return jnp.clip(j - begin, 0, length - 1)
+
+        rights.append(pl.BlockSpec((rows, columns), lambda j, p, at=at: (0, at(j))))
+        out_spec = pl.BlockSpec((levels, 2, HALF, columns), lambda j, p, at=at: (0, 0, 0, at(j)))
+        outs += [(out_spec, shape_of((levels, 2, HALF, right.shape[1])))] * 2
+        begin += length
+    results = order(
+        functools.partial(outer_group_kernel, steps),
+        name,
+        [left for left, _ in pairs] + [right for _, right in pairs],
+        [whole((rows, m))] + [ANY] * (len(pairs) - 1) + rights,
+        outs,
+        grid=(sum(steps),),
+        scratch=[pltpu.VMEM((m, rows), bf16)]
+        + [pltpu.VMEM((rows, m), bf16)] * (len(pairs) - 1)
+        + [pltpu.SemaphoreType.DMA((len(pairs) - 1,))],
+        vmem=56,
+    )
+    return [results[2 * i : 2 * i + 2] for i in range(len(pairs))]
 
 
 def split_kernel(sets, place_ref, *refs):
@@ -588,12 +663,19 @@
     levels = pairs[0][0].shape[0]
     total = sum(keep.shape[3] for keep, _ in pairs)
     shape = (levels, HALF, total // 2)
+    if len(pairs) == 1:
+        ins, out, grid, vmem = [VMEM] * 2, VMEM, (), 32
+    else:
+        ins = [pl.BlockSpec((1,) + keep.shape[1:], lambda k, p: (k, 0, 0, 0)) for keep, _ in pairs for _ in range(2)]
+        out, grid, vmem = pl.BlockSpec((1,) + shape[1:], lambda k, p: (k, 0, 0)), (levels,), 56
     return order(
         functools.partial(split_kernel, sets),
         name,
         [array for pair in pairs for array in pair],
-        [VMEM] * (2 * len(pairs)),
-        [(VMEM, shape_of(shape))] * 4,
+        ins,
+        [(out, shape_of(shape))] * 4,
+        grid=grid,
+        vmem=vmem,
     )
 
 
@@ -606,7 +688,10 @@
             total = total + ref[level].astype(f32)
         out_ref[:, :columns] = total.astype(bf16)
         if lines:
-            out_ref[0:FEW, columns:] = lines[0][level] + lines[1][level]
+            total = lines[0][level].astype(f32)
+            for ref in lines[1:]:
+                total = total + ref[level].astype(f32)
+            out_ref[0:FEW, columns:] = total.astype(bf16)
             out_ref[FEW:, columns:] = jnp.zeros((HALF - FEW, TILE), bf16)
 
 
@@ -620,6 +705,23 @@
         [VMEM] * (4 + len(lines)),
         [(VMEM, shape_of((height, columns)))] * levels,
     )
+
+
+def halves_kernel(place_ref, *refs):
+    ins, outs = refs[:-2], refs[-2:]
+    half = ins[0].shape[0] // 2
+    for out, out_ref in enumerate(outs):
+        part = slice(out * half, (out + 1) * half)
+        total = ins[0][part].astype(f32)
+        for ref in ins[1:]:
+            total = total + ref[part].astype(f32)
+        out_ref[...] = total.astype(bf16).reshape(out_ref.shape)
+
+
+def by_half(order, arrays, name):
+    levels, height, columns = arrays[0].shape
+    shape = (height, columns) if levels == 2 else (levels // 2, height, columns)
+    return order(halves_kernel, name, arrays, [VMEM] * len(arrays), [(VMEM, shape_of(shape))] * 2)
 
 
 def add_kernel(parts, place_ref, *refs):
@@ -663,8 +765,8 @@
                     outs[number][y, :, across * half : (across + 1) * half] = ref[:, at : at + half].astype(f32)
                     at += half
 
-    at = sum(members) // 2
     if beside:
+        at = sum(members) // 2 + (TILE if lengths else 0)
         out_ref = outs[len(members)]
         width = out_ref.shape[3]
         for quarter, ref in enumerate(quarters):
@@ -674,11 +776,12 @@
                 out_ref[owner, band] = ref[:, columns].astype(f32)
 
     if lengths:
+        at = sum(members) // 2
         lines = quarters[0][0:FEW, at : at + TILE].astype(f32)
         for ref in quarters[1:]:
             lines = lines + ref[0:FEW, at : at + TILE].astype(f32)
         line = 0
-        for part, out_ref in zip(lengths, outs[len(members) :]):
+        for part, out_ref in zip(lengths, outs[len(members) + (1 if beside else 0) :]):
             rows = []
             for length in part:
                 pieces = []
@@ -729,6 +832,13 @@
         self.parts = [parts[0]]
         self.parts += [swap(part, self.name + "_column", fsdp=2 * level) for level, part in enumerate(parts) if level]
 
+    def halve(self):
+        arrays = self.quarters
+        levels = arrays[0].shape[0]
+        near, far = by_half(self.order, arrays, f"{self.name}_half_{levels}")
+        self.quarters = [near, swap(far, self.name + "_column", fsdp=levels)]
+        self.parts = self.quarters
+
     def total(self, beside=()):
         near = add_up(self.order, self.parts, beside, self.name + "_total")
         self.near = [near] + [swap(near, self.name + "_back", dp=j) for j in (1, 2, 3)]
@@ -742,14 +852,17 @@
     return -(-length // TILE)
 
 
-def pack_kernel(lengths, place_ref, sums_ref, first_ref, qv_ref, keep_ref, send_ref):
+def pack_kernel(lengths, members, place_ref, *refs):
+    arrays, (keep_ref, send_ref) = refs[:-2], refs[-2:]
     levels = keep_ref.shape[0]
     first = place_ref[CORE] == 0
-    late = {GAIN_ONE: (first_ref, 0), SHIFT_ONE: (first_ref, 1), B_Q: (qv_ref, 0), B_V: (qv_ref, 1)}
     values = []
     for index, length in enumerate(lengths):
-        ref, line = late.get(index, (sums_ref, index))
-        values.append(ref[line : line + 1, : 2 * levels * length])
+        if index in members:
+            array, line = members[index]
+            values.append(arrays[array][line : line + 1, : 2 * levels * length])
+        else:
+            values.append(jnp.zeros((1, 2 * levels * length), f32))
 
     def lines(shard):
         rows = []
@@ -767,14 +880,15 @@
         send_ref[level] = jnp.where(first, high, low).astype(bf16)
 
 
-def pack_vectors(order, sums, lengths, levels):
+def pack_vectors(order, arrays, members, lengths, levels, name, after=()):
     shape = (levels, FEW, TILE)
     return order(
-        functools.partial(pack_kernel, lengths),
-        "pack_vectors",
-        sums,
-        [VMEM] * len(sums),
+        functools.partial(pack_kernel, lengths, members),
+        name,
+        arrays,
+        [VMEM] * len(arrays),
         [(VMEM, shape_of(shape))] * 2,
+        after=after,
     )
 
 
@@ -933,10 +1047,10 @@
     sums_ref[1:2, :] += jnp.sum(dh, axis=0, keepdims=True)
     t = dh * row(vec_ref, GAIN_ONE, width)
     inner = t - jnp.mean(t, axis=-1, keepdims=True) - n1 * jnp.mean(t * n1, axis=-1, keepdims=True)
-    out_ref[...] = (dx_ref[...] + inverse * inner).astype(bf16)
-
-
-def first_back(order, tokens, dx1, dqkv, weight, vectors, after):
+    out_ref[...] = (dx_ref[...].astype(f32) + inverse * inner).astype(bf16)
+
+
+def first_back(order, tokens, dx1, dqkv, weight, vectors):
     rows, width = tokens.shape
     size = row_tile(rows, 320)
     rowwise = pl.BlockSpec((size, width), lambda i, p: (i, 0))
@@ -948,7 +1062,6 @@
         + [ANY] * len(weight.arrays),
         [(rowwise, shape_of((rows, width))), (out_whole((2, width)), shape_of((2, width), f32))],
         grid=(rows // size,),
-        after=after,
         scratch=weight_scratch([weight]),
         vmem=56,
     )
@@ -999,20 +1112,18 @@
         wide = [w_up, w_head, w_proj]
         p_qkv, p_wide = start_gather(order, own_vectors, lengths, [[w_qkv], wide])
         got = [p_qkv] + [swap(p_qkv, "qkv_column", fsdp=2 * level) for level in range(1, levels)]
-        got_wide = [swap(p_wide, "wide_column", fsdp=2 * level) for level in range(2, levels)]
+        got_wide = [p_wide] + [swap(p_wide, "wide_column", fsdp=2 * level) for level in range(1, levels)]
         bias = make_masks(order, clip_counts, rows)
         near, lines = near_levels(order, got, True, "qkv_near")
         quarters = across_plane(near, "qkv")
         other_lines = swap(lines, "vectors_core", fsdp=1)
         own = assemble(order, [w_qkv], quarters, "qkv_assemble")
         full_qkv = Weight([own, swap(own, "qkv_core", fsdp=1)], 0, (width, w_qkv.shape[1]))
-        later, own = lax.optimization_barrier((p_wide, own))
-        got_wide = [p_wide, swap(later, "wide_column", fsdp=2)] + got_wide
+        later, own = lax.optimization_barrier((w_down, own))
+        full_down = gather(later)
         vectors = unpack_vectors(order, lines, other_lines, lengths)
         (near,) = near_levels(order, got_wide, False, "wide_near")
         quarters = across_plane(near, "wide")
-        later, near = lax.optimization_barrier((w_down, near))
-        full_down = gather(later)
     else:
         pieces = [piece for v in own_vectors for piece in ([v[0], v[1]] if v.ndim == 2 else [v])]
         joined = gather(jnp.concatenate(pieces)[None])
@@ -1037,7 +1148,7 @@
         full_up, full_head, full_proj = (
             Weight(both_cores, column, (width, w.shape[1])) for column, w in zip(at, wide)
         )
-    block_out, aligned, z, e_al, h2, g, du, dm, dx1, da, do, sums = middle(
+    block_out, aligned, z, e_al, h2, g, du, dm, da, do, sums = middle(
         order,
         clip_counts,
         tokens,
@@ -1047,33 +1158,38 @@
         (full_proj, full_up, full_down, full_head),
         vectors,
     )
+    if paired:
+        r_wide = Reduction(order, "wide")
+        pairs = outer_group(order, [(h2, du), (z, e_al), (o, da)], [768, 512, 768], levels, "grad_wide")
+        for pair, w in zip(pairs, wide):
+            r_wide.add(*pair, [w.shape[1]])
     d_down = scatter(outer(order, g, dm, 512, 768, "grad_down"))
     if paired:
-        r_wide = Reduction(order, "wide")
-        pair = outer_split(order, h2, du, levels, 768, w_up.shape[1], 0, (), "grad_up")
-        r_wide.add(*pair, [w_up.shape[1]])
-        members = [w_head.shape[1], w_proj.shape[1]]
-        pair = outer_split(order, z, e_al, levels, 512, sum(members), 0, (), "grad_head")
-        pair = outer_split(order, o, da, levels, 256, sum(members), members[0], pair, "grad_proj")
-        r_wide.add(*pair, members)
         r_wide.split()
     dqkv, s_qv = attend_back(order, bias, q, k, v, o, do, lse)
     if paired:
         r_qkv = Reduction(order, "qkv")
         n = w_qkv.shape[1]
         r_qkv.add(*outer_split(order, h1, dqkv, levels, width, n, 0, (), "grad_qkv"), [n])
-    grad_tokens, s_first = first_back(order, tokens, dx1, dqkv, full_qkv, vectors, [d_down])
+        early = {B_Q: (1, 0), B_V: (1, 1)}
+        early.update({i: (0, i) for i in range(B_PROJ, B_HEAD + 1)})
+        keep, send = pack_vectors(order, [sums, s_qv], early, lengths, levels, "pack_early")
+        lines = [keep, swap(send, "vectors_core", fsdp=1)]
+        r_qkv.split()
+        r_wide.halve()
+    grad_tokens, s_first = first_back(order, tokens, da, dqkv, full_qkv, vectors)
     if paired:
+        late = {GAIN_ONE: (0, 0), SHIFT_ONE: (0, 1)}
+        keep, send = pack_vectors(order, [s_first], late, lengths, levels, "pack_late", [d_down])
+        lines += [keep, swap(send, "vectors_core", fsdp=1)]
         d_down = lax.psum_scatter(d_down, "dp", scatter_dimension=0, tiled=True)
-        r_qkv.split()
-        lines, send = pack_vectors(order, [sums, s_first, s_qv], lengths, levels)
-        lines = [lines, swap(send, "vectors_core", fsdp=1)]
-        r_wide.levels()
         r_qkv.levels(lines)
-        r_wide.total([d_down])
-        r_qkv.total()
-        d_up, d_head, d_proj, d_down = r_wide.join(beside=w_down.shape)
-        d_qkv, *mine = r_qkv.join(lengths=parts)
+        while r_wide.quarters[0].ndim == 3:
+            r_wide.halve()
+        r_qkv.total([d_down])
+        r_wide.total()
+        d_qkv, d_down, *mine = r_qkv.join(lengths=parts, beside=w_down.shape)
+        d_up, d_head, d_proj = r_wide.join()
     else:
 
         def reduce(value):

time: 303 us -> 283 us (0.934)
  waiting for transfers between devices: 91.1 us -> 71.9 us
    ppermute x37 -> x38, waiting for transfers between devices: 79.8 us -> 69.1 us  [swap(): return lax.ppermute(value, ('dp', 'fsdp'), pairs)]
    all_gather x1, waiting for transfers between devices: 7.96 us -> 2.69 us  [gather(): return lax.all_gather(value, 'fsdp', axis=0, tiled=True)]
    reduce_scatter x1, waiting for transfers between devices: 3.36 us -> 0.01 us  [local(): d_down = lax.psum_scatter(d_down, 'dp', scatter_dimension=0, tiled=True)]
    unnamed x88 -> x70, local copies, waits for them, and re-layouts: 13.3 us -> 10.9 us
    ppermute x37 -> x38, starting transfers between devices: 37.6 us -> 38.2 us  [swap(): return lax.ppermute(value, ('dp', 'fsdp'), pairs)]
  transfers between devices with their start and end apart: 40 -> 41, of which waited for: 17 -> 18; matrix products, arithmetic and copies ran while one was open for 0% -> 0% of each run, Pallas kernels for 31% -> 31%
where the time goes in v4:
time: 283 us; the launch traced here: 281 us
  Pallas kernels  145 us (51%)
  waiting for transfers between devices  71.9 us (25%)
  starting transfers between devices  38.3 us (14%)
  between operations  14.4 us (5%)
  local copies, waits for them, and re-layouts  11.5 us (4%)
    pallas_call x26, Pallas kernels, __call__(): pl.pallas_call(body, grid_spec=pltpu.PrefetchScalarGridSpec(num_scalar_pr...  145 us
    ppermute x38, waiting for transfers between devices, swap(): return lax.ppermute(value, ('dp', 'fsdp'), pairs)  69.1 us
    ppermute x38, starting transfers between devices, swap(): return lax.ppermute(value, ('dp', 'fsdp'), pairs)  38.2 us
    unnamed x70, local copies, waits for them, and re-layouts  10.9 us
  transfers between devices with their start and end apart: 41, of which 18 were waited for; matrix products, arithmetic and copies ran while one was open for 0% of the time, Pallas kernels for 31%

profile of v4, /device:TPU:0, one launch (start us, length us, event | category | flops | bytes accessed | tf_op | source)
XLA Modules:
  0.0 281.2 jit_solution(6745688471595934362)
XLA Ops:
  7.9 2.6 quarters.1
  10.5 5.0 %collective-permute-start.2 = (bf16[48,1280]{1,0:T(8,128)(2,1)}, bf16[48,1280]{1,0:T(8,128)(2,1)S(1)}, u32[]{:S(2)}, u32[]{:S(2)}) collective-permute-start(bf16[48,1280]{1,0:T(8,128)(2,1)} %get-tuple-element.85.refs_2_.refs_1_), channel_id=1, source_target_pairs={{0,6},{1,7},{2,4},{3,5},{4,2},{5,3},{6,0},{7,1},{8,14},{9,15},{10,... | collective-permute-start | bytes 368648 | tf_op jit(solution)/shard_map/qkv_column_0_6/ppermute | solution.py:135
  17.1 3.2 %masks.1.refs_5_.refs_1_ = f32[3072,128]{1,0:T(8,128)S(1)} custom-call(s32[5]{0:T(128)S(1)} %copy-done.7, s32[32,32]{1,0:T(8,128)S(1)} %copy-done.6, bf16[48,1280]{1,0:T(8,128)(2,1)S(1)} %copy-done.19), custom_call_target="tpu_custom_call" | custom-call | flops 10000000000 | bytes 1 | tf_op jit(solution)/shard_map/masks/pallas_call | solution.py:103
  20.4 5.8 %collective-permute-done.1.refs_3_ = bf16[48,1280]{1,0:T(8,128)(2,1)S(1)} collective-permute-done((bf16[48,1280]{1,0:T(8,128)(2,1)}, bf16[48,1280]{1,0:T(8,128)(2,1)S(1)}, u32[]{:S(2)}, u32[]{:S(2)}) %collective-permute-start.1) | collective-permute-done | bytes 122912 | tf_op jit(solution)/shard_map/qkv_column_0_4/ppermute | solution.py:135
  26.7 2.5 collective-permute-start.6
  30.3 2.5 collective-permute-start.10
  32.8 5.7 %collective-permute-done.6.refs_5_ = bf16[3,48,1152]{2,1,0:T(8,128)(2,1)S(1)} collective-permute-done((bf16[3,48,1152]{2,1,0:T(8,128)(2,1)S(1)}, bf16[3,48,1152]{2,1,0:T(8,128)(2,1)S(1)}, u32[]{:S(2)}, u32[]{:S(2)}) %collective-permute-start.6) | collective-permute-done | bytes 331808 | tf_op jit(solution)/shard_map/qkv_plane_3_0/ppermute | solution.py:135
  38.5 5.2 %collective-permute-done.5.refs_4_ = bf16[3,48,1152]{2,1,0:T(8,128)(2,1)S(1)} collective-permute-done((bf16[3,48,1152]{2,1,0:T(8,128)(2,1)S(1)}, bf16[3,48,1152]{2,1,0:T(8,128)(2,1)S(1)}, u32[]{:S(2)}, u32[]{:S(2)}) %collective-permute-start.5) | collective-permute-done | bytes 331808 | tf_op jit(solution)/shard_map/qkv_plane_2_0/ppermute | solution.py:135
  45.7 5.1 %collective-permute-done.9.refs_3_ = bf16[48,2432]{1,0:T(8,128)(2,1)} collective-permute-done((bf16[48,2432]{1,0:T(8,128)(2,1)}, bf16[48,2432]{1,0:T(8,128)(2,1)}, u32[]{:S(2)}, u32[]{:S(2)}) %collective-permute-start.9) | collective-permute-done | bytes 233504 | tf_op jit(solution)/shard_map/wide_column_0_4/ppermute | solution.py:135
  50.8 2.0 wide_near.1.refs_5_.refs_4_
  52.8 2.5 collective-permute-start.13
  56.4 6.9 %norm_qkv.1 = (bf16[960,768]{1,0:T(8,128)(2,1)S(1)}, bf16[960,768]{1,0:T(8,128)(2,1)S(1)}, bf16[960,768]{1,0:T(8,128)(2,1)S(1)}, bf16[960,768]{1,0:T(8,128)(2,1)S(1)}) custom-call(s32[5]{0:T(128)S(1)} %copy-done.7, bf16[960,768]{1,0:T(8,128)(2,1)S(1)} %copy-done.1, bf16[16,3072]{1,0:T(8,128)(2,1)S(1)} %unpack_vectors.1.refs_5_.refs_2_.refs_6_.refs_4_, ...), custom_call_target="tpu_custom_call" | custom-call | flops 10000000000 | bytes 1 | tf_op jit(solution)/shard_map/norm_qkv/pallas_call | solution.py:103
  63.4 10.0 %attend.1 = (bf16[960,768]{1,0:T(8,128)(2,1)S(1)}, f32[6,8,256]{2,1,0:T(8,128)S(1)}) custom-call(s32[5]{0:T(128)S(1)} %copy-done.7, f32[3072,128]{1,0:T(8,128)S(1)} %copy-done.27, bf16[960,768]{1,0:T(8,128)(2,1)S(1)} %get-tuple-element.89.refs_2_, bf16[960,768]{1,0:T(8,128)(2,1)S(1)} %get-tuple-element.90.refs_3_, ...), custom_call_target="tpu_custom_call" | custom-call | flops 10000000000 | bytes 1 | tf_op jit(solution)/shard_map/attend/pallas_call | solution.py:103
  73.5 10.5 %collective-permute-done.12.refs_6_ = bf16[3,48,2432]{2,1,0:T(8,128)(2,1)S(1)} collective-permute-done((bf16[3,48,2432]{2,1,0:T(8,128)(2,1)S(1)}, bf16[3,48,2432]{2,1,0:T(8,128)(2,1)S(1)}, u32[]{:S(2)}, u32[]{:S(2)}) %collective-permute-start.12) | collective-permute-done | bytes 700448 | tf_op jit(solution)/shard_map/wide_plane_2_0/ppermute | solution.py:135
  86.8 6.6 %collective-permute-done.14.refs_8_.refs_10_.refs_13_ = bf16[4,96,4864]{2,1,0:T(8,128)(2,1)} collective-permute-done((bf16[4,96,4864]{2,1,0:T(8,128)(2,1)S(1)}, bf16[4,96,4864]{2,1,0:T(8,128)(2,1)}, u32[]{:S(2)}, u32[]{:S(2)}) %collective-permute-start.14) | collective-permute-done | bytes 3735584 | tf_op jit(solution)/shard_map/wide_core_0_1/ppermute | solution.py:135
  93.4 2.7 all-gather.2.cloned.1.call-done.refs_11_
  96.1 36.4 %middle.1 = (bf16[960,768]{1,0:T(8,128)(2,1)}, bf16[960,1024]{1,0:T(8,128)(2,1)}, bf16[960,768]{1,0:T(8,128)(2,1)}, bf16[960,1024]{1,0:T(8,128)(2,1)}, bf16[960,...) custom-call(s32[5]{0:T(128)} %stack.23.refs_0_, ...), custom_call_target="tpu_custom_call" | custom-call | flops 10000000000 | bytes 1 | tf_op jit(solution)/shard_map/middle/pallas_call | solution.py:103
  132.5 16.3 %grad_wide.1 = (bf16[4,2,48,3072]{3,2,1,0:T(8,128)(2,1)}, bf16[4,2,48,3072]{3,2,1,0:T(8,128)(2,1)}, bf16[4,2,48,1024]{3,2,1,0:T(8,128)(2,1)}, bf16[4,2,48,1024]{...) custom-call(s32[5]{0:T(128)} %stack.23.refs_0_, ...), custom_call_target="tpu_custom_call" | custom-call | flops 10000000000 | bytes 1 | tf_op jit(solution)/shard_map/grad_wide/pallas_call | solution.py:103
  149.7 10.5 %grad_down.1.refs_7_ = bf16[3072,768]{1,0:T(8,128)(2,1)} custom-call(s32[5]{0:T(128)} %stack.23.refs_0_, bf16[960,3072]{1,0:T(8,128)(2,1)} %get-tuple-element.110.refs_1_, bf16[960,768]{1,0:T(8,128)(2,1)} %get-tuple-element.111.refs_2_, bf16[4,2,48,3072]{3,2,1,0:T(8,128)(2,1)} %get-tuple-element.104.refs_3_.refs_1_), custom_call_target="tpu_custom_call" | custom-call | flops 30000001024 | bytes 1 | tf_op jit(solution)/shard_map/grad_down/pallas_call | solution.py:103
  161.9 6.1 %wide_split.1 = (bf16[4,48,2432]{2,1,0:T(8,128)(2,1)}, bf16[4,48,2432]{2,1,0:T(8,128)(2,1)}, bf16[4,48,2432]{2,1,0:T(8,128)(2,1)}, bf16[4,48,2432]{2,1,0:T(8,128)(2,1)}) custom-call(s32[5]{0:T(128)} %stack.23.refs_0_, bf16[4,2,48,3072]{3,2,1,0:T(8,128)(2,1)} %get-tuple-element.104.refs_3_.refs_1_, bf16[4,2,48,3072]{3,2,1,0:T(8,128)(2,1)} %copy-done.33, ...), custom_call_target="tpu_custom_call" | custom-call | flops 10000000000 | bytes 1 | tf_op jit(solution)/shard_map/wide_split/pallas_call | solution.py:103
  171.5 17.2 %attend_back.1 = (bf16[3,960,768]{2,1,0:T(8,128)(2,1)}, f32[2,768]{1,0:T(2,128)}) custom-call(s32[5]{0:T(128)} %stack.23.refs_0_, f32[3072,128]{1,0:T(8,128)} %copy-done.26, bf16[960,768]{1,0:T(8,128)(2,1)} %copy-done.28, bf16[960,768]{1,0:T(8,128)(2,1)} %copy-done.29, bf16[960,768]{1,0:T(8,128)(2,1)} %copy-done.30, bf16[960,768]{1,0:T(8,128)(2,1)} %copy-done.2, ...), custom_call_target="tpu_custom_call" | custom-call | flops 60000002048 | bytes 1 | tf_op jit(solution)/shard_map/attend_back/pallas_call | solution.py:103
  188.8 8.9 %grad_qkv.1 = (bf16[4,2,48,2304]{3,2,1,0:T(8,128)(2,1)}, bf16[4,2,48,2304]{3,2,1,0:T(8,128)(2,1)}) custom-call(s32[5]{0:T(128)} %stack.23.refs_0_, bf16[960,768]{1,0:T(8,128)(2,1)} %copy-done.25, bf16[3,960,768]{2,1,0:T(8,128)(2,1)} %get-tuple-element.113.refs_2_.refs_3_, bf16[3,960,768]{2,1,0:T(8,128)(2,1)} %get-tuple-element.113.refs_2_.refs_3_), custom_call_target="tpu_custom_call" | custom-call | flops 10000000000 | bytes 1 | tf_op jit(solution)/shard_map/grad_qkv/pallas_call | solution.py:103
  206.4 6.1 %collective-permute-done.19.refs_3_ = bf16[4,48,2432]{2,1,0:T(8,128)(2,1)S(1)} collective-permute-done((bf16[4,48,2432]{2,1,0:T(8,128)(2,1)}, bf16[4,48,2432]{2,1,0:T(8,128)(2,1)S(1)}, u32[]{:S(2)}, u32[]{:S(2)}) %collective-permute-start.19) | collective-permute-done | bytes 933920 | tf_op jit(solution)/shard_map/wide_plane_2_0/ppermute | solution.py:135
  216.8 10.7 %first_back.1 = (bf16[960,768]{1,0:T(8,128)(2,1)}, f32[2,768]{1,0:T(2,128)}) custom-call(s32[5]{0:T(128)} %stack.23.refs_0_, bf16[960,768]{1,0:T(8,128)(2,1)} %refs_1_.13, bf16[960,768]{1,0:T(8,128)(2,1)} %get-tuple-element.97.refs_6_.refs_2_, bf16[3,960,768]{2,1,0:T(8,128)(2,1)} %get-tuple-element.113.refs_2_.refs_3_, bf16[16,3072]{1,0:T(8,128)(2,1)} %copy-done.5, ...), custom_call_target="tpu_custom_call" | custom-call | flops 10000000000 | bytes 1 | tf_op jit(solution)/shard_map/first_back/pallas_call | solution.py:103
  230.4 3.8 %collective-permute-done.24.refs_4_ = bf16[4,48,1152]{2,1,0:T(8,128)(2,1)} collective-permute-done((bf16[4,48,1152]{2,1,0:T(8,128)(2,1)S(1)}, bf16[4,48,1152]{2,1,0:T(8,128)(2,1)}, u32[]{:S(2)}, u32[]{:S(2)}) %collective-permute-start.24) | collective-permute-done | bytes 442400 | tf_op jit(solution)/shard_map/qkv_plane_3_0/ppermute | solution.py:135
  237.3 3.2 %collective-permute-start.29 = (bf16[48,1280]{1,0:T(8,128)(2,1)S(1)}, bf16[48,1280]{1,0:T(8,128)(2,1)S(1)}, u32[]{:S(2)}, u32[]{:S(2)}) collective-permute-start(bf16[48,1280]{1,0:T(8,128)(2,1)S(1)} %get-tuple-element.135), channel_id=1, source_target_pairs={{0,6},{1,7},{2,4},{3,5},{4,2},{5,3},{6,0},{7,1},{8,14},{9,15},{10,... | collective-permute-start | bytes 368648 | tf_op jit(solution)/shard_map/qkv_column_0_6/ppermute | solution.py:135
  242.2 5.9 %collective-permute-done.28.refs_3_ = bf16[48,1280]{1,0:T(8,128)(2,1)S(1)} collective-permute-done((bf16[48,1280]{1,0:T(8,128)(2,1)S(1)}, bf16[48,1280]{1,0:T(8,128)(2,1)S(1)}, u32[]{:S(2)}, u32[]{:S(2)}) %collective-permute-start.28) | collective-permute-done | bytes 122912 | tf_op jit(solution)/shard_map/qkv_column_0_4/ppermute | solution.py:135
  256.5 3.7 %collective-permute-done.33.refs_4_ = bf16[48,2816]{1,0:T(8,128)(2,1)S(1)} collective-permute-done((bf16[48,2816]{1,0:T(8,128)(2,1)S(1)}, bf16[48,2816]{1,0:T(8,128)(2,1)S(1)}, u32[]{:S(2)}, u32[]{:S(2)}) %collective-permute-start.33) | collective-permute-done | bytes 270368 | tf_op jit(solution)/shard_map/qkv_back_3_0/ppermute | solution.py:135
  261.3 4.7 %collective-permute-done.32.refs_3_ = bf16[48,2816]{1,0:T(8,128)(2,1)S(1)} collective-permute-done((bf16[48,2816]{1,0:T(8,128)(2,1)S(1)}, bf16[48,2816]{1,0:T(8,128)(2,1)S(1)}, u32[]{:S(2)}, u32[]{:S(2)}) %collective-permute-start.32) | collective-permute-done | bytes 270368 | tf_op jit(solution)/shard_map/qkv_back_2_0/ppermute | solution.py:135
  266.0 2.0 qkv_join.1
  269.3 2.3 collective-permute-done.36.refs_3_
  272.8 1.9 wide_join.1
  (150 shorter events, 48.3 us)
Async XLA Ops:
  7.2 88.9 %all-gather.2.cloned.1.call-start = ((), (), s32[]{:S(2)}) async-start(), calls=%async_computation.2 | async-start | bytes 5308416 | tf_op jit(solution)/shard_map/all_gather | solution.py:1106
  26.7 11.7 %collective-permute-start.6 = (bf16[3,48,1152]{2,1,0:T(8,128)(2,1)S(1)}, bf16[3,48,1152]{2,1,0:T(8,128)(2,1)S(1)}, u32[]{:S(2)}, u32[]{:S(2)}) collective-permute-start(bf16[3,48,1152]{2,1,0:T(8,128)(2,1)S(1)} %get-tuple-element.87.refs_2_.refs_6_), channel_id=1, source_target_pairs={{0,24},{1,25},{2,26},{3,27},{4,28},{5,29},{6,30},{7,31},{8,16},{9,... | collective-permute-start | bytes 995336 | tf_op jit(solution)/shard_map/qkv_plane_3_0/ppermute | solution.py:135
  29.3 14.4 %collective-permute-start.5 = (bf16[3,48,1152]{2,1,0:T(8,128)(2,1)S(1)}, bf16[3,48,1152]{2,1,0:T(8,128)(2,1)S(1)}, u32[]{:S(2)}, u32[]{:S(2)}) collective-permute-start(bf16[3,48,1152]{2,1,0:T(8,128)(2,1)S(1)} %get-tuple-element.87.refs_2_.refs_6_), channel_id=1, source_target_pairs={{0,16},{1,17},{2,18},{3,19},{4,20},{5,21},{6,22},{7,23},{8,24},{9,... | collective-permute-start | bytes 995336 | tf_op jit(solution)/shard_map/qkv_plane_2_0/ppermute | solution.py:135
  29.8 14.0 %collective-permute-start.4 = (bf16[3,48,1152]{2,1,0:T(8,128)(2,1)S(1)}, bf16[3,48,1152]{2,1,0:T(8,128)(2,1)S(1)}, u32[]{:S(2)}, u32[]{:S(2)}) collective-permute-start(bf16[3,48,1152]{2,1,0:T(8,128)(2,1)S(1)} %get-tuple-element.87.refs_2_.refs_6_), channel_id=1, source_target_pairs={{0,8},{1,9},{2,10},{3,11},{4,12},{5,13},{6,14},{7,15},{8,0},{9,1},... | collective-permute-start | bytes 995336 | tf_op jit(solution)/shard_map/qkv_plane_1_0/ppermute | solution.py:135
  30.3 15.4 %collective-permute-start.10 = (bf16[48,2432]{1,0:T(8,128)(2,1)}, bf16[48,2432]{1,0:T(8,128)(2,1)}, u32[]{:S(2)}, u32[]{:S(2)}) collective-permute-start(bf16[48,2432]{1,0:T(8,128)(2,1)} %get-tuple-element.88.refs_1_), channel_id=1, source_target_pairs={{0,6},{1,7},{2,4},{3,5},{4,2},{5,3},{6,0},{7,1},{8,14},{9,15},{10,... | collective-permute-start | bytes 700424 | tf_op jit(solution)/shard_map/wide_column_0_6/ppermute | solution.py:135
  32.8 18.1 %collective-permute-start.9 = (bf16[48,2432]{1,0:T(8,128)(2,1)}, bf16[48,2432]{1,0:T(8,128)(2,1)}, u32[]{:S(2)}, u32[]{:S(2)}) collective-permute-start(bf16[48,2432]{1,0:T(8,128)(2,1)} %get-tuple-element.88.refs_1_), channel_id=1, source_target_pairs={{0,4},{1,5},{2,6},{3,7},{4,0},{5,1},{6,2},{7,3},{8,12},{9,13},{10,... | collective-permute-start | bytes 700424 | tf_op jit(solution)/shard_map/wide_column_0_4/ppermute | solution.py:135
  38.5 12.3 %collective-permute-start.8 = (bf16[48,2432]{1,0:T(8,128)(2,1)}, bf16[48,2432]{1,0:T(8,128)(2,1)}, u32[]{:S(2)}, u32[]{:S(2)}) collective-permute-start(bf16[48,2432]{1,0:T(8,128)(2,1)} %get-tuple-element.88.refs_1_), channel_id=1, source_target_pairs={{0,2},{1,3},{2,0},{3,1},{4,6},{5,7},{6,4},{7,5},{8,10},{9,11},{10,... | collective-permute-start | bytes 700424 | tf_op jit(solution)/shard_map/wide_column_0_2/ppermute | solution.py:135
  44.5 11.9 %collective-permute-start.7 = (bf16[4,96,2304]{2,1,0:T(8,128)(2,1)S(1)}, bf16[4,96,2304]{2,1,0:T(8,128)(2,1)}, u32[]{:S(2)}, u32[]{:S(2)}) collective-permute-start(bf16[4,96,2304]{2,1,0:T(8,128)(2,1)S(1)} %bitcast.16), channel_id=1, source_target_pairs={{0,1},{1,0},{2,3},{3,2},{4,5},{5,4},{6,7},{7,6},{8,9},{9,8},{10,11... | collective-permute-start | bytes 5308424 | tf_op jit(solution)/shard_map/qkv_core_0_1/ppermute | solution.py:135
  45.0 171.8 %reduce-scatter.3.cloned.1.call-start = ((), (), s32[]{:S(2)}) async-start(), calls=%async_computation.3 | async-start | bytes 5308416 | tf_op jit(solution)/shard_map/reduce_scatter | solution.py:1109
  52.8 20.7 %collective-permute-start.13 = (bf16[3,48,2432]{2,1,0:T(8,128)(2,1)S(1)}, bf16[3,48,2432]{2,1,0:T(8,128)(2,1)S(1)}, u32[]{:S(2)}, u32[]{:S(2)}) collective-permute-start(bf16[3,48,2432]{2,1,0:T(8,128)(2,1)S(1)} %wide_near.1.refs_5_.refs_4_), channel_id=1, source_target_pairs={{0,24},{1,25},{2,26},{3,27},{4,28},{5,29},{6,30},{7,31},{8,16},{9,... | collective-permute-start | bytes 2101256 | tf_op jit(solution)/shard_map/wide_plane_3_0/ppermute | solution.py:135
  55.3 28.6 %collective-permute-start.12 = (bf16[3,48,2432]{2,1,0:T(8,128)(2,1)S(1)}, bf16[3,48,2432]{2,1,0:T(8,128)(2,1)S(1)}, u32[]{:S(2)}, u32[]{:S(2)}) collective-permute-start(bf16[3,48,2432]{2,1,0:T(8,128)(2,1)S(1)} %wide_near.1.refs_5_.refs_4_), channel_id=1, source_target_pairs={{0,16},{1,17},{2,18},{3,19},{4,20},{5,21},{6,22},{7,23},{8,24},{9,... | collective-permute-start | bytes 2101256 | tf_op jit(solution)/shard_map/wide_plane_2_0/ppermute | solution.py:135
  55.8 28.2 %collective-permute-start.11 = (bf16[3,48,2432]{2,1,0:T(8,128)(2,1)S(1)}, bf16[3,48,2432]{2,1,0:T(8,128)(2,1)S(1)}, u32[]{:S(2)}, u32[]{:S(2)}) collective-permute-start(bf16[3,48,2432]{2,1,0:T(8,128)(2,1)S(1)} %wide_near.1.refs_5_.refs_4_), channel_id=1, source_target_pairs={{0,8},{1,9},{2,10},{3,11},{4,12},{5,13},{6,14},{7,15},{8,0},{9,1},... | collective-permute-start | bytes 2101256 | tf_op jit(solution)/shard_map/wide_plane_1_0/ppermute | solution.py:135
  148.8 11.4 %collective-permute-start.17 = (bf16[4,2,48,768]{3,2,1,0:T(8,128)(2,1)}, bf16[4,2,48,768]{3,2,1,0:T(8,128)(2,1)}, u32[]{:S(2)}, u32[]{:S(2)}) collective-permute-start(bf16[4,2,48,768]{3,2,1,0:T(8,128)(2,1)} %get-tuple-element.109), channel_id=1, source_target_pairs={{0,1},{1,0},{2,3},{3,2},{4,5},{5,4},{6,7},{7,6},{8,9},{9,8},{10,11... | collective-permute-start | bytes 1769480 | tf_op jit(solution)/shard_map/wide_core_0_1/ppermute | solution.py:135
  149.1 11.1 %collective-permute-start.16 = (bf16[4,2,48,1024]{3,2,1,0:T(8,128)(2,1)}, bf16[4,2,48,1024]{3,2,1,0:T(8,128)(2,1)S(1)}, u32[]{:S(2)}, u32[]{:S(2)}) collective-permute-start(bf16[4,2,48,1024]{3,2,1,0:T(8,128)(2,1)} %get-tuple-element.107), channel_id=1, source_target_pairs={{0,1},{1,0},{2,3},{3,2},{4,5},{5,4},{6,7},{7,6},{8,9},{9,8},{10,11... | collective-permute-start | bytes 2359304 | tf_op jit(solution)/shard_map/wide_core_0_1/ppermute | solution.py:135
  149.4 10.9 %collective-permute-start.15 = (bf16[4,2,48,3072]{3,2,1,0:T(8,128)(2,1)}, bf16[4,2,48,3072]{3,2,1,0:T(8,128)(2,1)S(1)}, u32[]{:S(2)}, u32[]{:S(2)}) collective-permute-start(bf16[4,2,48,3072]{3,2,1,0:T(8,128)(2,1)} %get-tuple-element.105), channel_id=1, source_target_pairs={{0,1},{1,0},{2,3},{3,2},{4,5},{5,4},{6,7},{7,6},{8,9},{9,8},{10,11... | collective-permute-start | bytes 7077896 | tf_op jit(solution)/shard_map/wide_core_0_1/ppermute | solution.py:135
  160.2 88.0 %reduce-scatter.5.cloned.1.call-start = ((), (), s32[]{:S(2)}) async-start(), calls=%async_computation.4 | async-start | bytes 737280 | tf_op jit(solution)/shard_map/reduce_scatter | solution.py:1185
  168.0 36.8 %collective-permute-start.18 = (bf16[4,48,2432]{2,1,0:T(8,128)(2,1)}, bf16[4,48,2432]{2,1,0:T(8,128)(2,1)S(1)}, u32[]{:S(2)}, u32[]{:S(2)}) collective-permute-start(bf16[4,48,2432]{2,1,0:T(8,128)(2,1)} %get-tuple-element.114), channel_id=1, source_target_pairs={{0,8},{1,9},{2,10},{3,11},{4,12},{5,13},{6,14},{7,15},{8,0},{9,1},... | collective-permute-start | bytes 2801672 | tf_op jit(solution)/shard_map/wide_plane_1_0/ppermute | solution.py:135
  169.6 42.9 %collective-permute-start.19 = (bf16[4,48,2432]{2,1,0:T(8,128)(2,1)}, bf16[4,48,2432]{2,1,0:T(8,128)(2,1)S(1)}, u32[]{:S(2)}, u32[]{:S(2)}) collective-permute-start(bf16[4,48,2432]{2,1,0:T(8,128)(2,1)} %get-tuple-element.115), channel_id=1, source_target_pairs={{0,16},{1,17},{2,18},{3,19},{4,20},{5,21},{6,22},{7,23},{8,24},{9,... | collective-permute-start | bytes 2801672 | tf_op jit(solution)/shard_map/wide_plane_2_0/ppermute | solution.py:135
  171.0 42.6 %collective-permute-start.20 = (bf16[4,48,2432]{2,1,0:T(8,128)(2,1)}, bf16[4,48,2432]{2,1,0:T(8,128)(2,1)S(1)}, u32[]{:S(2)}, u32[]{:S(2)}) collective-permute-start(bf16[4,48,2432]{2,1,0:T(8,128)(2,1)} %get-tuple-element.116), channel_id=1, source_target_pairs={{0,24},{1,25},{2,26},{3,27},{4,28},{5,29},{6,30},{7,31},{8,16},{9,... | collective-permute-start | bytes 2801672 | tf_op jit(solution)/shard_map/wide_plane_3_0/ppermute | solution.py:135
  199.8 30.5 %collective-permute-start.25 = (bf16[4,16,128]{2,1,0:T(8,128)(2,1)S(1)}, bf16[4,16,128]{2,1,0:T(8,128)(2,1)S(1)}, u32[]{:S(2)}, u32[]{:S(2)}) collective-permute-start(bf16[4,16,128]{2,1,0:T(8,128)(2,1)S(1)} %get-tuple-element.128), channel_id=1, source_target_pairs={{0,1},{1,0},{2,3},{3,2},{4,5},{5,4},{6,7},{7,6},{8,9},{9,8},{10,11... | collective-permute-start | bytes 49160 | tf_op jit(solution)/shard_map/vectors_core_0_1/ppermute | solution.py:135
  203.4 27.0 %collective-permute-start.22 = (bf16[4,48,1152]{2,1,0:T(8,128)(2,1)}, bf16[4,48,1152]{2,1,0:T(8,128)(2,1)S(1)}, u32[]{:S(2)}, u32[]{:S(2)}) collective-permute-start(bf16[4,48,1152]{2,1,0:T(8,128)(2,1)} %get-tuple-element.125), channel_id=1, source_target_pairs={{0,8},{1,9},{2,10},{3,11},{4,12},{5,13},{6,14},{7,15},{8,0},{9,1},... | collective-permute-start | bytes 1327112 | tf_op jit(solution)/shard_map/qkv_plane_1_0/ppermute | solution.py:135
  204.8 25.6 %collective-permute-start.23 = (bf16[4,48,1152]{2,1,0:T(8,128)(2,1)}, bf16[4,48,1152]{2,1,0:T(8,128)(2,1)S(1)}, u32[]{:S(2)}, u32[]{:S(2)}) collective-permute-start(bf16[4,48,1152]{2,1,0:T(8,128)(2,1)} %get-tuple-element.126), channel_id=1, source_target_pairs={{0,16},{1,17},{2,18},{3,19},{4,20},{5,21},{6,22},{7,23},{8,24},{9,... | collective-permute-start | bytes 1327112 | tf_op jit(solution)/shard_map/qkv_plane_2_0/ppermute | solution.py:135
  212.4 21.8 %collective-permute-start.24 = (bf16[4,48,1152]{2,1,0:T(8,128)(2,1)S(1)}, bf16[4,48,1152]{2,1,0:T(8,128)(2,1)}, u32[]{:S(2)}, u32[]{:S(2)}) collective-permute-start(bf16[4,48,1152]{2,1,0:T(8,128)(2,1)S(1)} %get-tuple-element.127), channel_id=1, source_target_pairs={{0,24},{1,25},{2,26},{3,27},{4,28},{5,29},{6,30},{7,31},{8,16},{9,... | collective-permute-start | bytes 1327112 | tf_op jit(solution)/shard_map/qkv_plane_3_0/ppermute | solution.py:135
  215.4 25.1 %collective-permute-start.30 = (bf16[2,48,2432]{2,1,0:T(8,128)(2,1)S(1)}, bf16[2,48,2432]{2,1,0:T(8,128)(2,1)S(1)}, u32[]{:S(2)}, u32[]{:S(2)}) collective-permute-start(bf16[2,48,2432]{2,1,0:T(8,128)(2,1)S(1)} %get-tuple-element.136), channel_id=1, source_target_pairs={{0,4},{1,5},{2,6},{3,7},{4,0},{5,1},{6,2},{7,3},{8,12},{9,13},{10,... | collective-permute-start | bytes 1400840 | tf_op jit(solution)/shard_map/wide_column_0_4/ppermute | solution.py:135
  236.1 11.9 %collective-permute-start.28 = (bf16[48,1280]{1,0:T(8,128)(2,1)S(1)}, bf16[48,1280]{1,0:T(8,128)(2,1)S(1)}, u32[]{:S(2)}, u32[]{:S(2)}) collective-permute-start(bf16[48,1280]{1,0:T(8,128)(2,1)S(1)} %get-tuple-element.134), channel_id=1, source_target_pairs={{0,4},{1,5},{2,6},{3,7},{4,0},{5,1},{6,2},{7,3},{8,12},{9,13},{10,... | collective-permute-start | bytes 368648 | tf_op jit(solution)/shard_map/qkv_column_0_4/ppermute | solution.py:135
  237.3 10.9 %collective-permute-start.29 = (bf16[48,1280]{1,0:T(8,128)(2,1)S(1)}, bf16[48,1280]{1,0:T(8,128)(2,1)S(1)}, u32[]{:S(2)}, u32[]{:S(2)}) collective-permute-start(bf16[48,1280]{1,0:T(8,128)(2,1)S(1)} %get-tuple-element.135), channel_id=1, source_target_pairs={{0,6},{1,7},{2,4},{3,5},{4,2},{5,3},{6,0},{7,1},{8,14},{9,15},{10,... | collective-permute-start | bytes 368648 | tf_op jit(solution)/shard_map/qkv_column_0_6/ppermute | solution.py:135
  241.2 12.1 %collective-permute-start.34 = (bf16[48,2432]{1,0:T(8,128)(2,1)S(1)}, bf16[48,2432]{1,0:T(8,128)(2,1)S(1)}, u32[]{:S(2)}, u32[]{:S(2)}) collective-permute-start(bf16[48,2432]{1,0:T(8,128)(2,1)S(1)} %get-tuple-element.138), channel_id=1, source_target_pairs={{0,2},{1,3},{2,0},{3,1},{4,6},{5,7},{6,4},{7,5},{8,10},{9,11},{10,... | collective-permute-start | bytes 700424 | tf_op jit(solution)/shard_map/wide_column_0_2/ppermute | solution.py:135
  251.6 14.4 %collective-permute-start.32 = (bf16[48,2816]{1,0:T(8,128)(2,1)S(1)}, bf16[48,2816]{1,0:T(8,128)(2,1)S(1)}, u32[]{:S(2)}, u32[]{:S(2)}) collective-permute-start(bf16[48,2816]{1,0:T(8,128)(2,1)S(1)} %qkv_total.1.refs_3_.refs_1_), channel_id=1, source_target_pairs={{0,16},{1,17},{2,18},{3,19},{4,20},{5,21},{6,22},{7,23},{8,24},{9,... | collective-permute-start | bytes 811016 | tf_op jit(solution)/shard_map/qkv_back_2_0/ppermute | solution.py:135
  252.4 13.6 %collective-permute-start.31 = (bf16[48,2816]{1,0:T(8,128)(2,1)S(1)}, bf16[48,2816]{1,0:T(8,128)(2,1)S(1)}, u32[]{:S(2)}, u32[]{:S(2)}) collective-permute-start(bf16[48,2816]{1,0:T(8,128)(2,1)S(1)} %qkv_total.1.refs_3_.refs_1_), channel_id=1, source_target_pairs={{0,8},{1,9},{2,10},{3,11},{4,12},{5,13},{6,14},{7,15},{8,0},{9,1},... | collective-permute-start | bytes 811016 | tf_op jit(solution)/shard_map/qkv_back_1_0/ppermute | solution.py:135
  253.9 15.4 %collective-permute-start.37 = (bf16[48,2432]{1,0:T(8,128)(2,1)S(1)}, bf16[48,2432]{1,0:T(8,128)(2,1)S(1)}, u32[]{:S(2)}, u32[]{:S(2)}) collective-permute-start(bf16[48,2432]{1,0:T(8,128)(2,1)S(1)} %wide_total.1.refs_5_.refs_1_), channel_id=1, source_target_pairs={{0,24},{1,25},{2,26},{3,27},{4,28},{5,29},{6,30},{7,31},{8,16},{9,... | collective-permute-start | bytes 700424 | tf_op jit(solution)/shard_map/wide_back_3_0/ppermute | solution.py:135
  255.7 15.9 %collective-permute-start.36 = (bf16[48,2432]{1,0:T(8,128)(2,1)S(1)}, bf16[48,2432]{1,0:T(8,128)(2,1)S(1)}, u32[]{:S(2)}, u32[]{:S(2)}) collective-permute-start(bf16[48,2432]{1,0:T(8,128)(2,1)S(1)} %wide_total.1.refs_5_.refs_1_), channel_id=1, source_target_pairs={{0,16},{1,17},{2,18},{3,19},{4,20},{5,21},{6,22},{7,23},{8,24},{9,... | collective-permute-start | bytes 700424 | tf_op jit(solution)/shard_map/wide_back_2_0/ppermute | solution.py:135
  260.2 11.4 %collective-permute-start.35 = (bf16[48,2432]{1,0:T(8,128)(2,1)S(1)}, bf16[48,2432]{1,0:T(8,128)(2,1)S(1)}, u32[]{:S(2)}, u32[]{:S(2)}) collective-permute-start(bf16[48,2432]{1,0:T(8,128)(2,1)S(1)} %wide_total.1.refs_5_.refs_1_), channel_id=1, source_target_pairs={{0,8},{1,9},{2,10},{3,11},{4,12},{5,13},{6,14},{7,15},{8,0},{9,1},... | collective-permute-start | bytes 700424 | tf_op jit(solution)/shard_map/wide_back_1_0/ppermute | solution.py:135
  (44 other events, 359.9 us)
Sparse Core Ops, SparseCore 0:
  45.1 50.9 all-gather.1
  160.3 53.7 reduce-scatter.2
  217.0 27.8 reduce-scatter.4

commit v5 on v4

--- a/solution.py
+++ b/solution.py
@@ -401,18 +401,13 @@
 
 def middle_kernel(weights, place_ref, counts_ref, tok_ref, o_ref, cot_out_ref, cot_align_ref, vec_ref, *refs):
     arrays, refs = split_refs(refs, weights)
-    out_ref, aligned_ref, z_ref, e_ref, h_ref, g_ref, du_ref, dm_ref, da_ref, do_ref = refs[:10]
-    sums_ref, w_proj_ref, w_up_ref, w_down_ref, w_head_ref, sems = refs[10:]
+    out_ref, z_ref, e_ref, h_ref, g_ref, du_ref, dm_ref, da_ref, do_ref = refs[:9]
+    sums_ref, w_proj_ref, w_up_ref, w_down_ref, w_head_ref, sems = refs[9:]
     step = pl.program_id(0)
     size, width = tok_ref.shape
     hidden_units = w_up_ref.shape[-1]
     part = hidden_units // PARTS
-    seq = place_ref[SEQ]
-    total = jnp.int32(0)
-    for slot in range(counts_ref.shape[1]):
-        total = total + counts_ref[seq, slot]
-    places = lax.broadcasted_iota(jnp.int32, (size, 1), 0) + step * size
-    valid = jnp.where(places < total, 1.0, 0.0).astype(f32)
+    valid = rows_valid(place_ref, counts_ref, step, size)
 
     @pl.when(step == 0)
     def _():
@@ -454,7 +449,6 @@
     out_ref[...] = (x2 * valid).astype(bf16)
     z = x2.astype(bf16)
     z_ref[...] = z
-    aligned_ref[...] = ((dot_nn(z, matrix(w_head_ref)) + row(vec_ref, B_HEAD, cot_align_ref.shape[1])) * valid).astype(bf16)
 
     add_sum(GAIN_TWO, 0, dh2 * n2)
     add_sum(SHIFT_TWO, 0, dh2)
@@ -480,7 +474,6 @@
 
     outs = [
         (by_row(width), row_shape(width)),
-        (by_row(align), row_shape(align)),
         (by_row(width), row_shape(width)),
         (by_row(align), row_shape(align)),
         (by_row(width), row_shape(width)),
@@ -503,6 +496,42 @@
         vmem=54,
         scratch=weight_scratch(weights),
     )
+
+
+def rows_valid(place_ref, counts_ref, step, size):
+    total = jnp.int32(0)
+    for slot in range(counts_ref.shape[1]):
+        total = total + counts_ref[place_ref[SEQ], slot]
+    places = lax.broadcasted_iota(jnp.int32, (size, 1), 0) + step * size
+    return jnp.where(places < total, 1.0, 0.0).astype(f32)
+
+
+def align_kernel(weight, place_ref, counts_ref, z_ref, vec_ref, *refs):
+    arrays, (out_ref, w_ref, sems) = split_refs(refs, [weight])
+    step = pl.program_id(0)
+
+    @pl.when(step == 0)
+    def _():
+        fetch_all(place_ref, [weight], arrays, [w_ref], sems)
+
+    valid = rows_valid(place_ref, counts_ref, step, z_ref.shape[0])
+    value = dot_nn(z_ref[...], matrix(w_ref)) + row(vec_ref, B_HEAD, out_ref.shape[1])
+    out_ref[...] = (value * valid).astype(bf16)
+
+
+def align(order, counts, z, weight, vectors):
+    rows, width = z.shape
+    size = row_tile(rows, 320)
+    return order(
+        functools.partial(align_kernel, weight),
+        "align",
+        [counts, z, vectors] + weight.arrays,
+        [SMEM, pl.BlockSpec((size, width), lambda i, p: (i, 0)), whole(vectors.shape)] + [ANY] * len(weight.arrays),
+        [(pl.BlockSpec((size, weight.shape[1]), lambda i, p: (i, 0)), shape_of((rows, weight.shape[1])))],
+        grid=(rows // size,),
+        scratch=weight_scratch([weight]),
+        vmem=56,
+    )[0]
 
 
 def outer_kernel(place_ref, l_ref, r_ref, out_ref):
@@ -1050,7 +1079,7 @@
     out_ref[...] = (dx_ref[...].astype(f32) + inverse * inner).astype(bf16)
 
 
-def first_back(order, tokens, dx1, dqkv, weight, vectors):
+def first_back(order, tokens, dx1, dqkv, weight, vectors, after):
     rows, width = tokens.shape
     size = row_tile(rows, 320)
     rowwise = pl.BlockSpec((size, width), lambda i, p: (i, 0))
@@ -1062,6 +1091,7 @@
         + [ANY] * len(weight.arrays),
         [(rowwise, shape_of((rows, width))), (out_whole((2, width)), shape_of((2, width), f32))],
         grid=(rows // size,),
+        after=after,
         scratch=weight_scratch([weight]),
         vmem=56,
     )
@@ -1148,7 +1178,7 @@
         full_up, full_head, full_proj = (
             Weight(both_cores, column, (width, w.shape[1])) for column, w in zip(at, wide)
         )
-    block_out, aligned, z, e_al, h2, g, du, dm, da, do, sums = middle(
+    block_out, z, e_al, h2, g, du, dm, da, do, sums = middle(
         order,
         clip_counts,
         tokens,
@@ -1163,7 +1193,7 @@
         pairs = outer_group(order, [(h2, du), (z, e_al), (o, da)], [768, 512, 768], levels, "grad_wide")
         for pair, w in zip(pairs, wide):
             r_wide.add(*pair, [w.shape[1]])
-    d_down = scatter(outer(order, g, dm, 512, 768, "grad_down"))
+    d_down = scatter(outer(order, g, dm, 1024, 768, "grad_down"))
     if paired:
         r_wide.split()
     dqkv, s_qv = attend_back(order, bias, q, k, v, o, do, lse)
@@ -1176,11 +1206,12 @@
         keep, send = pack_vectors(order, [sums, s_qv], early, lengths, levels, "pack_early")
         lines = [keep, swap(send, "vectors_core", fsdp=1)]
         r_qkv.split()
+        aligned = align(order, clip_counts, z, full_head, vectors)
         r_wide.halve()
-    grad_tokens, s_first = first_back(order, tokens, da, dqkv, full_qkv, vectors)
+    grad_tokens, s_first = first_back(order, tokens, da, dqkv, full_qkv, vectors, [d_down] if paired else [])
     if paired:
         late = {GAIN_ONE: (0, 0), SHIFT_ONE: (0, 1)}
-        keep, send = pack_vectors(order, [s_first], late, lengths, levels, "pack_late", [d_down])
+        keep, send = pack_vectors(order, [s_first], late, lengths, levels, "pack_late")
         lines += [keep, swap(send, "vectors_core", fsdp=1)]
         d_down = lax.psum_scatter(d_down, "dp", scatter_dimension=0, tiled=True)
         r_qkv.levels(lines)
@@ -1191,6 +1222,7 @@
         d_qkv, d_down, *mine = r_qkv.join(lengths=parts, beside=w_down.shape)
         d_up, d_head, d_proj = r_wide.join()
     else:
+        aligned = align(order, clip_counts, z, full_head, vectors)
 
         def reduce(value):
             return lax.psum(scatter(value), "dp").astype(f32)

time: 283 us -> 281 us (level)
  waiting for transfers between devices: 71.9 us -> 66.3 us
  Pallas kernels: 145 us -> 148 us
    ppermute x38, waiting for transfers between devices: 69.1 us -> 63.8 us  [swap(): return lax.ppermute(value, ('dp', 'fsdp'), pairs)]
    pallas_call x26 -> x27, Pallas kernels: 145 us -> 148 us  [__call__(): pl.pallas_call(body, grid_spec=pltpu.PrefetchScalarGridSpec(num_scalar_pr...]
    unnamed x70 -> x76, local copies, waits for them, and re-layouts: 10.9 us -> 13.3 us
  transfers between devices with their start and end apart: 41 -> 41, of which waited for: 18 -> 19; matrix products, arithmetic and copies ran while one was open for 0% -> 0% of each run, Pallas kernels for 31% -> 33%
where the time goes in v5:
time: 281 us; the launch traced here: 280 us
  Pallas kernels  148 us (53%)
  waiting for transfers between devices  66.3 us (24%)
  starting transfers between devices  36.6 us (13%)
  between operations  14.4 us (5%)
  local copies, waits for them, and re-layouts  13.9 us (5%)
    pallas_call x27, Pallas kernels, __call__(): pl.pallas_call(body, grid_spec=pltpu.PrefetchScalarGridSpec(num_scalar_pr...  148 us
    ppermute x38, waiting for transfers between devices, swap(): return lax.ppermute(value, ('dp', 'fsdp'), pairs)  63.8 us
    ppermute x38, starting transfers between devices, swap(): return lax.ppermute(value, ('dp', 'fsdp'), pairs)  36.5 us
    unnamed x76, local copies, waits for them, and re-layouts  13.3 us
  transfers between devices with their start and end apart: 41, of which 19 were waited for; matrix products, arithmetic and copies ran while one was open for 0% of the time, Pallas kernels for 33%

profile of v5, /device:TPU:0, one launch (start us, length us, event | category | flops | bytes accessed | tf_op | source)
XLA Modules:
  0.0 279.7 jit_solution(6244393026140874879)
XLA Ops:
  7.9 2.6 quarters.1
  10.5 5.0 %collective-permute-start.2 = (bf16[48,1280]{1,0:T(8,128)(2,1)}, bf16[48,1280]{1,0:T(8,128)(2,1)S(1)}, u32[]{:S(2)}, u32[]{:S(2)}) collective-permute-start(bf16[48,1280]{1,0:T(8,128)(2,1)} %get-tuple-element.84.refs_2_.refs_1_), channel_id=1, source_target_pairs={{0,6},{1,7},{2,4},{3,5},{4,2},{5,3},{6,0},{7,1},{8,14},{9,15},{10,... | collective-permute-start | bytes 368648 | tf_op jit(solution)/shard_map/qkv_column_0_6/ppermute | solution.py:135
  17.1 3.2 %masks.1.refs_5_.refs_1_ = f32[3072,128]{1,0:T(8,128)S(1)} custom-call(s32[5]{0:T(128)S(1)} %copy-done.7, s32[32,32]{1,0:T(8,128)S(1)} %copy-done.6, bf16[48,1280]{1,0:T(8,128)(2,1)S(1)} %copy-done.20), custom_call_target="tpu_custom_call" | custom-call | flops 10000000000 | bytes 1 | tf_op jit(solution)/shard_map/masks/pallas_call | solution.py:103
  20.4 5.8 %collective-permute-done.1.refs_3_ = bf16[48,1280]{1,0:T(8,128)(2,1)S(1)} collective-permute-done((bf16[48,1280]{1,0:T(8,128)(2,1)}, bf16[48,1280]{1,0:T(8,128)(2,1)S(1)}, u32[]{:S(2)}, u32[]{:S(2)}) %collective-permute-start.1) | collective-permute-done | bytes 122912 | tf_op jit(solution)/shard_map/qkv_column_0_4/ppermute | solution.py:135
  26.7 2.5 collective-permute-start.6
  30.3 2.5 collective-permute-start.10
  32.8 5.7 %collective-permute-done.6.refs_5_ = bf16[3,48,1152]{2,1,0:T(8,128)(2,1)S(1)} collective-permute-done((bf16[3,48,1152]{2,1,0:T(8,128)(2,1)S(1)}, bf16[3,48,1152]{2,1,0:T(8,128)(2,1)S(1)}, u32[]{:S(2)}, u32[]{:S(2)}) %collective-permute-start.6) | collective-permute-done | bytes 331808 | tf_op jit(solution)/shard_map/qkv_plane_3_0/ppermute | solution.py:135
  38.5 5.2 %collective-permute-done.5.refs_4_ = bf16[3,48,1152]{2,1,0:T(8,128)(2,1)S(1)} collective-permute-done((bf16[3,48,1152]{2,1,0:T(8,128)(2,1)S(1)}, bf16[3,48,1152]{2,1,0:T(8,128)(2,1)S(1)}, u32[]{:S(2)}, u32[]{:S(2)}) %collective-permute-start.5) | collective-permute-done | bytes 331808 | tf_op jit(solution)/shard_map/qkv_plane_2_0/ppermute | solution.py:135
  45.7 5.1 %collective-permute-done.9.refs_3_ = bf16[48,2432]{1,0:T(8,128)(2,1)} collective-permute-done((bf16[48,2432]{1,0:T(8,128)(2,1)}, bf16[48,2432]{1,0:T(8,128)(2,1)}, u32[]{:S(2)}, u32[]{:S(2)}) %collective-permute-start.9) | collective-permute-done | bytes 233504 | tf_op jit(solution)/shard_map/wide_column_0_4/ppermute | solution.py:135
  50.8 2.0 wide_near.1.refs_5_.refs_4_
  52.8 2.5 collective-permute-start.13
  56.4 6.9 %norm_qkv.1 = (bf16[960,768]{1,0:T(8,128)(2,1)S(1)}, bf16[960,768]{1,0:T(8,128)(2,1)S(1)}, bf16[960,768]{1,0:T(8,128)(2,1)S(1)}, bf16[960,768]{1,0:T(8,128)(2,1)S(1)}) custom-call(s32[5]{0:T(128)S(1)} %copy-done.7, bf16[960,768]{1,0:T(8,128)(2,1)S(1)} %copy-done.2, bf16[16,3072]{1,0:T(8,128)(2,1)S(1)} %unpack_vectors.1.refs_5_.refs_2_.refs_6_.refs_3_.refs_4_, ...), custom_call_target="tpu_custom_call" | custom-call | flops 10000000000 | bytes 1 | tf_op jit(solution)/shard_map/norm_qkv/pallas_call | solution.py:103
  63.4 10.0 %attend.1 = (bf16[960,768]{1,0:T(8,128)(2,1)S(1)}, f32[6,8,256]{2,1,0:T(8,128)S(1)}) custom-call(s32[5]{0:T(128)S(1)} %copy-done.7, f32[3072,128]{1,0:T(8,128)S(1)} %copy-done.29, bf16[960,768]{1,0:T(8,128)(2,1)S(1)} %get-tuple-element.88.refs_2_, bf16[960,768]{1,0:T(8,128)(2,1)S(1)} %get-tuple-element.89.refs_3_, ...), custom_call_target="tpu_custom_call" | custom-call | flops 10000000000 | bytes 1 | tf_op jit(solution)/shard_map/attend/pallas_call | solution.py:103
  73.5 10.5 %collective-permute-done.12.refs_6_ = bf16[3,48,2432]{2,1,0:T(8,128)(2,1)S(1)} collective-permute-done((bf16[3,48,2432]{2,1,0:T(8,128)(2,1)S(1)}, bf16[3,48,2432]{2,1,0:T(8,128)(2,1)S(1)}, u32[]{:S(2)}, u32[]{:S(2)}) %collective-permute-start.12) | collective-permute-done | bytes 700448 | tf_op jit(solution)/shard_map/wide_plane_2_0/ppermute | solution.py:135
  87.0 6.6 %collective-permute-done.14.refs_8_.refs_10_.refs_13_.refs_5_ = bf16[4,96,4864]{2,1,0:T(8,128)(2,1)} collective-permute-done((bf16[4,96,4864]{2,1,0:T(8,128)(2,1)S(1)}, bf16[4,96,4864]{2,1,0:T(8,128)(2,1)}, u32[]{:S(2)}, u32[]{:S(2)}) %collective-permute-start.14) | collective-permute-done | bytes 3735584 | tf_op jit(solution)/shard_map/wide_core_0_1/ppermute | solution.py:135
  93.6 2.5 all-gather.2.cloned.1.call-done.refs_11_
  96.1 34.3 %middle.1 = (bf16[960,768]{1,0:T(8,128)(2,1)}, bf16[960,768]{1,0:T(8,128)(2,1)}, bf16[960,1024]{1,0:T(8,128)(2,1)}, bf16[960,768]{1,0:T(8,128)(2,1)}, bf16[960,3...) custom-call(s32[5]{0:T(128)} %stack.23.refs_0_, ...), custom_call_target="tpu_custom_call" | custom-call | flops 10000000000 | bytes 1 | tf_op jit(solution)/shard_map/middle/pallas_call | solution.py:103
  130.4 16.3 %grad_wide.1 = (bf16[4,2,48,3072]{3,2,1,0:T(8,128)(2,1)}, bf16[4,2,48,3072]{3,2,1,0:T(8,128)(2,1)}, bf16[4,2,48,1024]{3,2,1,0:T(8,128)(2,1)}, bf16[4,2,48,1024]{...) custom-call(s32[5]{0:T(128)} %stack.23.refs_0_, ...), custom_call_target="tpu_custom_call" | custom-call | flops 10000000000 | bytes 1 | tf_op jit(solution)/shard_map/grad_wide/pallas_call | solution.py:103
  147.5 9.9 %grad_down.1.refs_7_ = bf16[3072,768]{1,0:T(8,128)(2,1)} custom-call(s32[5]{0:T(128)} %stack.23.refs_0_, bf16[960,3072]{1,0:T(8,128)(2,1)} %get-tuple-element.108.refs_1_, bf16[960,768]{1,0:T(8,128)(2,1)} %get-tuple-element.109.refs_2_, bf16[4,2,48,3072]{3,2,1,0:T(8,128)(2,1)} %get-tuple-element.102.refs_3_.refs_1_), custom_call_target="tpu_custom_call" | custom-call | flops 30000001024 | bytes 1 | tf_op jit(solution)/shard_map/grad_down/pallas_call | solution.py:103
  159.2 6.1 %wide_split.1 = (bf16[4,48,2432]{2,1,0:T(8,128)(2,1)}, bf16[4,48,2432]{2,1,0:T(8,128)(2,1)}, bf16[4,48,2432]{2,1,0:T(8,128)(2,1)}, bf16[4,48,2432]{2,1,0:T(8,128)(2,1)}) custom-call(s32[5]{0:T(128)} %stack.23.refs_0_, bf16[4,2,48,3072]{3,2,1,0:T(8,128)(2,1)} %get-tuple-element.102.refs_3_.refs_1_, bf16[4,2,48,3072]{3,2,1,0:T(8,128)(2,1)} %copy-done.36, ...), custom_call_target="tpu_custom_call" | custom-call | flops 10000000000 | bytes 1 | tf_op jit(solution)/shard_map/wide_split/pallas_call | solution.py:103
  168.8 17.2 %attend_back.1 = (bf16[3,960,768]{2,1,0:T(8,128)(2,1)}, f32[2,768]{1,0:T(2,128)}) custom-call(s32[5]{0:T(128)} %stack.23.refs_0_, f32[3072,128]{1,0:T(8,128)} %copy-done.28, bf16[960,768]{1,0:T(8,128)(2,1)} %copy-done.30, bf16[960,768]{1,0:T(8,128)(2,1)} %copy-done.31, bf16[960,768]{1,0:T(8,128)(2,1)} %copy-done.32, bf16[960,768]{1,0:T(8,128)(2,1)} %copy-done.3, ...), custom_call_target="tpu_custom_call" | custom-call | flops 60000002048 | bytes 1 | tf_op jit(solution)/shard_map/attend_back/pallas_call | solution.py:103
  186.0 8.8 %grad_qkv.1 = (bf16[4,2,48,2304]{3,2,1,0:T(8,128)(2,1)}, bf16[4,2,48,2304]{3,2,1,0:T(8,128)(2,1)}) custom-call(s32[5]{0:T(128)} %stack.23.refs_0_, bf16[960,768]{1,0:T(8,128)(2,1)} %copy-done.27, bf16[3,960,768]{2,1,0:T(8,128)(2,1)} %get-tuple-element.111.refs_2_.refs_3_, bf16[3,960,768]{2,1,0:T(8,128)(2,1)} %get-tuple-element.111.refs_2_.refs_3_), custom_call_target="tpu_custom_call" | custom-call | flops 10000000000 | bytes 1 | tf_op jit(solution)/shard_map/grad_qkv/pallas_call | solution.py:103
  202.0 6.8 %align.1.refs_5_ = bf16[960,1024]{1,0:T(8,128)(2,1)} custom-call(s32[5]{0:T(128)} %stack.23.refs_0_, s32[32,32]{1,0:T(8,128)} %refs_1_.14, bf16[960,768]{1,0:T(8,128)(2,1)} %get-tuple-element.95.refs_2_, bf16[16,3072]{1,0:T(8,128)(2,1)} %copy-done.5, bf16[4,96,4864]{2,1,0:T(8,128)(2,1)} %bitcast.16, ...), custom_call_target="tpu_custom_call" | custom-call | flops 10000000000 | bytes 1 | tf_op jit(solution)/shard_map/align/pallas_call | solution.py:103
  215.5 10.7 %first_back.1 = (bf16[960,768]{1,0:T(8,128)(2,1)}, f32[2,768]{1,0:T(2,128)}) custom-call(s32[5]{0:T(128)} %stack.23.refs_0_, bf16[960,768]{1,0:T(8,128)(2,1)} %refs_1_.15, bf16[960,768]{1,0:T(8,128)(2,1)} %get-tuple-element.101.refs_6_.refs_2_, bf16[3,960,768]{2,1,0:T(8,128)(2,1)} %get-tuple-element.111.refs_2_.refs_3_, bf16[16,3072]{1,0:T(8,128)(2,1)} %copy-done.5, ...), custom_call_target="tpu_custom_call" | custom-call | flops 10000000000 | bytes 1 | tf_op jit(solution)/shard_map/first_back/pallas_call | solution.py:103
  229.1 3.6 %collective-permute-done.23.refs_3_ = bf16[4,48,1152]{2,1,0:T(8,128)(2,1)S(1)} collective-permute-done((bf16[4,48,1152]{2,1,0:T(8,128)(2,1)S(1)}, bf16[4,48,1152]{2,1,0:T(8,128)(2,1)S(1)}, u32[]{:S(2)}, u32[]{:S(2)}) %collective-permute-start.23) | collective-permute-done | bytes 442400 | tf_op jit(solution)/shard_map/qkv_plane_2_0/ppermute | solution.py:135
  235.8 3.2 %collective-permute-start.29 = (bf16[48,1280]{1,0:T(8,128)(2,1)S(1)}, bf16[48,1280]{1,0:T(8,128)(2,1)S(1)}, u32[]{:S(2)}, u32[]{:S(2)}) collective-permute-start(bf16[48,1280]{1,0:T(8,128)(2,1)S(1)} %get-tuple-element.133), channel_id=1, source_target_pairs={{0,6},{1,7},{2,4},{3,5},{4,2},{5,3},{6,0},{7,1},{8,14},{9,15},{10,... | collective-permute-start | bytes 368648 | tf_op jit(solution)/shard_map/qkv_column_0_6/ppermute | solution.py:135
  239.7 3.4 %collective-permute-done.27.refs_2_ = bf16[48,1280]{1,0:T(8,128)(2,1)S(1)} collective-permute-done((bf16[48,1280]{1,0:T(8,128)(2,1)S(1)}, bf16[48,1280]{1,0:T(8,128)(2,1)S(1)}, u32[]{:S(2)}, u32[]{:S(2)}) %collective-permute-start.27) | collective-permute-done | bytes 122912 | tf_op jit(solution)/shard_map/qkv_column_0_2/ppermute | solution.py:135
  254.3 4.1 %collective-permute-done.33.refs_4_ = bf16[48,2816]{1,0:T(8,128)(2,1)S(1)} collective-permute-done((bf16[48,2816]{1,0:T(8,128)(2,1)S(1)}, bf16[48,2816]{1,0:T(8,128)(2,1)S(1)}, u32[]{:S(2)}, u32[]{:S(2)}) %collective-permute-start.33) | collective-permute-done | bytes 270368 | tf_op jit(solution)/shard_map/qkv_back_3_0/ppermute | solution.py:135
  259.1 5.2 %collective-permute-done.32.refs_3_ = bf16[48,2816]{1,0:T(8,128)(2,1)S(1)} collective-permute-done((bf16[48,2816]{1,0:T(8,128)(2,1)S(1)}, bf16[48,2816]{1,0:T(8,128)(2,1)S(1)}, u32[]{:S(2)}, u32[]{:S(2)}) %collective-permute-start.32) | collective-permute-done | bytes 270368 | tf_op jit(solution)/shard_map/qkv_back_2_0/ppermute | solution.py:135
  264.4 2.0 qkv_join.1
  267.7 2.3 collective-permute-done.36.refs_3_
  271.2 1.9 wide_join.1
  (157 shorter events, 50.6 us)
Async XLA Ops:
  7.2 88.9 %all-gather.2.cloned.1.call-start = ((), (), s32[]{:S(2)}) async-start(), calls=%async_computation.2 | async-start | bytes 5308416 | tf_op jit(solution)/shard_map/all_gather | solution.py:1136
  15.6 10.6 %collective-permute-start.1 = (bf16[48,1280]{1,0:T(8,128)(2,1)}, bf16[48,1280]{1,0:T(8,128)(2,1)S(1)}, u32[]{:S(2)}, u32[]{:S(2)}) collective-permute-start(bf16[48,1280]{1,0:T(8,128)(2,1)} %get-tuple-element.84.refs_2_.refs_1_), channel_id=1, source_target_pairs={{0,4},{1,5},{2,6},{3,7},{4,0},{5,1},{6,2},{7,3},{8,12},{9,13},{10,... | collective-permute-start | bytes 368648 | tf_op jit(solution)/shard_map/qkv_column_0_4/ppermute | solution.py:135
  15.6 10.6 %collective-permute-start = (bf16[48,1280]{1,0:T(8,128)(2,1)}, bf16[48,1280]{1,0:T(8,128)(2,1)S(1)}, u32[]{:S(2)}, u32[]{:S(2)}) collective-permute-start(bf16[48,1280]{1,0:T(8,128)(2,1)} %get-tuple-element.84.refs_2_.refs_1_), channel_id=1, source_target_pairs={{0,2},{1,3},{2,0},{3,1},{4,6},{5,7},{6,4},{7,5},{8,10},{9,11},{10,... | collective-permute-start | bytes 368648 | tf_op jit(solution)/shard_map/qkv_column_0_2/ppermute | solution.py:135
  26.7 11.7 %collective-permute-start.6 = (bf16[3,48,1152]{2,1,0:T(8,128)(2,1)S(1)}, bf16[3,48,1152]{2,1,0:T(8,128)(2,1)S(1)}, u32[]{:S(2)}, u32[]{:S(2)}) collective-permute-start(bf16[3,48,1152]{2,1,0:T(8,128)(2,1)S(1)} %get-tuple-element.86.refs_2_.refs_6_), channel_id=1, source_target_pairs={{0,24},{1,25},{2,26},{3,27},{4,28},{5,29},{6,30},{7,31},{8,16},{9,... | collective-permute-start | bytes 995336 | tf_op jit(solution)/shard_map/qkv_plane_3_0/ppermute | solution.py:135
  29.3 14.4 %collective-permute-start.5 = (bf16[3,48,1152]{2,1,0:T(8,128)(2,1)S(1)}, bf16[3,48,1152]{2,1,0:T(8,128)(2,1)S(1)}, u32[]{:S(2)}, u32[]{:S(2)}) collective-permute-start(bf16[3,48,1152]{2,1,0:T(8,128)(2,1)S(1)} %get-tuple-element.86.refs_2_.refs_6_), channel_id=1, source_target_pairs={{0,16},{1,17},{2,18},{3,19},{4,20},{5,21},{6,22},{7,23},{8,24},{9,... | collective-permute-start | bytes 995336 | tf_op jit(solution)/shard_map/qkv_plane_2_0/ppermute | solution.py:135
  29.8 14.0 %collective-permute-start.4 = (bf16[3,48,1152]{2,1,0:T(8,128)(2,1)S(1)}, bf16[3,48,1152]{2,1,0:T(8,128)(2,1)S(1)}, u32[]{:S(2)}, u32[]{:S(2)}) collective-permute-start(bf16[3,48,1152]{2,1,0:T(8,128)(2,1)S(1)} %get-tuple-element.86.refs_2_.refs_6_), channel_id=1, source_target_pairs={{0,8},{1,9},{2,10},{3,11},{4,12},{5,13},{6,14},{7,15},{8,0},{9,1},... | collective-permute-start | bytes 995336 | tf_op jit(solution)/shard_map/qkv_plane_1_0/ppermute | solution.py:135
  30.3 15.4 %collective-permute-start.10 = (bf16[48,2432]{1,0:T(8,128)(2,1)}, bf16[48,2432]{1,0:T(8,128)(2,1)}, u32[]{:S(2)}, u32[]{:S(2)}) collective-permute-start(bf16[48,2432]{1,0:T(8,128)(2,1)} %get-tuple-element.87.refs_1_), channel_id=1, source_target_pairs={{0,6},{1,7},{2,4},{3,5},{4,2},{5,3},{6,0},{7,1},{8,14},{9,15},{10,... | collective-permute-start | bytes 700424 | tf_op jit(solution)/shard_map/wide_column_0_6/ppermute | solution.py:135
  32.8 18.1 %collective-permute-start.9 = (bf16[48,2432]{1,0:T(8,128)(2,1)}, bf16[48,2432]{1,0:T(8,128)(2,1)}, u32[]{:S(2)}, u32[]{:S(2)}) collective-permute-start(bf16[48,2432]{1,0:T(8,128)(2,1)} %get-tuple-element.87.refs_1_), channel_id=1, source_target_pairs={{0,4},{1,5},{2,6},{3,7},{4,0},{5,1},{6,2},{7,3},{8,12},{9,13},{10,... | collective-permute-start | bytes 700424 | tf_op jit(solution)/shard_map/wide_column_0_4/ppermute | solution.py:135
  38.5 12.3 %collective-permute-start.8 = (bf16[48,2432]{1,0:T(8,128)(2,1)}, bf16[48,2432]{1,0:T(8,128)(2,1)}, u32[]{:S(2)}, u32[]{:S(2)}) collective-permute-start(bf16[48,2432]{1,0:T(8,128)(2,1)} %get-tuple-element.87.refs_1_), channel_id=1, source_target_pairs={{0,2},{1,3},{2,0},{3,1},{4,6},{5,7},{6,4},{7,5},{8,10},{9,11},{10,... | collective-permute-start | bytes 700424 | tf_op jit(solution)/shard_map/wide_column_0_2/ppermute | solution.py:135
  44.5 11.9 %collective-permute-start.7 = (bf16[4,96,2304]{2,1,0:T(8,128)(2,1)S(1)}, bf16[4,96,2304]{2,1,0:T(8,128)(2,1)}, u32[]{:S(2)}, u32[]{:S(2)}) collective-permute-start(bf16[4,96,2304]{2,1,0:T(8,128)(2,1)S(1)} %bitcast.17), channel_id=1, source_target_pairs={{0,1},{1,0},{2,3},{3,2},{4,5},{5,4},{6,7},{7,6},{8,9},{9,8},{10,11... | collective-permute-start | bytes 5308424 | tf_op jit(solution)/shard_map/qkv_core_0_1/ppermute | solution.py:135
  45.0 170.5 %reduce-scatter.3.cloned.1.call-start = ((), (), s32[]{:S(2)}) async-start(), calls=%async_computation.3 | async-start | bytes 5308416 | tf_op jit(solution)/shard_map/reduce_scatter | solution.py:1139
  52.8 20.7 %collective-permute-start.13 = (bf16[3,48,2432]{2,1,0:T(8,128)(2,1)S(1)}, bf16[3,48,2432]{2,1,0:T(8,128)(2,1)S(1)}, u32[]{:S(2)}, u32[]{:S(2)}) collective-permute-start(bf16[3,48,2432]{2,1,0:T(8,128)(2,1)S(1)} %wide_near.1.refs_5_.refs_4_), channel_id=1, source_target_pairs={{0,24},{1,25},{2,26},{3,27},{4,28},{5,29},{6,30},{7,31},{8,16},{9,... | collective-permute-start | bytes 2101256 | tf_op jit(solution)/shard_map/wide_plane_3_0/ppermute | solution.py:135
  55.3 28.6 %collective-permute-start.12 = (bf16[3,48,2432]{2,1,0:T(8,128)(2,1)S(1)}, bf16[3,48,2432]{2,1,0:T(8,128)(2,1)S(1)}, u32[]{:S(2)}, u32[]{:S(2)}) collective-permute-start(bf16[3,48,2432]{2,1,0:T(8,128)(2,1)S(1)} %wide_near.1.refs_5_.refs_4_), channel_id=1, source_target_pairs={{0,16},{1,17},{2,18},{3,19},{4,20},{5,21},{6,22},{7,23},{8,24},{9,... | collective-permute-start | bytes 2101256 | tf_op jit(solution)/shard_map/wide_plane_2_0/ppermute | solution.py:135
  55.8 28.2 %collective-permute-start.11 = (bf16[3,48,2432]{2,1,0:T(8,128)(2,1)S(1)}, bf16[3,48,2432]{2,1,0:T(8,128)(2,1)S(1)}, u32[]{:S(2)}, u32[]{:S(2)}) collective-permute-start(bf16[3,48,2432]{2,1,0:T(8,128)(2,1)S(1)} %wide_near.1.refs_5_.refs_4_), channel_id=1, source_target_pairs={{0,8},{1,9},{2,10},{3,11},{4,12},{5,13},{6,14},{7,15},{8,0},{9,1},... | collective-permute-start | bytes 2101256 | tf_op jit(solution)/shard_map/wide_plane_1_0/ppermute | solution.py:135
  146.7 10.8 %collective-permute-start.17 = (bf16[4,2,48,768]{3,2,1,0:T(8,128)(2,1)}, bf16[4,2,48,768]{3,2,1,0:T(8,128)(2,1)}, u32[]{:S(2)}, u32[]{:S(2)}) collective-permute-start(bf16[4,2,48,768]{3,2,1,0:T(8,128)(2,1)} %get-tuple-element.107), channel_id=1, source_target_pairs={{0,1},{1,0},{2,3},{3,2},{4,5},{5,4},{6,7},{7,6},{8,9},{9,8},{10,11... | collective-permute-start | bytes 1769480 | tf_op jit(solution)/shard_map/wide_core_0_1/ppermute | solution.py:135
  147.0 10.5 %collective-permute-start.16 = (bf16[4,2,48,1024]{3,2,1,0:T(8,128)(2,1)}, bf16[4,2,48,1024]{3,2,1,0:T(8,128)(2,1)S(1)}, u32[]{:S(2)}, u32[]{:S(2)}) collective-permute-start(bf16[4,2,48,1024]{3,2,1,0:T(8,128)(2,1)} %get-tuple-element.105), channel_id=1, source_target_pairs={{0,1},{1,0},{2,3},{3,2},{4,5},{5,4},{6,7},{7,6},{8,9},{9,8},{10,11... | collective-permute-start | bytes 2359304 | tf_op jit(solution)/shard_map/wide_core_0_1/ppermute | solution.py:135
  157.5 88.9 %reduce-scatter.5.cloned.1.call-start = ((), (), s32[]{:S(2)}) async-start(), calls=%async_computation.4 | async-start | bytes 737280 | tf_op jit(solution)/shard_map/reduce_scatter | solution.py:1216
  165.3 43.5 %collective-permute-start.19 = (bf16[4,48,2432]{2,1,0:T(8,128)(2,1)}, bf16[4,48,2432]{2,1,0:T(8,128)(2,1)S(1)}, u32[]{:S(2)}, u32[]{:S(2)}) collective-permute-start(bf16[4,48,2432]{2,1,0:T(8,128)(2,1)} %get-tuple-element.118), channel_id=1, source_target_pairs={{0,8},{1,9},{2,10},{3,11},{4,12},{5,13},{6,14},{7,15},{8,0},{9,1},... | collective-permute-start | bytes 2801672 | tf_op jit(solution)/shard_map/wide_plane_1_0/ppermute | solution.py:135
  166.9 43.5 %collective-permute-start.20 = (bf16[4,48,2432]{2,1,0:T(8,128)(2,1)}, bf16[4,48,2432]{2,1,0:T(8,128)(2,1)S(1)}, u32[]{:S(2)}, u32[]{:S(2)}) collective-permute-start(bf16[4,48,2432]{2,1,0:T(8,128)(2,1)} %get-tuple-element.119), channel_id=1, source_target_pairs={{0,16},{1,17},{2,18},{3,19},{4,20},{5,21},{6,22},{7,23},{8,24},{9,... | collective-permute-start | bytes 2801672 | tf_op jit(solution)/shard_map/wide_plane_2_0/ppermute | solution.py:135
  168.3 42.7 %collective-permute-start.21 = (bf16[4,48,2432]{2,1,0:T(8,128)(2,1)}, bf16[4,48,2432]{2,1,0:T(8,128)(2,1)S(1)}, u32[]{:S(2)}, u32[]{:S(2)}) collective-permute-start(bf16[4,48,2432]{2,1,0:T(8,128)(2,1)} %get-tuple-element.120), channel_id=1, source_target_pairs={{0,24},{1,25},{2,26},{3,27},{4,28},{5,29},{6,30},{7,31},{8,16},{9,... | collective-permute-start | bytes 2801672 | tf_op jit(solution)/shard_map/wide_plane_3_0/ppermute | solution.py:135
  197.1 31.9 %collective-permute-start.25 = (bf16[4,16,128]{2,1,0:T(8,128)(2,1)S(1)}, bf16[4,16,128]{2,1,0:T(8,128)(2,1)S(1)}, u32[]{:S(2)}, u32[]{:S(2)}) collective-permute-start(bf16[4,16,128]{2,1,0:T(8,128)(2,1)S(1)} %get-tuple-element.126), channel_id=1, source_target_pairs={{0,1},{1,0},{2,3},{3,2},{4,5},{5,4},{6,7},{7,6},{8,9},{9,8},{10,11... | collective-permute-start | bytes 49160 | tf_op jit(solution)/shard_map/vectors_core_0_1/ppermute | solution.py:135
  200.6 28.5 %collective-permute-start.22 = (bf16[4,48,1152]{2,1,0:T(8,128)(2,1)S(1)}, bf16[4,48,1152]{2,1,0:T(8,128)(2,1)S(1)}, u32[]{:S(2)}, u32[]{:S(2)}) collective-permute-start(bf16[4,48,1152]{2,1,0:T(8,128)(2,1)S(1)} %get-tuple-element.123), channel_id=1, source_target_pairs={{0,8},{1,9},{2,10},{3,11},{4,12},{5,13},{6,14},{7,15},{8,0},{9,1},... | collective-permute-start | bytes 1327112 | tf_op jit(solution)/shard_map/qkv_plane_1_0/ppermute | solution.py:135
  208.8 23.9 %collective-permute-start.23 = (bf16[4,48,1152]{2,1,0:T(8,128)(2,1)S(1)}, bf16[4,48,1152]{2,1,0:T(8,128)(2,1)S(1)}, u32[]{:S(2)}, u32[]{:S(2)}) collective-permute-start(bf16[4,48,1152]{2,1,0:T(8,128)(2,1)S(1)} %get-tuple-element.124), channel_id=1, source_target_pairs={{0,16},{1,17},{2,18},{3,19},{4,20},{5,21},{6,22},{7,23},{8,24},{9,... | collective-permute-start | bytes 1327112 | tf_op jit(solution)/shard_map/qkv_plane_2_0/ppermute | solution.py:135
  210.4 22.3 %collective-permute-start.24 = (bf16[4,48,1152]{2,1,0:T(8,128)(2,1)S(1)}, bf16[4,48,1152]{2,1,0:T(8,128)(2,1)}, u32[]{:S(2)}, u32[]{:S(2)}) collective-permute-start(bf16[4,48,1152]{2,1,0:T(8,128)(2,1)S(1)} %get-tuple-element.125), channel_id=1, source_target_pairs={{0,24},{1,25},{2,26},{3,27},{4,28},{5,29},{6,30},{7,31},{8,16},{9,... | collective-permute-start | bytes 1327112 | tf_op jit(solution)/shard_map/qkv_plane_3_0/ppermute | solution.py:135
  214.4 24.6 %collective-permute-start.30 = (bf16[2,48,2432]{2,1,0:T(8,128)(2,1)S(1)}, bf16[2,48,2432]{2,1,0:T(8,128)(2,1)S(1)}, u32[]{:S(2)}, u32[]{:S(2)}) collective-permute-start(bf16[2,48,2432]{2,1,0:T(8,128)(2,1)S(1)} %get-tuple-element.134), channel_id=1, source_target_pairs={{0,4},{1,5},{2,6},{3,7},{4,0},{5,1},{6,2},{7,3},{8,12},{9,13},{10,... | collective-permute-start | bytes 1400840 | tf_op jit(solution)/shard_map/wide_column_0_4/ppermute | solution.py:135
  235.8 10.7 %collective-permute-start.29 = (bf16[48,1280]{1,0:T(8,128)(2,1)S(1)}, bf16[48,1280]{1,0:T(8,128)(2,1)S(1)}, u32[]{:S(2)}, u32[]{:S(2)}) collective-permute-start(bf16[48,1280]{1,0:T(8,128)(2,1)S(1)} %get-tuple-element.133), channel_id=1, source_target_pairs={{0,6},{1,7},{2,4},{3,5},{4,2},{5,3},{6,0},{7,1},{8,14},{9,15},{10,... | collective-permute-start | bytes 368648 | tf_op jit(solution)/shard_map/qkv_column_0_6/ppermute | solution.py:135
  239.6 11.9 %collective-permute-start.34 = (bf16[48,2432]{1,0:T(8,128)(2,1)S(1)}, bf16[48,2432]{1,0:T(8,128)(2,1)S(1)}, u32[]{:S(2)}, u32[]{:S(2)}) collective-permute-start(bf16[48,2432]{1,0:T(8,128)(2,1)S(1)} %get-tuple-element.136), channel_id=1, source_target_pairs={{0,2},{1,3},{2,0},{3,1},{4,6},{5,7},{6,4},{7,5},{8,10},{9,11},{10,... | collective-permute-start | bytes 700424 | tf_op jit(solution)/shard_map/wide_column_0_2/ppermute | solution.py:135
  249.8 14.4 %collective-permute-start.32 = (bf16[48,2816]{1,0:T(8,128)(2,1)S(1)}, bf16[48,2816]{1,0:T(8,128)(2,1)S(1)}, u32[]{:S(2)}, u32[]{:S(2)}) collective-permute-start(bf16[48,2816]{1,0:T(8,128)(2,1)S(1)} %qkv_total.1.refs_3_.refs_1_), channel_id=1, source_target_pairs={{0,16},{1,17},{2,18},{3,19},{4,20},{5,21},{6,22},{7,23},{8,24},{9,... | collective-permute-start | bytes 811016 | tf_op jit(solution)/shard_map/qkv_back_2_0/ppermute | solution.py:135
  250.2 14.2 %collective-permute-start.31 = (bf16[48,2816]{1,0:T(8,128)(2,1)S(1)}, bf16[48,2816]{1,0:T(8,128)(2,1)S(1)}, u32[]{:S(2)}, u32[]{:S(2)}) collective-permute-start(bf16[48,2816]{1,0:T(8,128)(2,1)S(1)} %qkv_total.1.refs_3_.refs_1_), channel_id=1, source_target_pairs={{0,8},{1,9},{2,10},{3,11},{4,12},{5,13},{6,14},{7,15},{8,0},{9,1},... | collective-permute-start | bytes 811016 | tf_op jit(solution)/shard_map/qkv_back_1_0/ppermute | solution.py:135
  252.1 15.6 %collective-permute-start.37 = (bf16[48,2432]{1,0:T(8,128)(2,1)S(1)}, bf16[48,2432]{1,0:T(8,128)(2,1)S(1)}, u32[]{:S(2)}, u32[]{:S(2)}) collective-permute-start(bf16[48,2432]{1,0:T(8,128)(2,1)S(1)} %wide_total.1.refs_5_.refs_1_), channel_id=1, source_target_pairs={{0,24},{1,25},{2,26},{3,27},{4,28},{5,29},{6,30},{7,31},{8,16},{9,... | collective-permute-start | bytes 700424 | tf_op jit(solution)/shard_map/wide_back_3_0/ppermute | solution.py:135
  254.0 16.0 %collective-permute-start.36 = (bf16[48,2432]{1,0:T(8,128)(2,1)S(1)}, bf16[48,2432]{1,0:T(8,128)(2,1)S(1)}, u32[]{:S(2)}, u32[]{:S(2)}) collective-permute-start(bf16[48,2432]{1,0:T(8,128)(2,1)S(1)} %wide_total.1.refs_5_.refs_1_), channel_id=1, source_target_pairs={{0,16},{1,17},{2,18},{3,19},{4,20},{5,21},{6,22},{7,23},{8,24},{9,... | collective-permute-start | bytes 700424 | tf_op jit(solution)/shard_map/wide_back_2_0/ppermute | solution.py:135
  258.4 11.6 %collective-permute-start.35 = (bf16[48,2432]{1,0:T(8,128)(2,1)S(1)}, bf16[48,2432]{1,0:T(8,128)(2,1)S(1)}, u32[]{:S(2)}, u32[]{:S(2)}) collective-permute-start(bf16[48,2432]{1,0:T(8,128)(2,1)S(1)} %wide_total.1.refs_5_.refs_1_), channel_id=1, source_target_pairs={{0,8},{1,9},{2,10},{3,11},{4,12},{5,13},{6,14},{7,15},{8,0},{9,1},... | collective-permute-start | bytes 700424 | tf_op jit(solution)/shard_map/wide_back_1_0/ppermute | solution.py:135
  (47 other events, 364.0 us)
Sparse Core Ops, SparseCore 0:
  45.1 50.9 all-gather.1
  157.6 53.7 reduce-scatter.2
  215.6 27.9 reduce-scatter.4

commit v6 on v5

--- a/solution.py
+++ b/solution.py
@@ -189,7 +189,7 @@
 
 
 def row(vectors_ref, index, length):
-    return vectors_ref[index : index + 1, :length].astype(f32)
+    return vectors_ref[index : index + 1, :length]
 
 
 def mask_kernel(tiles, place_ref, counts_ref, bias_ref, seg_ref):
@@ -436,7 +436,7 @@
     dh2 = jnp.zeros((size, width), f32)
     for index in range(PARTS):
         span = slice(index * part, (index + 1) * part)
-        u = dot_nn(h2, matrix(w_up_ref, span)) + vec_ref[B_UP : B_UP + 1, span].astype(f32)
+        u = dot_nn(h2, matrix(w_up_ref, span)) + vec_ref[B_UP : B_UP + 1, span]
         cdf = 0.5 * (1.0 + lax.erf(u * (1.0 / math.sqrt(2.0))))
         pdf = jnp.exp(-0.5 * u * u) * (1.0 / math.sqrt(2.0 * math.pi))
         g = (u * cdf).astype(bf16)
@@ -935,7 +935,7 @@
         for shard in shards:
             for line in range(lines_of(length)):
                 pieces.append(shard[at + line : at + line + 1, : min(TILE, length - line * TILE)])
-        out_ref[index : index + 1, : length * len(shards)] = jnp.concatenate(pieces, axis=1).astype(bf16)
+        out_ref[index : index + 1, : length * len(shards)] = jnp.concatenate(pieces, axis=1)
         at += lines_of(length)
 
 
@@ -946,7 +946,7 @@
         "unpack_vectors",
         [own, other],
         [VMEM] * 2,
-        [(VMEM, shape_of((ROWS, 2 * levels * max(lengths))))],
+        [(VMEM, shape_of((ROWS, 2 * levels * max(lengths)), f32))],
     )[0]
 
 
@@ -1162,7 +1162,7 @@
             line = joined[:, at : at + length].reshape(1, -1)
             lines.append(jnp.pad(line, ((0, 0), (0, shards * max(lengths) - line.shape[1]))))
             at += length
-        vectors = jnp.pad(jnp.concatenate(lines), ((0, ROWS - len(lines)), (0, 0)))
+        vectors = jnp.pad(jnp.concatenate(lines), ((0, ROWS - len(lines)), (0, 0))).astype(f32)
         full_qkv, full_proj, full_up, full_head = (
             Weight([full], 0, full.shape) for full in (gather(w) for w in (w_qkv, w_proj, w_up, w_head))
         )

time: 281 us -> 281 us (level)
  no operation moved by 1% of the time
where the time goes in v6:
time: 281 us; the launch traced here: 280 us
  Pallas kernels  149 us (53%)
  waiting for transfers between devices  66.2 us (24%)
  starting transfers between devices  36.6 us (13%)
  between operations  14.4 us (5%)
  local copies, waits for them, and re-layouts  13.9 us (5%)
    pallas_call x27, Pallas kernels, __call__(): pl.pallas_call(body, grid_spec=pltpu.PrefetchScalarGridSpec(num_scalar_pr...  149 us
    ppermute x38, waiting for transfers between devices, swap(): return lax.ppermute(value, ('dp', 'fsdp'), pairs)  63.7 us
    ppermute x38, starting transfers between devices, swap(): return lax.ppermute(value, ('dp', 'fsdp'), pairs)  36.5 us
    unnamed x76, local copies, waits for them, and re-layouts  13.3 us
  transfers between devices with their start and end apart: 41, of which 19 were waited for; matrix products, arithmetic and copies ran while one was open for 0% of the time, Pallas kernels for 33%

profile of v6, /device:TPU:0, one launch (start us, length us, event | category | flops | bytes accessed | tf_op | source)
XLA Modules:
  0.0 279.7 jit_solution(1737737393911884151)
XLA Ops:
  7.9 2.6 quarters.1
  10.5 5.0 %collective-permute-start.2 = (bf16[48,1280]{1,0:T(8,128)(2,1)}, bf16[48,1280]{1,0:T(8,128)(2,1)S(1)}, u32[]{:S(2)}, u32[]{:S(2)}) collective-permute-start(bf16[48,1280]{1,0:T(8,128)(2,1)} %get-tuple-element.84.refs_2_.refs_1_), channel_id=1, source_target_pairs={{0,6},{1,7},{2,4},{3,5},{4,2},{5,3},{6,0},{7,1},{8,14},{9,15},{10,... | collective-permute-start | bytes 368648 | tf_op jit(solution)/shard_map/qkv_column_0_6/ppermute | solution.py:135
  17.1 3.2 %masks.1.refs_5_.refs_1_ = f32[3072,128]{1,0:T(8,128)S(1)} custom-call(s32[5]{0:T(128)S(1)} %copy-done.7, s32[32,32]{1,0:T(8,128)S(1)} %copy-done.6, bf16[48,1280]{1,0:T(8,128)(2,1)S(1)} %copy-done.20), custom_call_target="tpu_custom_call" | custom-call | flops 10000000000 | bytes 1 | tf_op jit(solution)/shard_map/masks/pallas_call | solution.py:103
  20.4 5.8 %collective-permute-done.1.refs_3_ = bf16[48,1280]{1,0:T(8,128)(2,1)S(1)} collective-permute-done((bf16[48,1280]{1,0:T(8,128)(2,1)}, bf16[48,1280]{1,0:T(8,128)(2,1)S(1)}, u32[]{:S(2)}, u32[]{:S(2)}) %collective-permute-start.1) | collective-permute-done | bytes 122912 | tf_op jit(solution)/shard_map/qkv_column_0_4/ppermute | solution.py:135
  26.7 2.5 collective-permute-start.6
  30.3 2.5 collective-permute-start.10
  32.8 5.7 %collective-permute-done.6.refs_5_ = bf16[3,48,1152]{2,1,0:T(8,128)(2,1)S(1)} collective-permute-done((bf16[3,48,1152]{2,1,0:T(8,128)(2,1)S(1)}, bf16[3,48,1152]{2,1,0:T(8,128)(2,1)S(1)}, u32[]{:S(2)}, u32[]{:S(2)}) %collective-permute-start.6) | collective-permute-done | bytes 331808 | tf_op jit(solution)/shard_map/qkv_plane_3_0/ppermute | solution.py:135
  38.5 5.2 %collective-permute-done.5.refs_4_ = bf16[3,48,1152]{2,1,0:T(8,128)(2,1)S(1)} collective-permute-done((bf16[3,48,1152]{2,1,0:T(8,128)(2,1)S(1)}, bf16[3,48,1152]{2,1,0:T(8,128)(2,1)S(1)}, u32[]{:S(2)}, u32[]{:S(2)}) %collective-permute-start.5) | collective-permute-done | bytes 331808 | tf_op jit(solution)/shard_map/qkv_plane_2_0/ppermute | solution.py:135
  45.7 5.1 %collective-permute-done.9.refs_3_ = bf16[48,2432]{1,0:T(8,128)(2,1)} collective-permute-done((bf16[48,2432]{1,0:T(8,128)(2,1)}, bf16[48,2432]{1,0:T(8,128)(2,1)}, u32[]{:S(2)}, u32[]{:S(2)}) %collective-permute-start.9) | collective-permute-done | bytes 233504 | tf_op jit(solution)/shard_map/wide_column_0_4/ppermute | solution.py:135
  50.8 2.0 wide_near.1.refs_5_.refs_4_
  52.8 2.5 collective-permute-start.13
  56.4 6.9 %norm_qkv.1 = (bf16[960,768]{1,0:T(8,128)(2,1)S(1)}, bf16[960,768]{1,0:T(8,128)(2,1)S(1)}, bf16[960,768]{1,0:T(8,128)(2,1)S(1)}, bf16[960,768]{1,0:T(8,128)(2,1)S(1)}) custom-call(s32[5]{0:T(128)S(1)} %copy-done.7, bf16[960,768]{1,0:T(8,128)(2,1)S(1)} %copy-done.2, f32[16,3072]{1,0:T(8,128)S(1)} %unpack_vectors.1.refs_5_.refs_2_.refs_6_.refs_3_.refs_4_, ...), custom_call_target="tpu_custom_call" | custom-call | flops 10000000000 | bytes 1 | tf_op jit(solution)/shard_map/norm_qkv/pallas_call | solution.py:103
  63.4 10.0 %attend.1 = (bf16[960,768]{1,0:T(8,128)(2,1)S(1)}, f32[6,8,256]{2,1,0:T(8,128)S(1)}) custom-call(s32[5]{0:T(128)S(1)} %copy-done.7, f32[3072,128]{1,0:T(8,128)S(1)} %copy-done.29, bf16[960,768]{1,0:T(8,128)(2,1)S(1)} %get-tuple-element.88.refs_2_, bf16[960,768]{1,0:T(8,128)(2,1)S(1)} %get-tuple-element.89.refs_3_, ...), custom_call_target="tpu_custom_call" | custom-call | flops 10000000000 | bytes 1 | tf_op jit(solution)/shard_map/attend/pallas_call | solution.py:103
  73.5 10.5 %collective-permute-done.12.refs_6_ = bf16[3,48,2432]{2,1,0:T(8,128)(2,1)S(1)} collective-permute-done((bf16[3,48,2432]{2,1,0:T(8,128)(2,1)S(1)}, bf16[3,48,2432]{2,1,0:T(8,128)(2,1)S(1)}, u32[]{:S(2)}, u32[]{:S(2)}) %collective-permute-start.12) | collective-permute-done | bytes 700448 | tf_op jit(solution)/shard_map/wide_plane_2_0/ppermute | solution.py:135
  87.0 6.6 %collective-permute-done.14.refs_8_.refs_10_.refs_13_.refs_5_ = bf16[4,96,4864]{2,1,0:T(8,128)(2,1)} collective-permute-done((bf16[4,96,4864]{2,1,0:T(8,128)(2,1)S(1)}, bf16[4,96,4864]{2,1,0:T(8,128)(2,1)}, u32[]{:S(2)}, u32[]{:S(2)}) %collective-permute-start.14) | collective-permute-done | bytes 3735584 | tf_op jit(solution)/shard_map/wide_core_0_1/ppermute | solution.py:135
  93.6 2.5 all-gather.2.cloned.1.call-done.refs_11_
  96.1 34.3 %middle.1 = (bf16[960,768]{1,0:T(8,128)(2,1)}, bf16[960,768]{1,0:T(8,128)(2,1)}, bf16[960,1024]{1,0:T(8,128)(2,1)}, bf16[960,768]{1,0:T(8,128)(2,1)}, bf16[960,3...) custom-call(s32[5]{0:T(128)} %stack.23.refs_0_, ...), custom_call_target="tpu_custom_call" | custom-call | flops 10000000000 | bytes 1 | tf_op jit(solution)/shard_map/middle/pallas_call | solution.py:103
  130.4 16.3 %grad_wide.1 = (bf16[4,2,48,3072]{3,2,1,0:T(8,128)(2,1)}, bf16[4,2,48,3072]{3,2,1,0:T(8,128)(2,1)}, bf16[4,2,48,1024]{3,2,1,0:T(8,128)(2,1)}, bf16[4,2,48,1024]{...) custom-call(s32[5]{0:T(128)} %stack.23.refs_0_, ...), custom_call_target="tpu_custom_call" | custom-call | flops 10000000000 | bytes 1 | tf_op jit(solution)/shard_map/grad_wide/pallas_call | solution.py:103
  147.6 9.9 %grad_down.1.refs_7_ = bf16[3072,768]{1,0:T(8,128)(2,1)} custom-call(s32[5]{0:T(128)} %stack.23.refs_0_, bf16[960,3072]{1,0:T(8,128)(2,1)} %get-tuple-element.108.refs_1_, bf16[960,768]{1,0:T(8,128)(2,1)} %get-tuple-element.109.refs_2_, bf16[4,2,48,3072]{3,2,1,0:T(8,128)(2,1)} %get-tuple-element.102.refs_3_.refs_1_), custom_call_target="tpu_custom_call" | custom-call | flops 30000001024 | bytes 1 | tf_op jit(solution)/shard_map/grad_down/pallas_call | solution.py:103
  159.2 6.1 %wide_split.1 = (bf16[4,48,2432]{2,1,0:T(8,128)(2,1)}, bf16[4,48,2432]{2,1,0:T(8,128)(2,1)}, bf16[4,48,2432]{2,1,0:T(8,128)(2,1)}, bf16[4,48,2432]{2,1,0:T(8,128)(2,1)}) custom-call(s32[5]{0:T(128)} %stack.23.refs_0_, bf16[4,2,48,3072]{3,2,1,0:T(8,128)(2,1)} %get-tuple-element.102.refs_3_.refs_1_, bf16[4,2,48,3072]{3,2,1,0:T(8,128)(2,1)} %copy-done.36, ...), custom_call_target="tpu_custom_call" | custom-call | flops 10000000000 | bytes 1 | tf_op jit(solution)/shard_map/wide_split/pallas_call | solution.py:103
  168.9 17.2 %attend_back.1 = (bf16[3,960,768]{2,1,0:T(8,128)(2,1)}, f32[2,768]{1,0:T(2,128)}) custom-call(s32[5]{0:T(128)} %stack.23.refs_0_, f32[3072,128]{1,0:T(8,128)} %copy-done.28, bf16[960,768]{1,0:T(8,128)(2,1)} %copy-done.30, bf16[960,768]{1,0:T(8,128)(2,1)} %copy-done.31, bf16[960,768]{1,0:T(8,128)(2,1)} %copy-done.32, bf16[960,768]{1,0:T(8,128)(2,1)} %copy-done.3, ...), custom_call_target="tpu_custom_call" | custom-call | flops 60000002048 | bytes 1 | tf_op jit(solution)/shard_map/attend_back/pallas_call | solution.py:103
  186.1 8.8 %grad_qkv.1 = (bf16[4,2,48,2304]{3,2,1,0:T(8,128)(2,1)}, bf16[4,2,48,2304]{3,2,1,0:T(8,128)(2,1)}) custom-call(s32[5]{0:T(128)} %stack.23.refs_0_, bf16[960,768]{1,0:T(8,128)(2,1)} %copy-done.27, bf16[3,960,768]{2,1,0:T(8,128)(2,1)} %get-tuple-element.111.refs_2_.refs_3_, bf16[3,960,768]{2,1,0:T(8,128)(2,1)} %get-tuple-element.111.refs_2_.refs_3_), custom_call_target="tpu_custom_call" | custom-call | flops 10000000000 | bytes 1 | tf_op jit(solution)/shard_map/grad_qkv/pallas_call | solution.py:103
  202.1 6.9 %align.1.refs_5_ = bf16[960,1024]{1,0:T(8,128)(2,1)} custom-call(s32[5]{0:T(128)} %stack.23.refs_0_, s32[32,32]{1,0:T(8,128)} %refs_1_.14, bf16[960,768]{1,0:T(8,128)(2,1)} %get-tuple-element.95.refs_2_, f32[16,3072]{1,0:T(8,128)} %copy-done.5, bf16[4,96,4864]{2,1,0:T(8,128)(2,1)} %bitcast.16, ...), custom_call_target="tpu_custom_call" | custom-call | flops 10000000000 | bytes 1 | tf_op jit(solution)/shard_map/align/pallas_call | solution.py:103
  215.6 10.7 %first_back.1 = (bf16[960,768]{1,0:T(8,128)(2,1)}, f32[2,768]{1,0:T(2,128)}) custom-call(s32[5]{0:T(128)} %stack.23.refs_0_, bf16[960,768]{1,0:T(8,128)(2,1)} %refs_1_.15, bf16[960,768]{1,0:T(8,128)(2,1)} %get-tuple-element.101.refs_6_.refs_2_, bf16[3,960,768]{2,1,0:T(8,128)(2,1)} %get-tuple-element.111.refs_2_.refs_3_, f32[16,3072]{1,0:T(8,128)} %copy-done.5, ...), custom_call_target="tpu_custom_call" | custom-call | flops 10000000000 | bytes 1 | tf_op jit(solution)/shard_map/first_back/pallas_call | solution.py:103
  229.2 3.6 %collective-permute-done.23.refs_3_ = bf16[4,48,1152]{2,1,0:T(8,128)(2,1)S(1)} collective-permute-done((bf16[4,48,1152]{2,1,0:T(8,128)(2,1)S(1)}, bf16[4,48,1152]{2,1,0:T(8,128)(2,1)S(1)}, u32[]{:S(2)}, u32[]{:S(2)}) %collective-permute-start.23) | collective-permute-done | bytes 442400 | tf_op jit(solution)/shard_map/qkv_plane_2_0/ppermute | solution.py:135
  235.8 3.3 %collective-permute-start.29 = (bf16[48,1280]{1,0:T(8,128)(2,1)S(1)}, bf16[48,1280]{1,0:T(8,128)(2,1)S(1)}, u32[]{:S(2)}, u32[]{:S(2)}) collective-permute-start(bf16[48,1280]{1,0:T(8,128)(2,1)S(1)} %get-tuple-element.133), channel_id=1, source_target_pairs={{0,6},{1,7},{2,4},{3,5},{4,2},{5,3},{6,0},{7,1},{8,14},{9,15},{10,... | collective-permute-start | bytes 368648 | tf_op jit(solution)/shard_map/qkv_column_0_6/ppermute | solution.py:135
  239.8 3.4 %collective-permute-done.27.refs_2_ = bf16[48,1280]{1,0:T(8,128)(2,1)S(1)} collective-permute-done((bf16[48,1280]{1,0:T(8,128)(2,1)S(1)}, bf16[48,1280]{1,0:T(8,128)(2,1)S(1)}, u32[]{:S(2)}, u32[]{:S(2)}) %collective-permute-start.27) | collective-permute-done | bytes 122912 | tf_op jit(solution)/shard_map/qkv_column_0_2/ppermute | solution.py:135
  247.9 1.9 collective-permute-start.33
  254.3 4.1 %collective-permute-done.33.refs_4_ = bf16[48,2816]{1,0:T(8,128)(2,1)S(1)} collective-permute-done((bf16[48,2816]{1,0:T(8,128)(2,1)S(1)}, bf16[48,2816]{1,0:T(8,128)(2,1)S(1)}, u32[]{:S(2)}, u32[]{:S(2)}) %collective-permute-start.33) | collective-permute-done | bytes 270368 | tf_op jit(solution)/shard_map/qkv_back_3_0/ppermute | solution.py:135
  259.0 5.3 %collective-permute-done.32.refs_3_ = bf16[48,2816]{1,0:T(8,128)(2,1)S(1)} collective-permute-done((bf16[48,2816]{1,0:T(8,128)(2,1)S(1)}, bf16[48,2816]{1,0:T(8,128)(2,1)S(1)}, u32[]{:S(2)}, u32[]{:S(2)}) %collective-permute-start.32) | collective-permute-done | bytes 270368 | tf_op jit(solution)/shard_map/qkv_back_2_0/ppermute | solution.py:135
  264.5 2.0 qkv_join.1
  267.7 2.3 collective-permute-done.36.refs_3_
  (157 shorter events, 50.3 us)
Async XLA Ops:
  7.2 88.9 %all-gather.2.cloned.1.call-start = ((), (), s32[]{:S(2)}) async-start(), calls=%async_computation.2 | async-start | bytes 5308416 | tf_op jit(solution)/shard_map/all_gather | solution.py:1136
  15.6 10.6 %collective-permute-start.1 = (bf16[48,1280]{1,0:T(8,128)(2,1)}, bf16[48,1280]{1,0:T(8,128)(2,1)S(1)}, u32[]{:S(2)}, u32[]{:S(2)}) collective-permute-start(bf16[48,1280]{1,0:T(8,128)(2,1)} %get-tuple-element.84.refs_2_.refs_1_), channel_id=1, source_target_pairs={{0,4},{1,5},{2,6},{3,7},{4,0},{5,1},{6,2},{7,3},{8,12},{9,13},{10,... | collective-permute-start | bytes 368648 | tf_op jit(solution)/shard_map/qkv_column_0_4/ppermute | solution.py:135
  15.6 10.6 %collective-permute-start = (bf16[48,1280]{1,0:T(8,128)(2,1)}, bf16[48,1280]{1,0:T(8,128)(2,1)S(1)}, u32[]{:S(2)}, u32[]{:S(2)}) collective-permute-start(bf16[48,1280]{1,0:T(8,128)(2,1)} %get-tuple-element.84.refs_2_.refs_1_), channel_id=1, source_target_pairs={{0,2},{1,3},{2,0},{3,1},{4,6},{5,7},{6,4},{7,5},{8,10},{9,11},{10,... | collective-permute-start | bytes 368648 | tf_op jit(solution)/shard_map/qkv_column_0_2/ppermute | solution.py:135
  26.7 11.7 %collective-permute-start.6 = (bf16[3,48,1152]{2,1,0:T(8,128)(2,1)S(1)}, bf16[3,48,1152]{2,1,0:T(8,128)(2,1)S(1)}, u32[]{:S(2)}, u32[]{:S(2)}) collective-permute-start(bf16[3,48,1152]{2,1,0:T(8,128)(2,1)S(1)} %get-tuple-element.86.refs_2_.refs_6_), channel_id=1, source_target_pairs={{0,24},{1,25},{2,26},{3,27},{4,28},{5,29},{6,30},{7,31},{8,16},{9,... | collective-permute-start | bytes 995336 | tf_op jit(solution)/shard_map/qkv_plane_3_0/ppermute | solution.py:135
  29.3 14.4 %collective-permute-start.5 = (bf16[3,48,1152]{2,1,0:T(8,128)(2,1)S(1)}, bf16[3,48,1152]{2,1,0:T(8,128)(2,1)S(1)}, u32[]{:S(2)}, u32[]{:S(2)}) collective-permute-start(bf16[3,48,1152]{2,1,0:T(8,128)(2,1)S(1)} %get-tuple-element.86.refs_2_.refs_6_), channel_id=1, source_target_pairs={{0,16},{1,17},{2,18},{3,19},{4,20},{5,21},{6,22},{7,23},{8,24},{9,... | collective-permute-start | bytes 995336 | tf_op jit(solution)/shard_map/qkv_plane_2_0/ppermute | solution.py:135
  29.8 14.0 %collective-permute-start.4 = (bf16[3,48,1152]{2,1,0:T(8,128)(2,1)S(1)}, bf16[3,48,1152]{2,1,0:T(8,128)(2,1)S(1)}, u32[]{:S(2)}, u32[]{:S(2)}) collective-permute-start(bf16[3,48,1152]{2,1,0:T(8,128)(2,1)S(1)} %get-tuple-element.86.refs_2_.refs_6_), channel_id=1, source_target_pairs={{0,8},{1,9},{2,10},{3,11},{4,12},{5,13},{6,14},{7,15},{8,0},{9,1},... | collective-permute-start | bytes 995336 | tf_op jit(solution)/shard_map/qkv_plane_1_0/ppermute | solution.py:135
  30.3 15.4 %collective-permute-start.10 = (bf16[48,2432]{1,0:T(8,128)(2,1)}, bf16[48,2432]{1,0:T(8,128)(2,1)}, u32[]{:S(2)}, u32[]{:S(2)}) collective-permute-start(bf16[48,2432]{1,0:T(8,128)(2,1)} %get-tuple-element.87.refs_1_), channel_id=1, source_target_pairs={{0,6},{1,7},{2,4},{3,5},{4,2},{5,3},{6,0},{7,1},{8,14},{9,15},{10,... | collective-permute-start | bytes 700424 | tf_op jit(solution)/shard_map/wide_column_0_6/ppermute | solution.py:135
  32.8 18.1 %collective-permute-start.9 = (bf16[48,2432]{1,0:T(8,128)(2,1)}, bf16[48,2432]{1,0:T(8,128)(2,1)}, u32[]{:S(2)}, u32[]{:S(2)}) collective-permute-start(bf16[48,2432]{1,0:T(8,128)(2,1)} %get-tuple-element.87.refs_1_), channel_id=1, source_target_pairs={{0,4},{1,5},{2,6},{3,7},{4,0},{5,1},{6,2},{7,3},{8,12},{9,13},{10,... | collective-permute-start | bytes 700424 | tf_op jit(solution)/shard_map/wide_column_0_4/ppermute | solution.py:135
  38.5 12.3 %collective-permute-start.8 = (bf16[48,2432]{1,0:T(8,128)(2,1)}, bf16[48,2432]{1,0:T(8,128)(2,1)}, u32[]{:S(2)}, u32[]{:S(2)}) collective-permute-start(bf16[48,2432]{1,0:T(8,128)(2,1)} %get-tuple-element.87.refs_1_), channel_id=1, source_target_pairs={{0,2},{1,3},{2,0},{3,1},{4,6},{5,7},{6,4},{7,5},{8,10},{9,11},{10,... | collective-permute-start | bytes 700424 | tf_op jit(solution)/shard_map/wide_column_0_2/ppermute | solution.py:135
  44.5 11.9 %collective-permute-start.7 = (bf16[4,96,2304]{2,1,0:T(8,128)(2,1)S(1)}, bf16[4,96,2304]{2,1,0:T(8,128)(2,1)}, u32[]{:S(2)}, u32[]{:S(2)}) collective-permute-start(bf16[4,96,2304]{2,1,0:T(8,128)(2,1)S(1)} %bitcast.17), channel_id=1, source_target_pairs={{0,1},{1,0},{2,3},{3,2},{4,5},{5,4},{6,7},{7,6},{8,9},{9,8},{10,11... | collective-permute-start | bytes 5308424 | tf_op jit(solution)/shard_map/qkv_core_0_1/ppermute | solution.py:135
  45.0 170.6 %reduce-scatter.3.cloned.1.call-start = ((), (), s32[]{:S(2)}) async-start(), calls=%async_computation.3 | async-start | bytes 5308416 | tf_op jit(solution)/shard_map/reduce_scatter | solution.py:1139
  52.8 20.7 %collective-permute-start.13 = (bf16[3,48,2432]{2,1,0:T(8,128)(2,1)S(1)}, bf16[3,48,2432]{2,1,0:T(8,128)(2,1)S(1)}, u32[]{:S(2)}, u32[]{:S(2)}) collective-permute-start(bf16[3,48,2432]{2,1,0:T(8,128)(2,1)S(1)} %wide_near.1.refs_5_.refs_4_), channel_id=1, source_target_pairs={{0,24},{1,25},{2,26},{3,27},{4,28},{5,29},{6,30},{7,31},{8,16},{9,... | collective-permute-start | bytes 2101256 | tf_op jit(solution)/shard_map/wide_plane_3_0/ppermute | solution.py:135
  55.3 28.6 %collective-permute-start.12 = (bf16[3,48,2432]{2,1,0:T(8,128)(2,1)S(1)}, bf16[3,48,2432]{2,1,0:T(8,128)(2,1)S(1)}, u32[]{:S(2)}, u32[]{:S(2)}) collective-permute-start(bf16[3,48,2432]{2,1,0:T(8,128)(2,1)S(1)} %wide_near.1.refs_5_.refs_4_), channel_id=1, source_target_pairs={{0,16},{1,17},{2,18},{3,19},{4,20},{5,21},{6,22},{7,23},{8,24},{9,... | collective-permute-start | bytes 2101256 | tf_op jit(solution)/shard_map/wide_plane_2_0/ppermute | solution.py:135
  55.8 28.2 %collective-permute-start.11 = (bf16[3,48,2432]{2,1,0:T(8,128)(2,1)S(1)}, bf16[3,48,2432]{2,1,0:T(8,128)(2,1)S(1)}, u32[]{:S(2)}, u32[]{:S(2)}) collective-permute-start(bf16[3,48,2432]{2,1,0:T(8,128)(2,1)S(1)} %wide_near.1.refs_5_.refs_4_), channel_id=1, source_target_pairs={{0,8},{1,9},{2,10},{3,11},{4,12},{5,13},{6,14},{7,15},{8,0},{9,1},... | collective-permute-start | bytes 2101256 | tf_op jit(solution)/shard_map/wide_plane_1_0/ppermute | solution.py:135
  146.7 10.8 %collective-permute-start.17 = (bf16[4,2,48,768]{3,2,1,0:T(8,128)(2,1)}, bf16[4,2,48,768]{3,2,1,0:T(8,128)(2,1)}, u32[]{:S(2)}, u32[]{:S(2)}) collective-permute-start(bf16[4,2,48,768]{3,2,1,0:T(8,128)(2,1)} %get-tuple-element.107), channel_id=1, source_target_pairs={{0,1},{1,0},{2,3},{3,2},{4,5},{5,4},{6,7},{7,6},{8,9},{9,8},{10,11... | collective-permute-start | bytes 1769480 | tf_op jit(solution)/shard_map/wide_core_0_1/ppermute | solution.py:135
  147.1 10.5 %collective-permute-start.16 = (bf16[4,2,48,1024]{3,2,1,0:T(8,128)(2,1)}, bf16[4,2,48,1024]{3,2,1,0:T(8,128)(2,1)S(1)}, u32[]{:S(2)}, u32[]{:S(2)}) collective-permute-start(bf16[4,2,48,1024]{3,2,1,0:T(8,128)(2,1)} %get-tuple-element.105), channel_id=1, source_target_pairs={{0,1},{1,0},{2,3},{3,2},{4,5},{5,4},{6,7},{7,6},{8,9},{9,8},{10,11... | collective-permute-start | bytes 2359304 | tf_op jit(solution)/shard_map/wide_core_0_1/ppermute | solution.py:135
  157.5 88.9 %reduce-scatter.5.cloned.1.call-start = ((), (), s32[]{:S(2)}) async-start(), calls=%async_computation.4 | async-start | bytes 737280 | tf_op jit(solution)/shard_map/reduce_scatter | solution.py:1216
  165.4 43.6 %collective-permute-start.19 = (bf16[4,48,2432]{2,1,0:T(8,128)(2,1)}, bf16[4,48,2432]{2,1,0:T(8,128)(2,1)S(1)}, u32[]{:S(2)}, u32[]{:S(2)}) collective-permute-start(bf16[4,48,2432]{2,1,0:T(8,128)(2,1)} %get-tuple-element.118), channel_id=1, source_target_pairs={{0,8},{1,9},{2,10},{3,11},{4,12},{5,13},{6,14},{7,15},{8,0},{9,1},... | collective-permute-start | bytes 2801672 | tf_op jit(solution)/shard_map/wide_plane_1_0/ppermute | solution.py:135
  166.9 43.5 %collective-permute-start.20 = (bf16[4,48,2432]{2,1,0:T(8,128)(2,1)}, bf16[4,48,2432]{2,1,0:T(8,128)(2,1)S(1)}, u32[]{:S(2)}, u32[]{:S(2)}) collective-permute-start(bf16[4,48,2432]{2,1,0:T(8,128)(2,1)} %get-tuple-element.119), channel_id=1, source_target_pairs={{0,16},{1,17},{2,18},{3,19},{4,20},{5,21},{6,22},{7,23},{8,24},{9,... | collective-permute-start | bytes 2801672 | tf_op jit(solution)/shard_map/wide_plane_2_0/ppermute | solution.py:135
  168.4 42.6 %collective-permute-start.21 = (bf16[4,48,2432]{2,1,0:T(8,128)(2,1)}, bf16[4,48,2432]{2,1,0:T(8,128)(2,1)S(1)}, u32[]{:S(2)}, u32[]{:S(2)}) collective-permute-start(bf16[4,48,2432]{2,1,0:T(8,128)(2,1)} %get-tuple-element.120), channel_id=1, source_target_pairs={{0,24},{1,25},{2,26},{3,27},{4,28},{5,29},{6,30},{7,31},{8,16},{9,... | collective-permute-start | bytes 2801672 | tf_op jit(solution)/shard_map/wide_plane_3_0/ppermute | solution.py:135
  197.1 31.9 %collective-permute-start.25 = (bf16[4,16,128]{2,1,0:T(8,128)(2,1)S(1)}, bf16[4,16,128]{2,1,0:T(8,128)(2,1)S(1)}, u32[]{:S(2)}, u32[]{:S(2)}) collective-permute-start(bf16[4,16,128]{2,1,0:T(8,128)(2,1)S(1)} %get-tuple-element.126), channel_id=1, source_target_pairs={{0,1},{1,0},{2,3},{3,2},{4,5},{5,4},{6,7},{7,6},{8,9},{9,8},{10,11... | collective-permute-start | bytes 49160 | tf_op jit(solution)/shard_map/vectors_core_0_1/ppermute | solution.py:135
  200.5 28.6 %collective-permute-start.22 = (bf16[4,48,1152]{2,1,0:T(8,128)(2,1)S(1)}, bf16[4,48,1152]{2,1,0:T(8,128)(2,1)S(1)}, u32[]{:S(2)}, u32[]{:S(2)}) collective-permute-start(bf16[4,48,1152]{2,1,0:T(8,128)(2,1)S(1)} %get-tuple-element.123), channel_id=1, source_target_pairs={{0,8},{1,9},{2,10},{3,11},{4,12},{5,13},{6,14},{7,15},{8,0},{9,1},... | collective-permute-start | bytes 1327112 | tf_op jit(solution)/shard_map/qkv_plane_1_0/ppermute | solution.py:135
  208.9 23.9 %collective-permute-start.23 = (bf16[4,48,1152]{2,1,0:T(8,128)(2,1)S(1)}, bf16[4,48,1152]{2,1,0:T(8,128)(2,1)S(1)}, u32[]{:S(2)}, u32[]{:S(2)}) collective-permute-start(bf16[4,48,1152]{2,1,0:T(8,128)(2,1)S(1)} %get-tuple-element.124), channel_id=1, source_target_pairs={{0,16},{1,17},{2,18},{3,19},{4,20},{5,21},{6,22},{7,23},{8,24},{9,... | collective-permute-start | bytes 1327112 | tf_op jit(solution)/shard_map/qkv_plane_2_0/ppermute | solution.py:135
  210.5 22.4 %collective-permute-start.24 = (bf16[4,48,1152]{2,1,0:T(8,128)(2,1)S(1)}, bf16[4,48,1152]{2,1,0:T(8,128)(2,1)}, u32[]{:S(2)}, u32[]{:S(2)}) collective-permute-start(bf16[4,48,1152]{2,1,0:T(8,128)(2,1)S(1)} %get-tuple-element.125), channel_id=1, source_target_pairs={{0,24},{1,25},{2,26},{3,27},{4,28},{5,29},{6,30},{7,31},{8,16},{9,... | collective-permute-start | bytes 1327112 | tf_op jit(solution)/shard_map/qkv_plane_3_0/ppermute | solution.py:135
  214.3 24.8 %collective-permute-start.30 = (bf16[2,48,2432]{2,1,0:T(8,128)(2,1)S(1)}, bf16[2,48,2432]{2,1,0:T(8,128)(2,1)S(1)}, u32[]{:S(2)}, u32[]{:S(2)}) collective-permute-start(bf16[2,48,2432]{2,1,0:T(8,128)(2,1)S(1)} %get-tuple-element.134), channel_id=1, source_target_pairs={{0,4},{1,5},{2,6},{3,7},{4,0},{5,1},{6,2},{7,3},{8,12},{9,13},{10,... | collective-permute-start | bytes 1400840 | tf_op jit(solution)/shard_map/wide_column_0_4/ppermute | solution.py:135
  235.8 10.6 %collective-permute-start.29 = (bf16[48,1280]{1,0:T(8,128)(2,1)S(1)}, bf16[48,1280]{1,0:T(8,128)(2,1)S(1)}, u32[]{:S(2)}, u32[]{:S(2)}) collective-permute-start(bf16[48,1280]{1,0:T(8,128)(2,1)S(1)} %get-tuple-element.133), channel_id=1, source_target_pairs={{0,6},{1,7},{2,4},{3,5},{4,2},{5,3},{6,0},{7,1},{8,14},{9,15},{10,... | collective-permute-start | bytes 368648 | tf_op jit(solution)/shard_map/qkv_column_0_6/ppermute | solution.py:135
  239.8 11.7 %collective-permute-start.34 = (bf16[48,2432]{1,0:T(8,128)(2,1)S(1)}, bf16[48,2432]{1,0:T(8,128)(2,1)S(1)}, u32[]{:S(2)}, u32[]{:S(2)}) collective-permute-start(bf16[48,2432]{1,0:T(8,128)(2,1)S(1)} %get-tuple-element.136), channel_id=1, source_target_pairs={{0,2},{1,3},{2,0},{3,1},{4,6},{5,7},{6,4},{7,5},{8,10},{9,11},{10,... | collective-permute-start | bytes 700424 | tf_op jit(solution)/shard_map/wide_column_0_2/ppermute | solution.py:135
  249.9 14.4 %collective-permute-start.32 = (bf16[48,2816]{1,0:T(8,128)(2,1)S(1)}, bf16[48,2816]{1,0:T(8,128)(2,1)S(1)}, u32[]{:S(2)}, u32[]{:S(2)}) collective-permute-start(bf16[48,2816]{1,0:T(8,128)(2,1)S(1)} %qkv_total.1.refs_3_.refs_1_), channel_id=1, source_target_pairs={{0,16},{1,17},{2,18},{3,19},{4,20},{5,21},{6,22},{7,23},{8,24},{9,... | collective-permute-start | bytes 811016 | tf_op jit(solution)/shard_map/qkv_back_2_0/ppermute | solution.py:135
  250.1 14.3 %collective-permute-start.31 = (bf16[48,2816]{1,0:T(8,128)(2,1)S(1)}, bf16[48,2816]{1,0:T(8,128)(2,1)S(1)}, u32[]{:S(2)}, u32[]{:S(2)}) collective-permute-start(bf16[48,2816]{1,0:T(8,128)(2,1)S(1)} %qkv_total.1.refs_3_.refs_1_), channel_id=1, source_target_pairs={{0,8},{1,9},{2,10},{3,11},{4,12},{5,13},{6,14},{7,15},{8,0},{9,1},... | collective-permute-start | bytes 811016 | tf_op jit(solution)/shard_map/qkv_back_1_0/ppermute | solution.py:135
  252.1 15.6 %collective-permute-start.37 = (bf16[48,2432]{1,0:T(8,128)(2,1)S(1)}, bf16[48,2432]{1,0:T(8,128)(2,1)S(1)}, u32[]{:S(2)}, u32[]{:S(2)}) collective-permute-start(bf16[48,2432]{1,0:T(8,128)(2,1)S(1)} %wide_total.1.refs_5_.refs_1_), channel_id=1, source_target_pairs={{0,24},{1,25},{2,26},{3,27},{4,28},{5,29},{6,30},{7,31},{8,16},{9,... | collective-permute-start | bytes 700424 | tf_op jit(solution)/shard_map/wide_back_3_0/ppermute | solution.py:135
  254.0 16.0 %collective-permute-start.36 = (bf16[48,2432]{1,0:T(8,128)(2,1)S(1)}, bf16[48,2432]{1,0:T(8,128)(2,1)S(1)}, u32[]{:S(2)}, u32[]{:S(2)}) collective-permute-start(bf16[48,2432]{1,0:T(8,128)(2,1)S(1)} %wide_total.1.refs_5_.refs_1_), channel_id=1, source_target_pairs={{0,16},{1,17},{2,18},{3,19},{4,20},{5,21},{6,22},{7,23},{8,24},{9,... | collective-permute-start | bytes 700424 | tf_op jit(solution)/shard_map/wide_back_2_0/ppermute | solution.py:135
  258.4 11.6 %collective-permute-start.35 = (bf16[48,2432]{1,0:T(8,128)(2,1)S(1)}, bf16[48,2432]{1,0:T(8,128)(2,1)S(1)}, u32[]{:S(2)}, u32[]{:S(2)}) collective-permute-start(bf16[48,2432]{1,0:T(8,128)(2,1)S(1)} %wide_total.1.refs_5_.refs_1_), channel_id=1, source_target_pairs={{0,8},{1,9},{2,10},{3,11},{4,12},{5,13},{6,14},{7,15},{8,0},{9,1},... | collective-permute-start | bytes 700424 | tf_op jit(solution)/shard_map/wide_back_1_0/ppermute | solution.py:135
  (47 other events, 363.5 us)
Sparse Core Ops, SparseCore 0:
  45.1 50.9 all-gather.1
  157.6 53.7 reduce-scatter.2
  215.7 27.8 reduce-scatter.4
